TPU v7x, 32 devices: a whole 2x2x4 slice. The times are simulated.
32 devices in a mesh: seq: 4 (over y, x), batch: 8 (over z, core).
Axes of the slice: x: 2, y: 2, z: 4, core: 2. Of those that a mesh axis runs over, the one named last changes fastest.
Arguments:
- block_input: bfloat16 [8, 1024, 2048], P('batch', 'seq'), may hold values from -6 to 6
- lengths: int32 [8], P('batch'), may hold values from 769 to 1024, as said below
- ln1_gain: bfloat16 [2048], P(('seq', 'batch')), may hold values from 0.5 to 1.5
- ln1_bias: bfloat16 [2048], P(('seq', 'batch')), may hold values from -3 to 3
- w_qkv: bfloat16 [2048, 6144], P(('seq', 'batch')), may hold values from -0.125 to 0.125
- qv_bias: bfloat16 [4096], P(('seq', 'batch')), may hold values from -3 to 3
- w_out: bfloat16 [2048, 2048], P(('seq', 'batch')), may hold values from -1.5 to 1.5
- out_bias: bfloat16 [2048], P(('seq', 'batch')), may hold values from -3 to 3
- ln2_gain: bfloat16 [2048], P(('seq', 'batch')), may hold values from 0.5 to 1.5
- ln2_bias: bfloat16 [2048], P(('seq', 'batch')), may hold values from -3 to 3
- w_fc1: bfloat16 [2048, 8192], P(('seq', 'batch')), may hold values from -0.125 to 0.125
- fc1_bias: bfloat16 [8192], P(('seq', 'batch')), may hold values from -3 to 3
- w_fc2: bfloat16 [8192, 2048], P(('seq', 'batch')), may hold values from -0.0625 to 0.0625
- fc2_bias: bfloat16 [2048], P(('seq', 'batch')), may hold values from -3 to 3
- out_cotangent: bfloat16 [8, 1024, 2048], P('batch', 'seq'), may hold values from -6 to 6
Outputs:
- block_output: bfloat16 [8, 1024, 2048], P('batch', 'seq')
- grad_input: float32 [8, 1024, 2048], P('batch', 'seq')
- grad_ln1_gain: float32 [2048], P(('seq', 'batch'))
- grad_ln1_bias: float32 [2048], P(('seq', 'batch'))
- grad_w_qkv: float32 [2048, 6144], P(('seq', 'batch'))
- grad_qv_bias: float32 [4096], P(('seq', 'batch'))
- grad_w_out: float32 [2048, 2048], P(('seq', 'batch'))
- grad_out_bias: float32 [2048], P(('seq', 'batch'))
- grad_ln2_gain: float32 [2048], P(('seq', 'batch'))
- grad_ln2_bias: float32 [2048], P(('seq', 'batch'))
- grad_w_fc1: float32 [2048, 8192], P(('seq', 'batch'))
- grad_fc1_bias: float32 [8192], P(('seq', 'batch'))
- grad_w_fc2: float32 [8192, 2048], P(('seq', 'batch'))
- grad_fc2_bias: float32 [2048], P(('seq', 'batch'))
Inputs may be any that keep to these rules, and one draw needn't show every extreme that they name: `lengths`: positions from a sequence's length on are padding; one sequence has length 1024.
All inputs are finite; a program needn't handle non-finite values.
Results may differ from a plain program's by a relative error of at most 0.011.
Values may be sent and summed in bfloat16 or wider, within the bound.
A program may use at most 384 MiB of HBM per device.

v0:
```python
import jax
import jax.numpy as jnp
from jax import lax
from jax.sharding import PartitionSpec as P

HEADS = 16
HEAD_DIM = 128
WINDOW = 256


EPS = 1e-05


def from_behind(value, axis, steps):
    count = lax.axis_size(axis)
    first, last = (max(0, -steps), min(count, count - steps))
    return lax.ppermute(value, axis, [(source, source + steps) for source in range(first, last)])


def layer_norm(values, gain_vec, shift_vec):
    row_mean = jnp.mean(values, -1, keepdims=True)
    centred = values - row_mean
    row_var = jnp.mean(centred * centred, -1, keepdims=True)
    return centred * lax.rsqrt(row_var + EPS) * gain_vec + shift_vec


def gelu_tanh(values):
    return jax.nn.gelu(values, approximate=True)


def block_mask(start, rows, length):
    query_pos = start + lax.broadcasted_iota(jnp.int32, (rows, rows + WINDOW), 0)
    key_pos = start - WINDOW + lax.broadcasted_iota(jnp.int32, (rows, rows + WINDOW), 1)
    return (
        (key_pos >= 0)
        & (key_pos <= query_pos)
        & (query_pos - key_pos < WINDOW)
        & ((key_pos < length) | (key_pos == query_pos))
    )


def to_float(params):
    return tuple((weight.astype(jnp.float32) for weight in params))


def attend_forward(query_heads, key_all, value_all, start, length):
    rows = query_heads.shape[0]
    valid = block_mask(start, rows, length)[None]
    scores = jnp.einsum(
        "qhd,khd->hqk", query_heads, key_all, preferred_element_type=jnp.float32
    ) * HEAD_DIM ** (-0.5)
    masked = jnp.where(valid, scores, -1e30)
    row_max = jnp.max(masked, -1, keepdims=True)
    expo = jnp.exp(masked - row_max)
    row_sum = jnp.sum(expo, -1, keepdims=True)
    log_total = row_max + jnp.log(row_sum)
    probs_low = (expo / row_sum).astype(jnp.bfloat16)
    attended = jnp.einsum("hqk,khd->qhd", probs_low, value_all, preferred_element_type=jnp.float32)
    return (attended.reshape(rows, -1).astype(jnp.bfloat16), log_total)


def attend_backward(query_heads, key_all, value_all, grad_attended, log_total, start, length):
    rows = query_heads.shape[0]
    scale = HEAD_DIM ** (-0.5)
    valid = block_mask(start, rows, length)[None]
    scores = (
        jnp.einsum("qhd,khd->hqk", query_heads, key_all, preferred_element_type=jnp.float32) * scale
    )
    probs = jnp.exp(jnp.where(valid, scores, -1e30) - log_total)
    grad_probs = jnp.einsum(
        "qhd,khd->hqk", grad_attended, value_all, preferred_element_type=jnp.float32
    )
    row_delta = jnp.sum(grad_probs * probs, -1, keepdims=True)
    grad_scores = (probs * (grad_probs - row_delta)).astype(jnp.bfloat16)
    grad_query = (
        jnp.einsum("hqk,khd->qhd", grad_scores, key_all, preferred_element_type=jnp.float32) * scale
    )
    grad_keys = (
        jnp.einsum("hqk,qhd->khd", grad_scores, query_heads, preferred_element_type=jnp.float32)
        * scale
    )
    grad_vals = jnp.einsum(
        "hqk,qhd->khd",
        probs.astype(jnp.bfloat16),
        grad_attended,
        preferred_element_type=jnp.float32,
    )
    return (
        grad_query.reshape(rows, -1),
        grad_keys.reshape(key_all.shape[0], -1),
        grad_vals.reshape(key_all.shape[0], -1),
    )


def sharded_path(
    block_input,
    lengths,
    ln1_gain,
    ln1_bias,
    w_qkv,
    qv_bias,
    w_out,
    out_bias,
    ln2_gain,
    ln2_bias,
    w_fc1,
    fc1_bias,
    w_fc2,
    fc2_bias,
    out_cotangent,
):
    attn_params = (
        lax.all_gather(ln1_gain, ("seq", "batch"), axis=0, tiled=True),
        lax.all_gather(ln1_bias, ("seq", "batch"), axis=0, tiled=True),
        lax.all_gather(w_qkv, ("seq", "batch"), axis=0, tiled=True),
        lax.all_gather(qv_bias, ("seq", "batch"), axis=0, tiled=True),
        lax.all_gather(w_out, ("seq", "batch"), axis=0, tiled=True),
        lax.all_gather(out_bias, ("seq", "batch"), axis=0, tiled=True),
    )
    gain_one, shift_one, qkv_full, qv_full, out_full, obias_full = attn_params
    gain_one_f, shift_one_f, qv_full_f, obias_f = to_float(
        (gain_one, shift_one, qv_full, obias_full)
    )
    rows = block_input.shape[1]
    width = block_input.shape[2]
    start = lax.axis_index("seq") * rows
    length = lengths[0]
    acts = block_input[0].astype(jnp.float32)
    hidden_one = layer_norm(acts, gain_one_f, shift_one_f).astype(jnp.bfloat16)
    projected = jnp.dot(hidden_one, qkv_full, preferred_element_type=jnp.float32)
    queries = (projected[:, :width] + qv_full_f[:width]).astype(jnp.bfloat16)
    keys = projected[:, width : 2 * width].astype(jnp.bfloat16)
    values = (projected[:, 2 * width :] + qv_full_f[width:]).astype(jnp.bfloat16)
    key_tail = jnp.stack([keys, values])
    prior = from_behind(key_tail, "seq", 1)
    key_all = jnp.concatenate([prior[0], keys], 0).reshape(rows + WINDOW, HEADS, HEAD_DIM)
    value_all = jnp.concatenate([prior[1], values], 0).reshape(rows + WINDOW, HEADS, HEAD_DIM)
    query_heads = queries.reshape(rows, HEADS, HEAD_DIM)
    attended, log_total = attend_forward(query_heads, key_all, value_all, start, length)
    middle = acts + jnp.dot(attended, out_full, preferred_element_type=jnp.float32) + obias_f
    mlp_params = (
        lax.all_gather(ln2_gain, ("seq", "batch"), axis=0, tiled=True),
        lax.all_gather(ln2_bias, ("seq", "batch"), axis=0, tiled=True),
        lax.all_gather(w_fc1, ("seq", "batch"), axis=0, tiled=True),
        lax.all_gather(fc1_bias, ("seq", "batch"), axis=0, tiled=True),
        lax.all_gather(w_fc2, ("seq", "batch"), axis=0, tiled=True),
        lax.all_gather(fc2_bias, ("seq", "batch"), axis=0, tiled=True),
    )
    gain_two_f, shift_two_f, fc1_shift, fc2_shift = to_float(
        (mlp_params[0], mlp_params[1], mlp_params[3], mlp_params[5])
    )
    hidden_two = layer_norm(middle, gain_two_f, shift_two_f).astype(jnp.bfloat16)
    pre_act = jnp.dot(hidden_two, mlp_params[2], preferred_element_type=jnp.float32) + fc1_shift
    act_low = gelu_tanh(pre_act).astype(jnp.bfloat16)
    branch = jnp.dot(act_low, mlp_params[4], preferred_element_type=jnp.float32) + fc2_shift
    result = (middle + branch).astype(jnp.bfloat16)
    mlp_back = (
        lax.all_gather(ln2_gain, ("seq", "batch"), axis=0, tiled=True),
        lax.all_gather(ln2_bias, ("seq", "batch"), axis=0, tiled=True),
        lax.all_gather(w_fc1, ("seq", "batch"), axis=0, tiled=True),
        lax.all_gather(fc1_bias, ("seq", "batch"), axis=0, tiled=True),
        lax.all_gather(w_fc2, ("seq", "batch"), axis=0, tiled=True),
        lax.all_gather(fc2_bias, ("seq", "batch"), axis=0, tiled=True),
    )
    fc1_full = mlp_back[2]
    fc2_full = mlp_back[4]
    gain_two_b, shift_two_b = to_float((mlp_back[0], mlp_back[1]))
    grad_out = out_cotangent[0]
    grad_fc2 = jnp.einsum("tf,td->fd", act_low, grad_out, preferred_element_type=jnp.float32)
    grad_c2 = jnp.sum(grad_out.astype(jnp.float32), 0)
    grad_act = jnp.einsum("td,fd->tf", grad_out, fc2_full, preferred_element_type=jnp.float32)
    gelu_pull = jax.vjp(gelu_tanh, pre_act)[1]
    grad_pre = gelu_pull(grad_act)[0].astype(jnp.bfloat16)
    grad_fc1 = jnp.einsum("td,tf->df", hidden_two, grad_pre, preferred_element_type=jnp.float32)
    grad_c1 = jnp.sum(grad_pre.astype(jnp.float32), 0)
    grad_normed_two = jnp.einsum(
        "tf,df->td", grad_pre, fc1_full, preferred_element_type=jnp.float32
    )
    norm_pull_two = jax.vjp(layer_norm, middle, gain_two_b, shift_two_b)[1]
    grad_mid_norm, grad_gain_two, grad_shift_two = norm_pull_two(grad_normed_two)
    grad_mid = grad_mid_norm + grad_out.astype(jnp.float32)
    mlp_sums = (
        lax.psum_scatter(grad_gain_two, ("seq", "batch"), scatter_dimension=0, tiled=True),
        lax.psum_scatter(grad_shift_two, ("seq", "batch"), scatter_dimension=0, tiled=True),
        lax.psum_scatter(grad_fc1, ("seq", "batch"), scatter_dimension=0, tiled=True),
        lax.psum_scatter(grad_c1, ("seq", "batch"), scatter_dimension=0, tiled=True),
        lax.psum_scatter(grad_fc2, ("seq", "batch"), scatter_dimension=0, tiled=True),
        lax.psum_scatter(grad_c2, ("seq", "batch"), scatter_dimension=0, tiled=True),
    )
    attn_back = (
        lax.all_gather(ln1_gain, ("seq", "batch"), axis=0, tiled=True),
        lax.all_gather(ln1_bias, ("seq", "batch"), axis=0, tiled=True),
        lax.all_gather(w_qkv, ("seq", "batch"), axis=0, tiled=True),
        lax.all_gather(qv_bias, ("seq", "batch"), axis=0, tiled=True),
        lax.all_gather(w_out, ("seq", "batch"), axis=0, tiled=True),
        lax.all_gather(out_bias, ("seq", "batch"), axis=0, tiled=True),
    )
    qkv_back = attn_back[2]
    out_back = attn_back[4]
    gain_one_b, shift_one_b = to_float((attn_back[0], attn_back[1]))
    grad_attn = grad_mid.astype(jnp.bfloat16)
    grad_wout = jnp.einsum("td,te->de", attended, grad_attn, preferred_element_type=jnp.float32)
    grad_obias = jnp.sum(grad_attn.astype(jnp.float32), 0)
    grad_attended = jnp.einsum("te,de->td", grad_attn, out_back, preferred_element_type=jnp.float32)
    grad_attended = grad_attended.astype(jnp.bfloat16).reshape(rows, HEADS, HEAD_DIM)
    grad_query, grad_keys_all, grad_vals_all = attend_backward(
        query_heads, key_all, value_all, grad_attended, log_total, start, length
    )
    grad_query = grad_query.astype(jnp.bfloat16)
    returned = from_behind(
        jnp.stack([grad_keys_all[:WINDOW], grad_vals_all[:WINDOW]]).astype(jnp.bfloat16), "seq", -1
    ).astype(jnp.float32)
    lead_pad = jnp.zeros((rows - WINDOW, width), jnp.float32)
    grad_keys = (grad_keys_all[WINDOW:] + jnp.concatenate([lead_pad, returned[0]], 0)).astype(
        jnp.bfloat16
    )
    grad_vals = (grad_vals_all[WINDOW:] + jnp.concatenate([lead_pad, returned[1]], 0)).astype(
        jnp.bfloat16
    )
    grad_proj = jnp.concatenate([grad_query, grad_keys, grad_vals], 1)
    grad_wqkv = jnp.einsum("td,te->de", hidden_one, grad_proj, preferred_element_type=jnp.float32)
    grad_qvbias = jnp.concatenate(
        [jnp.sum(grad_query.astype(jnp.float32), 0), jnp.sum(grad_vals.astype(jnp.float32), 0)]
    )
    grad_normed_one = jnp.einsum(
        "te,de->td", grad_proj, qkv_back, preferred_element_type=jnp.float32
    )
    norm_pull_one = jax.vjp(layer_norm, acts, gain_one_b, shift_one_b)[1]
    grad_acts_norm, grad_gain_one, grad_shift_one = norm_pull_one(grad_normed_one)
    input_total = grad_mid + grad_acts_norm
    attn_sums = (
        lax.psum_scatter(grad_gain_one, ("seq", "batch"), scatter_dimension=0, tiled=True),
        lax.psum_scatter(grad_shift_one, ("seq", "batch"), scatter_dimension=0, tiled=True),
        lax.psum_scatter(grad_wqkv, ("seq", "batch"), scatter_dimension=0, tiled=True),
        lax.psum_scatter(grad_qvbias, ("seq", "batch"), scatter_dimension=0, tiled=True),
        lax.psum_scatter(grad_wout, ("seq", "batch"), scatter_dimension=0, tiled=True),
        lax.psum_scatter(grad_obias, ("seq", "batch"), scatter_dimension=0, tiled=True),
    )
    return (
        result[None],
        input_total[None],
        attn_sums[0],
        attn_sums[1],
        attn_sums[2],
        attn_sums[3],
        attn_sums[4],
        attn_sums[5],
        mlp_sums[0],
        mlp_sums[1],
        mlp_sums[2],
        mlp_sums[3],
        mlp_sums[4],
        mlp_sums[5],
    )


def body(
    block_input,
    lengths,
    ln1_gain,
    ln1_bias,
    w_qkv,
    qv_bias,
    w_out,
    out_bias,
    ln2_gain,
    ln2_bias,
    w_fc1,
    fc1_bias,
    w_fc2,
    fc2_bias,
    out_cotangent,
):
    return sharded_path(
        block_input,
        lengths,
        ln1_gain,
        ln1_bias,
        w_qkv,
        qv_bias,
        w_out,
        out_bias,
        ln2_gain,
        ln2_bias,
        w_fc1,
        fc1_bias,
        w_fc2,
        fc2_bias,
        out_cotangent,
    )


def solution(mesh):
    return jax.shard_map(
        body,
        mesh=mesh,
        in_specs=(
            P("batch", "seq", None),
            P("batch"),
            P(("seq", "batch")),
            P(("seq", "batch")),
            P(("seq", "batch"), None),
            P(("seq", "batch")),
            P(("seq", "batch"), None),
            P(("seq", "batch")),
            P(("seq", "batch")),
            P(("seq", "batch")),
            P(("seq", "batch"), None),
            P(("seq", "batch")),
            P(("seq", "batch"), None),
            P(("seq", "batch")),
            P("batch", "seq", None),
        ),
        out_specs=(
            P("batch", "seq", None),
            P("batch", "seq", None),
            P(("seq", "batch")),
            P(("seq", "batch")),
            P(("seq", "batch"), None),
            P(("seq", "batch")),
            P(("seq", "batch"), None),
            P(("seq", "batch")),
            P(("seq", "batch")),
            P(("seq", "batch")),
            P(("seq", "batch"), None),
            P(("seq", "batch")),
            P(("seq", "batch"), None),
            P(("seq", "batch")),
        ),
        check_vma=False,
    )
```

profile of v0, /device:TPU:0, one launch (start us, length us, event | category | flops | bytes accessed | tf_op | source)
XLA Modules:
  0.0 2986.9 jit_solution(4774713392197790985)
XLA Ops:
  11.6 43.8 %all-reduce.15 = (bf16[2048]{0:T(1024)(128)(2,1)S(1)}, bf16[2048]{0:T(1024)(128)(2,1)S(1)}, bf16[2048]{0:T(1024)(128)(2,1)S(1)}, bf16[2048]{0:T(1024)(128)(2,1)}...) all-reduce(bf16[2048]{0:T(1024)(128)(2,1)S(1)} %dynamic-update-slic, ...), channel_id=1, replica_groups=mesh['seq'=4,'batch'=8] {'seq','batch'}, use_global_device_ids=true, to_apply=%add.1 | all-reduce | flops 12288 | bytes 49152
  55.5 40.5 %all-gather = bf16[32,1,128]{2,1,0:T(2,128)(2,1)S(1)} all-gather(bf16[1,1,128]{2,1,0:T(2,128)(2,1)S(1)} %bitcast.151), channel_id=1, replica_groups=mesh['seq'=4,'batch'=8] {'seq','batch'}, dimensions={0}, use_global_device_ids=true | all-gather | bytes 8448 | tf_op jit(solution)/shard_map/all_gather | solution.py:116
  97.3 72.8 %all-gather.7.cloned.1.call-done = bf16[2048,6144]{1,0:T(8,128)(2,1)} async-done(((bf16[64,6144]{1,0:T(8,128)(2,1)}), bf16[2048,6144]{1,0:T(8,128)(2,1)}) %all-gather.7.cloned.1.call-update) | async-done | bytes 25165840 | tf_op jit(solution)/shard_map/all_gather | solution.py:115
  170.1 11.7 fusion.62
  183.1 1.5 fusion.36
  184.6 1.5 pad_maximum_fusion.1
  186.1 4.7 collective-permute-start
  191.5 36.6 %all-gather.1 = bf16[32,1,256]{2,1,0:T(2,128)(2,1)S(1)} all-gather(bf16[1,1,256]{2,1,0:T(2,128)(2,1)S(1)} %reshape.254), channel_id=1, replica_groups=mesh['seq'=4,'batch'=8] {'seq','batch'}, dimensions={0}, use_global_device_ids=true | all-gather | bytes 16896 | tf_op jit(solution)/shard_map/all_gather | solution.py:145
  229.1 1.9 copy.53
  230.9 26.6 collective-permute-done
  257.6 3.1 fusion.69
  260.7 2.3 copy.51
  262.9 1.5 copy.56
  265.1 2.1 fusion.71
  267.3 2.0 fusion.7
  269.3 1.4 copy-done
  270.7 3.8 fusion.38
  274.5 6.2 fusion.72
  281.1 185.8 %all-gather.11.cloned.1.call-done = bf16[2048,8192]{1,0:T(8,128)(2,1)} async-done(((bf16[64,8192]{1,0:T(8,128)(2,1)}), bf16[2048,8192]{1,0:T(8,128)(2,1)}) %all-gather.11.cloned.1.call-update) | async-done | bytes 33554448 | tf_op jit(solution)/shard_map/all_gather | solution.py:144
  466.9 18.0 convolution_add_fusion
  484.8 177.9 %all-gather.13.cloned.1.call-done = bf16[8192,2048]{1,0:T(8,128)(2,1)} async-done(((bf16[256,2048]{1,0:T(8,128)(2,1)}), bf16[8192,2048]{1,0:T(8,128)(2,1)}) %all-gather.13.cloned.1.call-update) | async-done | bytes 33554448 | tf_op jit(solution)/shard_map/all_gather | solution.py:146
  662.7 22.2 convert_reduce_fusion
  684.9 18.2 multiply_reduce_fusion.1
  703.1 2.3 fusion.68
  708.8 6.7 convolution_convert_fusion
  715.5 2.4 copy.54
  718.0 5.5 fusion.25
  723.4 7.3 multiply_reduce_fusion
  731.9 2.0 multiply_convert_fusion
  733.9 2.0 multiply_bitcast_fusion
  736.3 1.6 collective-permute-start.1
  739.0 2.3 convert_reduce_fusion.5
  741.4 44.9 %collective-permute-done.1 = bf16[2,256,2048]{1,2,0:T(8,128)(2,1)S(1)} collective-permute-done((bf16[2,256,2048]{1,2,0:T(8,128)(2,1)S(1)}, bf16[2,256,2048]{1,2,0:T(8,128)(2,1)S(1)}, u32[]{:S(2)}, u32[]{:S(2)}) %collective-permute-start.1) | collective-permute-done | bytes 2097184 | tf_op jit(solution)/shard_map/ppermute | solution.py:17
  788.5 1.6 fusion.34
  790.1 15.3 fusion.66
  806.8 1.5 fusion.30
  808.4 9.7 fusion.73
  818.8 19.6 fusion.41
  838.5 27.6 fusion.43
  866.8 25.8 fusion.65
  893.2 19.5 fusion.22
  912.8 4.8 add_bitcast_fusion
  917.5 13.8 all-reduce.18.cloned.1.call-done
  940.2 1.3 dynamic-slice.6
  941.5 180.5 %reduce-scatter.7.cloned.1.call-done = f32[64,2048]{1,0:T(8,128)} async-done(((f32[2048,2048]{1,0:T(8,128)}), f32[64,2048]{1,0:T(8,128)}) %reduce-scatter.7.cloned.1.call-update) | async-done | bytes 524304 | tf_op jit(solution)/shard_map/reduce_scatter | solution.py:236
  1122.0 437.5 %reduce-scatter.5.cloned.1.call-done = f32[64,6144]{1,0:T(8,128)} async-done(((f32[2048,6144]{1,0:T(8,128)}), f32[64,6144]{1,0:T(8,128)}) %reduce-scatter.5.cloned.1.call-update) | async-done | bytes 1572880 | tf_op jit(solution)/shard_map/reduce_scatter | solution.py:234
  1559.5 711.4 %reduce-scatter.11.cloned.1.call-done = f32[256,2048]{1,0:T(8,128)} async-done(((f32[8192,2048]{1,0:T(8,128)}), f32[256,2048]{1,0:T(8,128)}) %reduce-scatter.11.cloned.1.call-update) | async-done | bytes 2097168 | tf_op jit(solution)/shard_map/reduce_scatter | solution.py:187
  2270.9 709.0 %reduce-scatter.9.cloned.1.call-done = f32[64,8192]{1,0:T(8,128)} async-done(((f32[2048,8192]{1,0:T(8,128)}), f32[64,8192]{1,0:T(8,128)}) %reduce-scatter.9.cloned.1.call-update) | async-done | bytes 2097168 | tf_op jit(solution)/shard_map/reduce_scatter | solution.py:185
  (149 shorter events, 29.3 us)
Async XLA Ops:
  7.2 2.9 copy-start.27
  7.2 3.2 copy-start.28
  7.2 3.4 copy-start.29
  7.2 3.7 copy-start.30
  7.2 3.9 copy-start.31
  7.2 4.2 copy-start.32
  7.2 48.3 %copy-start.26 = (bf16[128]{0:T(256)(128)(2,1)S(1)}, bf16[128]{0:T(256)(128)(2,1)}, u32[]{:S(2)}) copy-start(bf16[128]{0:T(256)(128)(2,1)} %param.20) | copy-start | bytes 772
  7.3 88.8 %copy-start.1 = (bf16[1,256,2048]{2,1,0:T(8,128)(2,1)S(1)}, bf16[1,256,2048]{2,1,0:T(8,128)(2,1)}, u32[]{:S(2)}) copy-start(bf16[1,256,2048]{2,1,0:T(8,128)(2,1)} %param.15) | copy-start | bytes 3145732
  7.3 162.8 %all-gather.7.cloned.1.call-start = ((), (), s32[]{:S(2)}) async-start(), calls=%async_computation.4 | async-start | bytes 25952256 | tf_op jit(solution)/shard_map/all_gather | solution.py:115
  8.0 266.5 %all-gather.9.cloned.1.call-start = ((), (), s32[]{:S(2)}) async-start(), calls=%async_computation.5 | async-start | bytes 8650752 | tf_op jit(solution)/shard_map/all_gather | solution.py:117
  8.7 458.1 %all-gather.11.cloned.1.call-start = ((), (), s32[]{:S(2)}) async-start(), calls=%async_computation.6 | async-start | bytes 34603008 | tf_op jit(solution)/shard_map/all_gather | solution.py:144
  9.5 653.2 %all-gather.13.cloned.1.call-start = ((), (), s32[]{:S(2)}) async-start(), calls=%async_computation.7 | async-start | bytes 34603008 | tf_op jit(solution)/shard_map/all_gather | solution.py:146
  10.1 921.3 %all-reduce.18.cloned.1.call-start = ((), (), s32[]{:S(2)}) async-start(), calls=%async_computation.12 | async-start | bytes 196608
  55.5 126.3 %copy-start.15 = (f32[2048]{0:T(1024)}, f32[2048]{0:T(1024)S(1)}, u32[]{:S(2)}) copy-start(f32[2048]{0:T(1024)S(1)} %convert_element_type.124) | copy-start | bytes 24580
  96.7 0.6 copy-start.23
  97.3 84.6 %copy-start.19 = (f32[256]{0:T(256)}, f32[256]{0:T(256)S(1)}, u32[]{:S(2)}) copy-start(f32[256]{0:T(256)S(1)} %fusion.55) | copy-start | bytes 3076
  184.6 6.8 copy-start.33
  186.1 71.5 %collective-permute-start = (bf16[2,256,2048]{2,1,0:T(8,128)(2,1)}, bf16[2,256,2048]{2,1,0:T(8,128)(2,1)}, u32[]{:S(2)}, u32[]{:S(2)}) collective-permute-start(bf16[2,256,2048]{2,1,0:T(8,128)(2,1)} %pad_maximum_fusion.1), channel_id=1, source_target_pairs={{0,8},{8,16},{16,24},{1,9},{9,17},{17,25},{2,10},{10,18},{18,26},{... | collective-permute-start | bytes 6291464 | tf_op jit(solution)/shard_map/ppermute | solution.py:17
  191.5 275.4 %copy-start.17 = (f32[2048]{0:T(1024)}, f32[2048]{0:T(1024)S(1)}, u32[]{:S(2)}) copy-start(f32[2048]{0:T(1024)S(1)} %convert_element_type.135) | copy-start | bytes 24580
  229.0 40.2 %copy-start.11 = (bf16[256,2048]{0,1:T(8,128)(2,1)}, bf16[256,2048]{0,1:T(8,128)(2,1)S(1)}, u32[]{:S(2)}) copy-start(bf16[256,2048]{0,1:T(8,128)(2,1)S(1)} %copy.52) | copy-start | bytes 3145732
  230.9 34.2 %copy-start.7 = (bf16[256,2048]{0,1:T(8,128)(2,1)}, bf16[256,2048]{0,1:T(8,128)(2,1)S(1)}, u32[]{:S(2)}) copy-start(bf16[256,2048]{0,1:T(8,128)(2,1)S(1)} %copy.53) | copy-start | bytes 3145732
  262.9 1.8 copy-start.12
  265.1 2.1 copy-start.3
  267.2 3.4 copy-start
  267.2 3.4 copy-start.13
  703.1 3.6 copy-start.6
  705.4 1.3 copy-start.2
  705.4 10.1 copy-start.21
  707.9 1.0 copy-start.9
  718.0 13.9 slice-start
  723.4 8.5 slice-start.1
  733.9 2.2 copy-start.14
  735.9 2.0 copy-start.5
  736.3 2.7 copy-start.4
  736.3 49.9 %collective-permute-start.1 = (bf16[2,256,2048]{1,2,0:T(8,128)(2,1)S(1)}, bf16[2,256,2048]{1,2,0:T(8,128)(2,1)S(1)}, u32[]{:S(2)}, u32[]{:S(2)}) collective-permute-start(bf16[2,256,2048]{1,2,0:T(8,128)(2,1)S(1)} %pad_maximum_fusion.3), channel_id=1, source_target_pairs={{8,0},{16,8},{24,16},{9,1},{17,9},{25,17},{10,2},{18,10},{26,18},{... | collective-permute-start | bytes 6291464 | tf_op jit(solution)/shard_map/ppermute | solution.py:17
  786.9 1.6 slice-start.2
  790.1 15.3 copy-start.10
  790.1 15.3 copy-start.24
  790.1 16.7 copy-start.20
  805.5 1.4 copy-start.8
  808.4 313.6 %reduce-scatter.7.cloned.1.call-start = ((), (), s32[]{:S(2)}) async-start(), calls=%async_computation.9 | async-start | bytes 17301504 | tf_op jit(solution)/shard_map/reduce_scatter | solution.py:236
  818.1 0.7 copy-start.16
  818.1 741.4 %reduce-scatter.5.cloned.1.call-start = ((), (), s32[]{:S(2)}) async-start(), calls=%async_computation.8 | async-start | bytes 51904512 | tf_op jit(solution)/shard_map/reduce_scatter | solution.py:234
  838.5 1432.5 %reduce-scatter.11.cloned.1.call-start = ((), (), s32[]{:S(2)}) async-start(), calls=%async_computation.11 | async-start | bytes 69206016 | tf_op jit(solution)/shard_map/reduce_scatter | solution.py:187
  866.1 0.7 copy-start.18
  866.1 2113.8 %reduce-scatter.9.cloned.1.call-start = ((), (), s32[]{:S(2)}) async-start(), calls=%async_computation.10 | async-start | bytes 69206016 | tf_op jit(solution)/shard_map/reduce_scatter | solution.py:185
  892.5 0.7 copy-start.25
  893.2 19.5 copy-start.22
Sparse Core Ops, SparseCore 0:
  11.1 158.9 all-gather.6
  173.1 98.5 all-gather.8
  274.6 192.1 all-gather.10
  469.7 192.9 all-gather.12
  808.5 122.8 all-reduce.17
  934.2 187.7 reduce-scatter.6
  1130.1 429.3 reduce-scatter.4
  1562.6 708.3 reduce-scatter.10
  2274.0 705.8 reduce-scatter.8
where the time goes:
time: 2990 us
  waiting for transfers between devices  2560 us (86%)
  matrix products  224 us (7%)
  blocking collectives  121 us (4%)
  local copies, waits for them, and re-layouts  35.9 us (1%)
    reduce_scatter x1, waiting for transfers between devices, sharded_path(): lax.psum_scatter(grad_fc2, ('seq', 'batch'), scatter_dimension=0, tiled=T...  711 us
    reduce_scatter x1, waiting for transfers between devices, sharded_path(): lax.psum_scatter(grad_fc1, ('seq', 'batch'), scatter_dimension=0, tiled=T...  709 us
    reduce_scatter x1, waiting for transfers between devices, sharded_path(): lax.psum_scatter(grad_wqkv, ('seq', 'batch'), scatter_dimension=0, tiled=...  438 us
    all_gather x1, waiting for transfers between devices, sharded_path(): lax.all_gather(w_fc1, ('seq', 'batch'), axis=0, tiled=True)  186 us
    reduce_scatter x1, waiting for transfers between devices, sharded_path(): lax.psum_scatter(grad_wout, ('seq', 'batch'), scatter_dimension=0, tiled=...  180 us
    all_gather x1, waiting for transfers between devices, sharded_path(): lax.all_gather(w_fc2, ('seq', 'batch'), axis=0, tiled=True)  178 us
    all_gather x1, waiting for transfers between devices, sharded_path(): lax.all_gather(w_qkv, ('seq', 'batch'), axis=0, tiled=True)  72.8 us
    ppermute x2, waiting for transfers between devices, from_behind(): lax.ppermute(value, axis, [(source, source + steps) for source in range(f...  71.6 us
  transfers between devices with their start and end apart: 11, of which 10 were waited for; matrix products, arithmetic and copies ran while one was open for 6% of the time, Pallas kernels for 0%

commit v1 on v0

v1 whole, which is shorter than its diff:
```python
import jax
import jax.numpy as jnp
from jax import lax
from jax.sharding import PartitionSpec as P

HEAD_DIM = 128
WINDOW = 256
EPS = 1e-05
BF = jnp.bfloat16
F32 = jnp.float32


def swap(value, bit):
    count = lax.axis_size("seq")
    return lax.ppermute(value, "seq", [(i, i ^ bit) for i in range(count)])


def gather_xor(value):
    half = value.shape[0] // 2
    by_x = swap(value, 1)
    by_y = swap(value, 2)
    far_top = swap(by_x[:half], 2)
    far_low = swap(by_y[half:], 1)
    return [value, by_x, by_y, jnp.concatenate([far_top, far_low], 0)]


def gather_seq(value):
    count = lax.axis_size("seq")
    if count != 4:
        return lax.all_gather(value, "seq", axis=0, tiled=False)
    me = lax.axis_index("seq")
    got = gather_xor(value)
    out = jnp.zeros((4,) + value.shape, value.dtype)
    for k in range(4):
        out = lax.dynamic_update_index_in_dim(out, got[k], me ^ k, 0)
    return out


def scatter_seq(parts):
    count = lax.axis_size("seq")
    if count != 4:
        return lax.psum_scatter(parts.astype(BF).astype(F32), "seq", scatter_dimension=0, tiled=False)
    me = lax.axis_index("seq")
    half = parts.shape[1] // 2
    own, to_x, to_y, far = (lax.dynamic_index_in_dim(parts, me ^ k, 0, keepdims=False) for k in range(4))
    far = far.astype(BF)
    via_y = swap(far[:half], 2)
    via_x = swap(far[half:], 1)
    x_low = swap(to_x[half:].astype(BF), 1)
    y_top = swap(to_y[:half].astype(BF), 2)
    x_top = swap((to_x[:half] + via_y.astype(F32)).astype(BF), 1)
    y_low = swap((to_y[half:] + via_x.astype(F32)).astype(BF), 2)
    top = own[:half] + x_top.astype(F32) + y_top.astype(F32)
    low = own[half:] + x_low.astype(F32) + y_low.astype(F32)
    return jnp.concatenate([top, low], 0)


def scatter_batch(parts):
    flat = parts.astype(BF).reshape(-1, parts.shape[-1])
    return lax.psum_scatter(flat, "batch", scatter_dimension=0, tiled=True).reshape(parts.shape[1:])


def norm_stats(values):
    mean = jnp.mean(values, -1, keepdims=True)
    centred = values - mean
    rstd = lax.rsqrt(jnp.mean(centred * centred, -1, keepdims=True) + EPS)
    return centred * rstd, rstd


def norm_back(grad, normed, rstd, gain):
    dn = grad * gain
    return rstd * (
        dn - jnp.mean(dn, -1, keepdims=True) - normed * jnp.mean(dn * normed, -1, keepdims=True)
    )


def block_masks(count, rows, length):
    shape = (count, rows, rows + WINDOW)
    start = lax.broadcasted_iota(jnp.int32, shape, 0) * rows
    query_pos = start + lax.broadcasted_iota(jnp.int32, shape, 1)
    key_pos = start - WINDOW + lax.broadcasted_iota(jnp.int32, shape, 2)
    return (
        (key_pos >= 0)
        & (key_pos <= query_pos)
        & (query_pos - key_pos < WINDOW)
        & ((key_pos < length) | (key_pos == query_pos))
    )


def windows(value):
    prior = jnp.concatenate([jnp.zeros_like(value[:1]), value[:-1]], 0)
    return jnp.concatenate([prior, value], 1)


def unwindow(grad):
    rows = grad.shape[1] // 2
    own, prior = grad[:, rows:], grad[:, :rows]
    return own + jnp.concatenate([prior[1:], jnp.zeros_like(prior[:1])], 0)


def body(
    block_input,
    lengths,
    ln1_gain,
    ln1_bias,
    w_qkv,
    qv_bias,
    w_out,
    out_bias,
    ln2_gain,
    ln2_bias,
    w_fc1,
    fc1_bias,
    w_fc2,
    fc2_bias,
    out_cotangent,
):
    ns, nb = lax.axis_size("seq"), lax.axis_size("batch")
    seq = lax.axis_index("seq")
    rows, width = block_input.shape[1:]
    share = width // ns
    heads = share // HEAD_DIM
    tokens = ns * rows
    hidden = w_fc1.shape[1] // ns
    depth = w_fc1.shape[0]
    scale = HEAD_DIM ** (-0.5)
    length = lengths[0]

    vectors = (ln1_gain, ln1_bias, qv_bias, out_bias, ln2_gain, ln2_bias, fc1_bias, fc2_bias)
    packed = lax.all_gather(jnp.concatenate(vectors), ("seq", "batch"), axis=0, tiled=False)
    full, at = [], 0
    for vec in vectors:
        full.append(packed[:, at : at + vec.shape[0]].reshape(-1).astype(F32))
        at += vec.shape[0]
    gain1, shift1, qv, obias, gain2, shift2, bias1, bias2 = full
    bias1 = lax.dynamic_slice_in_dim(bias1, seq * hidden, hidden)
    qbias = lax.dynamic_slice_in_dim(qv[:width], seq * share, share)
    vbias = lax.dynamic_slice_in_dim(qv[width:], seq * share, share)

    qkv_part = lax.all_to_all(w_qkv.reshape(depth, 3, ns, share), "seq", 2, 0)
    qkv_part = lax.all_gather(qkv_part.reshape(ns, depth, 3 * share), "batch", axis=0)
    wqkv = qkv_part.transpose(1, 0, 2, 3).reshape(width, 3 * share)
    wout = lax.all_gather(w_out, "batch", axis=0, tiled=True)
    fc1_part = lax.all_to_all(w_fc1.reshape(depth, ns, hidden), "seq", 1, 0)
    fc1_part = lax.all_gather(fc1_part, "batch", axis=0)
    w1 = fc1_part.transpose(1, 0, 2, 3).reshape(width, hidden)
    w2 = lax.all_gather(w_fc2, "batch", axis=0, tiled=True)

    mine = block_input[0]
    acts = gather_seq(mine).reshape(tokens, width).astype(F32)
    normed1, _ = norm_stats(acts)
    h1 = (normed1 * gain1 + shift1).astype(BF)
    proj = jnp.dot(h1, wqkv, preferred_element_type=F32)
    shape = (ns, rows, heads, HEAD_DIM)
    q = (proj[:, :share] + qbias).astype(BF).reshape(shape)
    k = windows(proj[:, share : 2 * share].astype(BF).reshape(shape))
    v = windows((proj[:, 2 * share :] + vbias).astype(BF).reshape(shape))
    mask = block_masks(ns, rows, length)[:, None]
    scores = jnp.einsum("nqhd,nkhd->nhqk", q, k, preferred_element_type=F32) * scale
    scores = jnp.where(mask, scores, -1e30)
    top = jnp.max(scores, -1, keepdims=True)
    expo = jnp.exp(scores - top)
    total = jnp.sum(expo, -1, keepdims=True)
    probs = expo / total
    probs_low = probs.astype(BF)
    o = jnp.einsum("nhqk,nkhd->nqhd", probs_low, v, preferred_element_type=F32)
    o = o.astype(BF).reshape(tokens, share)
    a = jnp.dot(o, wout, preferred_element_type=F32)
    a = scatter_seq(a.reshape(ns, rows, width))
    mine_f = mine.astype(F32)
    x1 = mine_f + (a + obias)
    normed2, rstd2 = norm_stats(x1)
    h2_mine = (normed2 * gain2 + shift2).astype(BF)

    cot_mine = out_cotangent[0]
    h2 = gather_seq(h2_mine).reshape(tokens, width)
    cot = gather_seq(cot_mine).reshape(tokens, width)
    u = jnp.dot(h2, w1, preferred_element_type=F32) + bias1
    g, pull = jax.vjp(lambda t: jax.nn.gelu(t, approximate=True), u)
    g = g.astype(BF)
    y = jnp.dot(g, w2, preferred_element_type=F32)
    dg = jnp.einsum("td,fd->tf", cot, w2, preferred_element_type=F32)
    du = pull(dg)[0].astype(BF)
    gw2 = jnp.einsum("tf,td->fd", g, cot, preferred_element_type=F32)
    gw1 = jnp.einsum("td,tf->df", h2, du, preferred_element_type=F32)
    gb1 = jnp.sum(du.astype(F32), 0)
    dh2 = jnp.einsum("tf,df->td", du, w1, preferred_element_type=F32)
    gw2 = scatter_batch(gw2.reshape(nb, -1, width))
    gw1 = scatter_batch(gw1.reshape(ns, nb, depth, hidden).transpose(1, 0, 2, 3))
    dh2 = scatter_seq(dh2.reshape(ns, rows, width))
    y = scatter_seq(y.reshape(ns, rows, width))
    out = (x1 + (y + bias2)).astype(BF)
    gb2 = jnp.sum(cot_mine.astype(F32), 0)
    cot_f = cot_mine.astype(F32)
    ggain2 = jnp.sum(dh2 * normed2, 0)
    gshift2 = jnp.sum(dh2, 0)
    dx1 = cot_f + norm_back(dh2, normed2, rstd2, gain2)
    da_mine = dx1.astype(BF)

    gob = jnp.sum(da_mine.astype(F32), 0)
    da = gather_seq(da_mine).reshape(tokens, width)
    gwo = jnp.einsum("td,te->de", o, da, preferred_element_type=F32)
    do = jnp.einsum("te,de->td", da, wout, preferred_element_type=F32).astype(BF).reshape(shape)
    dp = jnp.einsum("nqhd,nkhd->nhqk", do, v, preferred_element_type=F32)
    ds = (probs * (dp - jnp.sum(dp * probs, -1, keepdims=True))).astype(BF)
    dq = jnp.einsum("nhqk,nkhd->nqhd", ds, k, preferred_element_type=F32) * scale
    dk = unwindow(jnp.einsum("nhqk,nqhd->nkhd", ds, q, preferred_element_type=F32)) * scale
    dv = unwindow(jnp.einsum("nhqk,nqhd->nkhd", probs_low, do, preferred_element_type=F32))
    dproj = jnp.concatenate([t.astype(BF).reshape(tokens, share) for t in (dq, dk, dv)], 1)
    gwqkv = jnp.einsum("td,te->de", h1, dproj, preferred_element_type=F32)
    gqv = jnp.sum(dproj.astype(F32), 0)
    dh1 = jnp.einsum("te,de->td", dproj, wqkv, preferred_element_type=F32)
    gwo = scatter_batch(gwo.reshape(nb, depth, width))
    gwqkv = scatter_batch(gwqkv.reshape(ns, nb, depth, 3 * share).transpose(1, 0, 2, 3))
    dh1 = scatter_seq(dh1.reshape(ns, rows, width))
    nmine, rmine = norm_stats(mine_f)
    ggain1 = jnp.sum(dh1 * nmine, 0)
    gshift1 = jnp.sum(dh1, 0)
    gx = dx1 + norm_back(dh1, nmine, rmine, gain1)

    gw1 = lax.all_to_all(gw1.astype(BF), "seq", 0, 1).astype(F32).reshape(depth, ns * hidden)
    gwqkv = lax.all_to_all(gwqkv.astype(BF).reshape(ns, depth, 3, share), "seq", 0, 2)
    gwqkv = gwqkv.astype(F32).reshape(depth, 3 * width)

    def place(part, size):
        return lax.dynamic_update_slice_in_dim(jnp.zeros((size,), F32), part, seq * part.shape[0], 0)

    gqv = jnp.concatenate([place(gqv[:share], width), place(gqv[2 * share :], width)])
    sums = (ggain1, gshift1, gqv, gob, ggain2, gshift2, place(gb1, ns * hidden), gb2)
    sums = jnp.concatenate([t.reshape(ns * nb, -1) for t in sums], 1)
    sums = lax.psum_scatter(sums, ("seq", "batch"), scatter_dimension=0, tiled=True)[0]
    small, at = [], 0
    for vec in vectors:
        small.append(sums[at : at + vec.shape[0]])
        at += vec.shape[0]
    return (
        out[None],
        gx[None],
        small[0],
        small[1],
        gwqkv,
        small[2],
        gwo.astype(F32),
        small[3],
        small[4],
        small[5],
        gw1,
        small[6],
        gw2.astype(F32),
        small[7],
    )


def solution(mesh):
    shard = P(("seq", "batch"))
    shard2 = P(("seq", "batch"), None)
    acts = P("batch", "seq", None)
    return jax.shard_map(
        body,
        mesh=mesh,
        in_specs=(acts, P("batch"), shard, shard, shard2, shard, shard2, shard, shard, shard, shard2, shard, shard2, shard, acts),
        out_specs=(acts, acts, shard, shard, shard2, shard, shard2, shard, shard, shard, shard2, shard, shard2, shard),
        check_vma=False,
    )
```

time: 2990 us -> 911 us (0.30)
  waiting for transfers between devices: 2560 us -> 398 us
  local copies, waits for them, and re-layouts: 35.9 us -> 147 us
  matrix products: 224 us -> 150 us
  other arithmetic: 21.4 us -> 74 us
  blocking collectives: 121 us -> 75.4 us
  starting transfers between devices: 6.6 us -> 41.4 us
    reduce_scatter x4, waiting for transfers between devices: 2040 us -> 120 us  [scatter_batch(): lax.psum_scatter(flat, 'batch', scatter_dimension=0, tiled=True)]
    all_gather x4, waiting for transfers between devices: 436 us -> 0.03 us  [the longest x1 0.02 us: body(): wout = lax.all_gather(w_out, 'batch', axis=0, tiled=True)]
    ppermute x2 -> x40, waiting for transfers between devices: 71.6 us -> 167 us  [swap(): return lax.ppermute(value, 'seq', [(i, i ^ bit) for i in range(count)])]
    unnamed x10, waiting for transfers between devices: 16.5 us -> 101 us
    dot_general x18, matrix products: 224 us -> 150 us  [the longest x1 19.4 us: body(): dg = jnp.einsum('td,fd->tf', cot, w2, preferred_element_type=F32)]
    unnamed x1 -> x0, blocking collectives: 43.8 us -> none
    convert_element_type x0 -> x24, local copies, waits for them, and re-layouts: none -> 37.6 us  [the longest x2 11.8 us: scatter_batch(): flat = parts.astype(BF).reshape(-1, parts.shape[-1])]
    all_gather x2 -> x1, blocking collectives: 77.2 us -> 43 us  [body(): lax.all_gather(jnp.concatenate(vectors), ('seq', 'batch'), axis=0, tiled=...]
  transfers between devices with their start and end apart: 11 -> 51, of which waited for: 10 -> 32; matrix products, arithmetic and copies ran while one was open for 6% -> 29% of each run, Pallas kernels for 0% -> 0%
where the time goes in v1:
time: 911 us; the launch traced here: 903 us
  waiting for transfers between devices  398 us (44%)
  matrix products  150 us (16%)
  local copies, waits for them, and re-layouts  147 us (16%)
  blocking collectives  75.4 us (8%)
  other arithmetic  74 us (8%)
  starting transfers between devices  41.4 us (5%)
  between operations  16.3 us (2%)
    ppermute x40, waiting for transfers between devices, swap(): return lax.ppermute(value, 'seq', [(i, i ^ bit) for i in range(count)])  167 us
    reduce_scatter x4, waiting for transfers between devices, scatter_batch(): lax.psum_scatter(flat, 'batch', scatter_dimension=0, tiled=True)  120 us
    unnamed x10, waiting for transfers between devices  101 us
    all_gather x1, blocking collectives, body(): lax.all_gather(jnp.concatenate(vectors), ('seq', 'batch'), axis=0, tiled=...  43 us
    ppermute x40, starting transfers between devices, swap(): return lax.ppermute(value, 'seq', [(i, i ^ bit) for i in range(count)])  32.3 us
    dot_general x1, matrix products, body(): dg = jnp.einsum('td,fd->tf', cot, w2, preferred_element_type=F32)  19.4 us
  transfers between devices with their start and end apart: 51, of which 32 were waited for; matrix products, arithmetic and copies ran while one was open for 29% of the time, Pallas kernels for 0%

profile of v1, /device:TPU:0, one launch (start us, length us, event | category | flops | bytes accessed | tf_op | source)
XLA Modules:
  0.0 902.8 jit_solution(6805463985590968957)
XLA Ops:
  9.7 16.4 %all_to_all.48 = bf16[1,64,3,4,512]{4,1,2,0,3:T(8,128)(2,1)S(1)} all-to-all(bf16[1,64,3,4,512]{4,1,2,0,3:T(8,128)(2,1)S(1)} %copy.137), channel_id=1, replica_groups=mesh['seq'=4,'batch'=8] {'seq'}, dimensions={3} | all-to-all | bytes 1572864 | tf_op jit(solution)/shard_map/all_to_all | solution.py:140
  31.0 16.0 %all_to_all.49 = bf16[1,64,4,2048]{3,1,0,2:T(8,128)(2,1)} all-to-all(bf16[1,64,4,2048]{3,1,0,2:T(8,128)(2,1)S(1)} %copy.146), channel_id=1, replica_groups=mesh['seq'=4,'batch'=8] {'seq'}, dimensions={2} | all-to-all | bytes 2097152 | tf_op jit(solution)/shard_map/all_to_all | solution.py:144
  48.9 43.0 %all-gather.2 = bf16[32,1,768]{2,1,0:T(2,128)(2,1)S(1)} all-gather(bf16[1,1,768]{2,1,0:T(2,128)(2,1)S(1)} %reshape.804), channel_id=2, replica_groups=mesh['seq'=4,'batch'=8] {'seq','batch'}, dimensions={0}, use_global_device_ids=true | all-gather | bytes 50688 | tf_op jit(solution)/shard_map/all_gather | solution.py:130
  97.0 13.1 %collective-permute-done.2 = bf16[128,2048]{1,0:T(8,128)(2,1)S(1)} collective-permute-done((bf16[128,2048]{1,0:T(8,128)(2,1)S(1)}, bf16[128,2048]{1,0:T(8,128)(2,1)S(1)}, u32[]{:S(2)}, u32[]{:S(2)}) %collective-permute-start.2) | collective-permute-done | bytes 524320 | tf_op jit(solution)/shard_map/ppermute | solution.py:15
  120.1 6.6 fusion.165
  153.7 6.3 fusion.166
  160.1 5.1 fusion.76
  180.5 6.2 collective-permute-done.4
  191.3 20.0 %collective-permute-done.8 = bf16[128,2048]{1,0:T(8,128)(2,1)S(1)} collective-permute-done((bf16[128,2048]{1,0:T(8,128)(2,1)}, bf16[128,2048]{1,0:T(8,128)(2,1)S(1)}, u32[]{:S(2)}, u32[]{:S(2)}) %collective-permute-start.8) | collective-permute-done | bytes 524320 | tf_op jit(solution)/shard_map/ppermute | solution.py:15
  211.4 7.2 collective-permute-done.6
  233.8 6.9 collective-permute-done.9
  247.1 4.8 collective-permute-done.22
  257.0 8.7 collective-permute-done.10
  267.1 7.2 collective-permute-done.11
  276.7 4.6 collective-permute-done.12
  284.8 8.3 copy.148
  293.1 16.8 %fusion.15 = (bf16[2048,1024]{0,1:T(8,128)(2,1)}, f32[1024,2048]{1,0:T(8,128)}) fusion(f32[2048]{0:T(1024)S(1)} %dynamic_slice.64, bf16[1024,2048]{1,0:T(8,128)(2,1)} %bitcast.28, bf16[2048,2048]{1,0:T(8,128)(2,1)} %bitcast.386), kind=kOutput, calls=%fused_computation.18 | convolution fusion | flops 8610906112 | bytes 25174016 | tf_op jit(solution)/shard_map/dot_general | solution.py:178
  309.8 19.4 %convert_reduce_fusion = (f32[2048]{0:T(1024)}, bf16[1024,2048]{1,0:T(8,128)(2,1)S(1)}) fusion(f32[1024,2048]{1,0:T(8,128)} %get-tuple-element.89, f32[2048]{0:T(1024)S(1)} %dynamic_slice.64, bf16[1024,2048]{1,0:T(8,128)(2,1)} %bitcast.403, bf16[2048,2048]{1,0:T(8,128)(2,1)} %all-gather.12.cloned.1.call-done), kind=kOutput, calls=%fused_computation.21 | convolution fusion | flops 8638167040 | bytes 25182208 | tf_op jit(solution)/shard_map/td,fd->tf/dot_general | solution.py:182
  329.2 11.2 %fusion.167 = f32[4,256,2048]{2,1,0:T(8,128)} fusion(bf16[4,256,2048]{2,1,0:T(8,128)(2,1)S(1)} %bitcast.429, bf16[2048,2048,1]{1,0,2:T(8,128)(2,1)S(1)} %bitcast.387), kind=kOutput, calls=%fused_computation.300 | convolution fusion | flops 8589934592 | bytes 20971520 | tf_op jit(solution)/shard_map/tf,df->td/dot_general | solution.py:187
  347.0 8.5 collective-permute-done.24
  361.1 8.6 collective-permute-done.25
  373.5 6.9 copy.160
  380.4 5.6 collective-permute-done.29
  399.4 12.4 %collective-permute-done.30 = bf16[256,2048]{1,0:T(8,128)(2,1)S(1)} collective-permute-done((bf16[256,2048]{1,0:T(8,128)(2,1)S(1)}, bf16[256,2048]{1,0:T(8,128)(2,1)S(1)}, u32[]{:S(2)}, u32[]{:S(2)}) %collective-permute-start.30) | collective-permute-done | bytes 1048608 | tf_op jit(solution)/shard_map/ppermute | solution.py:15
  413.0 8.1 collective-permute-done.32
  430.2 6.3 multiply_reduce_fusion
  436.5 4.3 multiply_convert_fusion
  463.2 8.9 convert_bitcast_fusion.1
  475.5 6.3 copy.166
  481.9 13.9 %convert_bitcast_fusion = bf16[8,4,64,2048]{3,2,0,1:T(8,128)(2,1)} fusion(bf16[4,8,64,1024]{3,2,1,0:T(8,128)(2,1)} %bitcast.401, bf16[1024,2048]{1,0:T(8,128)(2,1)} %copy-done.57), kind=kOutput, calls=%fused_computation.19 | convolution fusion | flops 8594128896 | bytes 16777216 | tf_op jit(solution)/shard_map/td,tf->df/dot_general | solution.py:185
  495.8 8.5 copy.167
  508.7 9.5 %fusion.29 = f32[4,256,2048]{2,1,0:T(8,128)S(1)} fusion(bf16[2048,1536,1]{1,0,2:T(8,128)(2,1)} %bitcast.390, bf16[4,256,512]{2,1,0:T(8,128)(2,1)S(1)} %copy.156, bf16[4,256,512]{2,1,0:T(8,128)(2,1)} %copy.155, bf16[4,256,512]{2,1,0:T(8,128)(2,1)} %copy.154), kind=kOutput, calls=%fused_computation.49 | convolution fusion | flops 6451888128 | bytes 17825792 | tf_op jit(solution)/shard_map/te,de->td/dot_general | solution.py:212
  522.5 6.5 collective-permute-done.34
  545.0 6.4 collective-permute-done.39
  554.7 6.2 convolution_convert_fusion.1
  561.0 6.7 copy.176
  567.6 14.0 %convolution_convert_fusion = bf16[8,256,2048]{2,1,0:T(8,128)(2,1)} fusion(bf16[8,256,1024]{2,1,0:T(8,128)(2,1)} %bitcast.402, bf16[1024,2048,1]{1,0,2:T(8,128)(2,1)} %bitcast.404), kind=kOutput, calls=%fused_computation.33 | convolution fusion | flops 8594128896 | bytes 16777216 | tf_op jit(solution)/shard_map/tf,td->fd/dot_general | solution.py:184
  582.3 15.6 %fusion.17 = f32[1024,2048]{1,0:T(8,128)S(1)} fusion(bf16[2048,2048]{1,0:T(8,128)(2,1)} %all-gather.12.cloned.1.call-done, f32[1024,2048]{1,0:T(8,128)} %get-tuple-element.89, f32[2048]{0:T(1024)S(1)} %copy-done.45), kind=kOutput, calls=%fused_computation.34 | convolution fusion | flops 8610906112 | bytes 25174016 | tf_op jit(solution)/shard_map/dot_general | solution.py:181
  601.9 5.9 collective-permute-done.14
  610.0 4.3 collective-permute-done.18
  614.3 6.1 collective-permute-done.16
  631.1 4.2 all-to-all-start.2
  638.0 9.8 %all-to-all-done.2 = bf16[4,64,3,1,512]{4,1,3,2,0:T(8,128)(2,1)} async-done(((bf16[4,64,3,1,512]{4,1,3,2,0:T(8,128)(2,1)}), bf16[4,64,3,1,512]{4,1,3,2,0:T(8,128)(2,1)}, u32[]{:S(2)}, u32[]{:S(2)}) %all-to-all-start.2) | async-done | bytes 786464 | tf_op jit(solution)/shard_map/all_to_all | solution.py:222
  647.8 4.6 all-to-all-start.3
  652.4 4.4 fusion.47
  656.8 100.7 %all-reduce.7.cloned.1.call-done = f32[32,768]{1,0:T(8,128)} async-done(((f32[32,768]{1,0:T(8,128)}), f32[32,768]{1,0:T(8,128)}) %all-reduce.7.cloned.1.call-update) | async-done | bytes 98320
  761.5 35.5 %reduce-scatter.7.cloned.1.call-done = bf16[64,2048]{1,0:T(8,128)(2,1)} async-done(((bf16[512,2048]{1,0:T(8,128)(2,1)}), bf16[64,2048]{1,0:T(8,128)(2,1)}) %reduce-scatter.7.cloned.1.call-update) | async-done | bytes 262160 | tf_op jit(solution)/shard_map/reduce_scatter | solution.py:60
  803.3 84.3 %reduce-scatter.11.cloned.1.call-done = bf16[256,2048]{1,0:T(8,128)(2,1)} async-done(((bf16[2048,2048]{1,0:T(8,128)(2,1)}), bf16[256,2048]{1,0:T(8,128)(2,1)}) %reduce-scatter.11.cloned.1.call-update) | async-done | bytes 1048592 | tf_op jit(solution)/shard_map/reduce_scatter | solution.py:60
  (378 shorter events, 235.9 us)
Async XLA Ops:
  7.2 108.9 %all-gather.8.cloned.1.call-start = ((), (), s32[]{:S(2)}) async-start(), calls=%async_computation.8 | async-start | bytes 7077888 | tf_op jit(solution)/shard_map/all_gather | solution.py:141
  28.7 136.5 %all-gather.10.cloned.1.call-start = ((), (), s32[]{:S(2)}) async-start(), calls=%async_computation.9 | async-start | bytes 2359296 | tf_op jit(solution)/shard_map/all_gather | solution.py:143
  29.5 255.2 %all-gather.14.cloned.1.call-start = ((), (), s32[]{:S(2)}) async-start(), calls=%async_computation.15 | async-start | bytes 9437184 | tf_op jit(solution)/shard_map/all_gather | solution.py:145
  47.0 262.8 %all-gather.12.cloned.1.call-start = ((), (), s32[]{:S(2)}) async-start(), calls=%async_computation.10 | async-start | bytes 9437184 | tf_op jit(solution)/shard_map/all_gather | solution.py:147
  47.1 48.7 %collective-permute-start = (bf16[256,2048]{1,0:T(8,128)(2,1)S(1)}, bf16[256,2048]{1,0:T(8,128)(2,1)S(1)}, u32[]{:S(2)}, u32[]{:S(2)}) collective-permute-start(bf16[256,2048]{1,0:T(8,128)(2,1)S(1)} %bitcast.364), channel_id=1, source_target_pairs={{0,8},{8,0},{16,24},{24,16},{1,9},{9,1},{17,25},{25,17},{2,10},{10... | collective-permute-start | bytes 3145736 | tf_op jit(solution)/shard_map/ppermute | solution.py:15
  48.1 48.6 %collective-permute-start.1 = (bf16[256,2048]{1,0:T(8,128)(2,1)S(1)}, bf16[256,2048]{1,0:T(8,128)(2,1)S(1)}, u32[]{:S(2)}, u32[]{:S(2)}) collective-permute-start(bf16[256,2048]{1,0:T(8,128)(2,1)S(1)} %bitcast.365), channel_id=1, source_target_pairs={{0,16},{8,24},{16,0},{24,8},{1,17},{9,25},{17,1},{25,9},{2,18},{10... | collective-permute-start | bytes 3145736 | tf_op jit(solution)/shard_map/ppermute | solution.py:15
  48.7 576.4 %reduce-scatter.5.cloned.1.call-start = ((), (), s32[]{:S(2)}) async-start(), calls=%async_computation.11 | async-start | bytes 7077888 | tf_op jit(solution)/shard_map/reduce_scatter | solution.py:60
  95.8 14.2 %collective-permute-start.2 = (bf16[128,2048]{1,0:T(8,128)(2,1)S(1)}, bf16[128,2048]{1,0:T(8,128)(2,1)S(1)}, u32[]{:S(2)}, u32[]{:S(2)}) collective-permute-start(bf16[128,2048]{1,0:T(8,128)(2,1)S(1)} %slice.442), channel_id=1, source_target_pairs={{0,16},{8,24},{16,0},{24,8},{1,17},{9,25},{17,1},{25,9},{2,18},{10... | collective-permute-start | bytes 1572872 | tf_op jit(solution)/shard_map/ppermute | solution.py:15
  96.7 14.0 %collective-permute-start.3 = (bf16[128,2048]{1,0:T(8,128)(2,1)S(1)}, bf16[128,2048]{1,0:T(8,128)(2,1)S(1)}, u32[]{:S(2)}, u32[]{:S(2)}) collective-permute-start(bf16[128,2048]{1,0:T(8,128)(2,1)S(1)} %slice.443), channel_id=1, source_target_pairs={{0,8},{8,0},{16,24},{24,16},{1,9},{9,1},{17,25},{25,17},{2,10},{10... | collective-permute-start | bytes 1572872 | tf_op jit(solution)/shard_map/ppermute | solution.py:15
  171.5 15.2 %collective-permute-start.4 = (bf16[128,2048]{1,0:T(8,128)(2,1)}, bf16[128,2048]{1,0:T(8,128)(2,1)}, u32[]{:S(2)}, u32[]{:S(2)}) collective-permute-start(bf16[128,2048]{1,0:T(8,128)(2,1)} %get-tuple-element.62), channel_id=1, source_target_pairs={{0,16},{8,24},{16,0},{24,8},{1,17},{9,25},{17,1},{25,9},{2,18},{10... | collective-permute-start | bytes 1572872 | tf_op jit(solution)/shard_map/ppermute | solution.py:15
  173.9 53.2 %collective-permute-start.20 = (bf16[256,2048]{1,0:T(8,128)(2,1)S(1)}, bf16[256,2048]{1,0:T(8,128)(2,1)}, u32[]{:S(2)}, u32[]{:S(2)}) collective-permute-start(bf16[256,2048]{1,0:T(8,128)(2,1)S(1)} %bitcast.376), channel_id=1, source_target_pairs={{0,8},{8,0},{16,24},{24,16},{1,9},{9,1},{17,25},{25,17},{2,10},{10... | collective-permute-start | bytes 3145736 | tf_op jit(solution)/shard_map/ppermute | solution.py:15
  174.1 55.1 %collective-permute-start.21 = (bf16[256,2048]{1,0:T(8,128)(2,1)S(1)}, bf16[256,2048]{1,0:T(8,128)(2,1)S(1)}, u32[]{:S(2)}, u32[]{:S(2)}) collective-permute-start(bf16[256,2048]{1,0:T(8,128)(2,1)S(1)} %bitcast.377), channel_id=1, source_target_pairs={{0,16},{8,24},{16,0},{24,8},{1,17},{9,25},{17,1},{25,9},{2,18},{10... | collective-permute-start | bytes 3145736 | tf_op jit(solution)/shard_map/ppermute | solution.py:15
  175.4 35.9 %collective-permute-start.8 = (bf16[128,2048]{1,0:T(8,128)(2,1)}, bf16[128,2048]{1,0:T(8,128)(2,1)S(1)}, u32[]{:S(2)}, u32[]{:S(2)}) collective-permute-start(bf16[128,2048]{1,0:T(8,128)(2,1)} %get-tuple-element.63), channel_id=1, source_target_pairs={{0,8},{8,0},{16,24},{24,16},{1,9},{9,1},{17,25},{25,17},{2,10},{10... | collective-permute-start | bytes 1572872 | tf_op jit(solution)/shard_map/ppermute | solution.py:15
  179.8 38.8 %collective-permute-start.6 = (bf16[128,2048]{1,0:T(8,128)(2,1)S(1)}, bf16[128,2048]{1,0:T(8,128)(2,1)S(1)}, u32[]{:S(2)}, u32[]{:S(2)}) collective-permute-start(bf16[128,2048]{1,0:T(8,128)(2,1)S(1)} %get-tuple-element.48), channel_id=1, source_target_pairs={{0,16},{8,24},{16,0},{24,8},{1,17},{9,25},{17,1},{25,9},{2,18},{10... | collective-permute-start | bytes 1572872 | tf_op jit(solution)/shard_map/ppermute | solution.py:15
  188.1 34.4 %collective-permute-start.5 = (bf16[128,2048]{1,0:T(8,128)(2,1)S(1)}, bf16[128,2048]{1,0:T(8,128)(2,1)S(1)}, u32[]{:S(2)}, u32[]{:S(2)}) collective-permute-start(bf16[128,2048]{1,0:T(8,128)(2,1)S(1)} %fusion.111), channel_id=1, source_target_pairs={{0,8},{8,0},{16,24},{24,16},{1,9},{9,1},{17,25},{25,17},{2,10},{10... | collective-permute-start | bytes 1572872 | tf_op jit(solution)/shard_map/ppermute | solution.py:15
  211.3 22.6 %collective-permute-start.7 = (bf16[128,2048]{1,0:T(8,128)(2,1)}, bf16[128,2048]{1,0:T(8,128)(2,1)}, u32[]{:S(2)}, u32[]{:S(2)}) collective-permute-start(bf16[128,2048]{1,0:T(8,128)(2,1)} %get-tuple-element.49), channel_id=1, source_target_pairs={{0,8},{8,0},{16,24},{24,16},{1,9},{9,1},{17,25},{25,17},{2,10},{10... | collective-permute-start | bytes 1572872 | tf_op jit(solution)/shard_map/ppermute | solution.py:15
  225.6 15.2 %collective-permute-start.9 = (bf16[128,2048]{1,0:T(8,128)(2,1)}, bf16[128,2048]{1,0:T(8,128)(2,1)}, u32[]{:S(2)}, u32[]{:S(2)}) collective-permute-start(bf16[128,2048]{1,0:T(8,128)(2,1)} %get-tuple-element.47), channel_id=1, source_target_pairs={{0,16},{8,24},{16,0},{24,8},{1,17},{9,25},{17,1},{25,9},{2,18},{10... | collective-permute-start | bytes 1572872 | tf_op jit(solution)/shard_map/ppermute | solution.py:15
  228.4 23.5 %collective-permute-start.22 = (bf16[128,2048]{1,0:T(8,128)(2,1)S(1)}, bf16[128,2048]{1,0:T(8,128)(2,1)S(1)}, u32[]{:S(2)}, u32[]{:S(2)}) collective-permute-start(bf16[128,2048]{1,0:T(8,128)(2,1)S(1)} %slice.465), channel_id=1, source_target_pairs={{0,16},{8,24},{16,0},{24,8},{1,17},{9,25},{17,1},{25,9},{2,18},{10... | collective-permute-start | bytes 1572872 | tf_op jit(solution)/shard_map/ppermute | solution.py:15
  229.2 22.7 %collective-permute-start.23 = (bf16[128,2048]{1,0:T(8,128)(2,1)S(1)}, bf16[128,2048]{1,0:T(8,128)(2,1)S(1)}, u32[]{:S(2)}, u32[]{:S(2)}) collective-permute-start(bf16[128,2048]{1,0:T(8,128)(2,1)S(1)} %slice.466), channel_id=1, source_target_pairs={{0,8},{8,0},{16,24},{24,16},{1,9},{9,1},{17,25},{25,17},{2,10},{10... | collective-permute-start | bytes 1572872 | tf_op jit(solution)/shard_map/ppermute | solution.py:15
  244.6 21.2 %collective-permute-start.10 = (bf16[256,2048]{1,0:T(8,128)(2,1)S(1)}, bf16[256,2048]{1,0:T(8,128)(2,1)S(1)}, u32[]{:S(2)}, u32[]{:S(2)}) collective-permute-start(bf16[256,2048]{1,0:T(8,128)(2,1)S(1)} %add_convert_fusion.2), channel_id=1, source_target_pairs={{0,8},{8,0},{16,24},{24,16},{1,9},{9,1},{17,25},{25,17},{2,10},{10... | collective-permute-start | bytes 3145736 | tf_op jit(solution)/shard_map/ppermute | solution.py:15
  244.8 29.6 %collective-permute-start.11 = (bf16[256,2048]{1,0:T(8,128)(2,1)S(1)}, bf16[256,2048]{1,0:T(8,128)(2,1)S(1)}, u32[]{:S(2)}, u32[]{:S(2)}) collective-permute-start(bf16[256,2048]{1,0:T(8,128)(2,1)S(1)} %add_convert_fusion.2), channel_id=1, source_target_pairs={{0,16},{8,24},{16,0},{24,8},{1,17},{9,25},{17,1},{25,9},{2,18},{10... | collective-permute-start | bytes 3145736 | tf_op jit(solution)/shard_map/ppermute | solution.py:15
  265.8 15.5 %collective-permute-start.12 = (bf16[128,2048]{1,0:T(8,128)(2,1)S(1)}, bf16[128,2048]{1,0:T(8,128)(2,1)S(1)}, u32[]{:S(2)}, u32[]{:S(2)}) collective-permute-start(bf16[128,2048]{1,0:T(8,128)(2,1)S(1)} %slice.459), channel_id=1, source_target_pairs={{0,16},{8,24},{16,0},{24,8},{1,17},{9,25},{17,1},{25,9},{2,18},{10... | collective-permute-start | bytes 1572872 | tf_op jit(solution)/shard_map/ppermute | solution.py:15
  274.4 9.2 %collective-permute-start.13 = (bf16[128,2048]{1,0:T(8,128)(2,1)S(1)}, bf16[128,2048]{1,0:T(8,128)(2,1)S(1)}, u32[]{:S(2)}, u32[]{:S(2)}) collective-permute-start(bf16[128,2048]{1,0:T(8,128)(2,1)S(1)} %slice.460), channel_id=1, source_target_pairs={{0,8},{8,0},{16,24},{24,16},{1,9},{9,1},{17,25},{25,17},{2,10},{10... | collective-permute-start | bytes 1572872 | tf_op jit(solution)/shard_map/ppermute | solution.py:15
  342.2 13.2 %collective-permute-start.24 = (bf16[128,2048]{1,0:T(8,128)(2,1)S(1)}, bf16[128,2048]{1,0:T(8,128)(2,1)S(1)}, u32[]{:S(2)}, u32[]{:S(2)}) collective-permute-start(bf16[128,2048]{1,0:T(8,128)(2,1)S(1)} %get-tuple-element.58), channel_id=1, source_target_pairs={{0,16},{8,24},{16,0},{24,8},{1,17},{9,25},{17,1},{25,9},{2,18},{10... | collective-permute-start | bytes 1572872 | tf_op jit(solution)/shard_map/ppermute | solution.py:15
  343.6 15.3 %collective-permute-start.28 = (bf16[128,2048]{1,0:T(8,128)(2,1)S(1)}, bf16[128,2048]{1,0:T(8,128)(2,1)S(1)}, u32[]{:S(2)}, u32[]{:S(2)}) collective-permute-start(bf16[128,2048]{1,0:T(8,128)(2,1)S(1)} %get-tuple-element.59), channel_id=1, source_target_pairs={{0,8},{8,0},{16,24},{24,16},{1,9},{9,1},{17,25},{25,17},{2,10},{10... | collective-permute-start | bytes 1572872 | tf_op jit(solution)/shard_map/ppermute | solution.py:15
  346.2 14.9 %collective-permute-start.26 = (bf16[128,2048]{1,0:T(8,128)(2,1)S(1)}, bf16[128,2048]{1,0:T(8,128)(2,1)S(1)}, u32[]{:S(2)}, u32[]{:S(2)}) collective-permute-start(bf16[128,2048]{1,0:T(8,128)(2,1)S(1)} %get-tuple-element.40), channel_id=1, source_target_pairs={{0,16},{8,24},{16,0},{24,8},{1,17},{9,25},{17,1},{25,9},{2,18},{10... | collective-permute-start | bytes 1572872 | tf_op jit(solution)/shard_map/ppermute | solution.py:15
  356.8 12.9 %collective-permute-start.25 = (bf16[128,2048]{1,0:T(8,128)(2,1)S(1)}, bf16[128,2048]{1,0:T(8,128)(2,1)S(1)}, u32[]{:S(2)}, u32[]{:S(2)}) collective-permute-start(bf16[128,2048]{1,0:T(8,128)(2,1)S(1)} %fusion.93), channel_id=1, source_target_pairs={{0,8},{8,0},{16,24},{24,16},{1,9},{9,1},{17,25},{25,17},{2,10},{10... | collective-permute-start | bytes 1572872 | tf_op jit(solution)/shard_map/ppermute | solution.py:15
  358.4 21.9 %collective-permute-start.27 = (bf16[128,2048]{1,0:T(8,128)(2,1)}, bf16[128,2048]{1,0:T(8,128)(2,1)}, u32[]{:S(2)}, u32[]{:S(2)}) collective-permute-start(bf16[128,2048]{1,0:T(8,128)(2,1)} %get-tuple-element.41), channel_id=1, source_target_pairs={{0,8},{8,0},{16,24},{24,16},{1,9},{9,1},{17,25},{25,17},{2,10},{10... | collective-permute-start | bytes 1572872 | tf_op jit(solution)/shard_map/ppermute | solution.py:15
  372.7 13.2 %collective-permute-start.29 = (bf16[128,2048]{1,0:T(8,128)(2,1)}, bf16[128,2048]{1,0:T(8,128)(2,1)}, u32[]{:S(2)}, u32[]{:S(2)}) collective-permute-start(bf16[128,2048]{1,0:T(8,128)(2,1)} %get-tuple-element.39), channel_id=1, source_target_pairs={{0,16},{8,24},{16,0},{24,8},{1,17},{9,25},{17,1},{25,9},{2,18},{10... | collective-permute-start | bytes 1572872 | tf_op jit(solution)/shard_map/ppermute | solution.py:15
  391.3 20.5 %collective-permute-start.30 = (bf16[256,2048]{1,0:T(8,128)(2,1)S(1)}, bf16[256,2048]{1,0:T(8,128)(2,1)S(1)}, u32[]{:S(2)}, u32[]{:S(2)}) collective-permute-start(bf16[256,2048]{1,0:T(8,128)(2,1)S(1)} %get-tuple-element.27), channel_id=1, source_target_pairs={{0,8},{8,0},{16,24},{24,16},{1,9},{9,1},{17,25},{25,17},{2,10},{10... | collective-permute-start | bytes 3145736 | tf_op jit(solution)/shard_map/ppermute | solution.py:15
  391.4 21.3 %collective-permute-start.31 = (bf16[256,2048]{1,0:T(8,128)(2,1)S(1)}, bf16[256,2048]{1,0:T(8,128)(2,1)S(1)}, u32[]{:S(2)}, u32[]{:S(2)}) collective-permute-start(bf16[256,2048]{1,0:T(8,128)(2,1)S(1)} %get-tuple-element.27), channel_id=1, source_target_pairs={{0,16},{8,24},{16,0},{24,8},{1,17},{9,25},{17,1},{25,9},{2,18},{10... | collective-permute-start | bytes 3145736 | tf_op jit(solution)/shard_map/ppermute | solution.py:15
  475.5 172.3 %reduce-scatter.9.cloned.1.call-start = ((), (), s32[]{:S(2)}) async-start(), calls=%async_computation.13 | async-start | bytes 9437184 | tf_op jit(solution)/shard_map/reduce_scatter | solution.py:60
  504.3 253.1 %all-reduce.7.cloned.1.call-start = ((), (), s32[]{:S(2)}) async-start(), calls=%async_computation.16 | async-start | bytes 196608
  519.2 9.8 %collective-permute-start.34 = (bf16[128,2048]{1,0:T(8,128)(2,1)S(1)}, bf16[128,2048]{1,0:T(8,128)(2,1)S(1)}, u32[]{:S(2)}, u32[]{:S(2)}) collective-permute-start(bf16[128,2048]{1,0:T(8,128)(2,1)S(1)} %get-tuple-element.56), channel_id=1, source_target_pairs={{0,16},{8,24},{16,0},{24,8},{1,17},{9,25},{17,1},{25,9},{2,18},{10... | collective-permute-start | bytes 1572872 | tf_op jit(solution)/shard_map/ppermute | solution.py:15
  520.6 16.7 %collective-permute-start.38 = (bf16[128,2048]{1,0:T(8,128)(2,1)}, bf16[128,2048]{1,0:T(8,128)(2,1)}, u32[]{:S(2)}, u32[]{:S(2)}) collective-permute-start(bf16[128,2048]{1,0:T(8,128)(2,1)} %get-tuple-element.57), channel_id=1, source_target_pairs={{0,8},{8,0},{16,24},{24,16},{1,9},{9,1},{17,25},{25,17},{2,10},{10... | collective-permute-start | bytes 1572872 | tf_op jit(solution)/shard_map/ppermute | solution.py:15
  522.0 17.7 %collective-permute-start.36 = (bf16[128,2048]{1,0:T(8,128)(2,1)}, bf16[128,2048]{1,0:T(8,128)(2,1)}, u32[]{:S(2)}, u32[]{:S(2)}) collective-permute-start(bf16[128,2048]{1,0:T(8,128)(2,1)} %get-tuple-element.37), channel_id=1, source_target_pairs={{0,16},{8,24},{16,0},{24,8},{1,17},{9,25},{17,1},{25,9},{2,18},{10... | collective-permute-start | bytes 1572872 | tf_op jit(solution)/shard_map/ppermute | solution.py:15
  530.0 9.8 %collective-permute-start.35 = (bf16[128,2048]{1,0:T(8,128)(2,1)}, bf16[128,2048]{1,0:T(8,128)(2,1)}, u32[]{:S(2)}, u32[]{:S(2)}) collective-permute-start(bf16[128,2048]{1,0:T(8,128)(2,1)} %fusion.85), channel_id=1, source_target_pairs={{0,8},{8,0},{16,24},{24,16},{1,9},{9,1},{17,25},{25,17},{2,10},{10... | collective-permute-start | bytes 1572872 | tf_op jit(solution)/shard_map/ppermute | solution.py:15
  532.8 12.1 %collective-permute-start.37 = (bf16[128,2048]{1,0:T(8,128)(2,1)}, bf16[128,2048]{1,0:T(8,128)(2,1)S(1)}, u32[]{:S(2)}, u32[]{:S(2)}) collective-permute-start(bf16[128,2048]{1,0:T(8,128)(2,1)} %get-tuple-element.38), channel_id=1, source_target_pairs={{0,8},{8,0},{16,24},{24,16},{1,9},{9,1},{17,25},{25,17},{2,10},{10... | collective-permute-start | bytes 1572872 | tf_op jit(solution)/shard_map/ppermute | solution.py:15
  554.6 242.3 %reduce-scatter.7.cloned.1.call-start = ((), (), s32[]{:S(2)}) async-start(), calls=%async_computation.12 | async-start | bytes 2359296 | tf_op jit(solution)/shard_map/reduce_scatter | solution.py:60
  560.9 326.7 %reduce-scatter.11.cloned.1.call-start = ((), (), s32[]{:S(2)}) async-start(), calls=%async_computation.14 | async-start | bytes 9437184 | tf_op jit(solution)/shard_map/reduce_scatter | solution.py:60
  598.1 9.7 %collective-permute-start.14 = (bf16[128,2048]{1,0:T(8,128)(2,1)S(1)}, bf16[128,2048]{1,0:T(8,128)(2,1)S(1)}, u32[]{:S(2)}, u32[]{:S(2)}) collective-permute-start(bf16[128,2048]{1,0:T(8,128)(2,1)S(1)} %get-tuple-element.60), channel_id=1, source_target_pairs={{0,16},{8,24},{16,0},{24,8},{1,17},{9,25},{17,1},{25,9},{2,18},{10... | collective-permute-start | bytes 1572872 | tf_op jit(solution)/shard_map/ppermute | solution.py:15
  600.0 14.3 %collective-permute-start.18 = (bf16[128,2048]{1,0:T(8,128)(2,1)S(1)}, bf16[128,2048]{1,0:T(8,128)(2,1)S(1)}, u32[]{:S(2)}, u32[]{:S(2)}) collective-permute-start(bf16[128,2048]{1,0:T(8,128)(2,1)S(1)} %get-tuple-element.61), channel_id=1, source_target_pairs={{0,8},{8,0},{16,24},{24,16},{1,9},{9,1},{17,25},{25,17},{2,10},{10... | collective-permute-start | bytes 1572872 | tf_op jit(solution)/shard_map/ppermute | solution.py:15
  601.4 19.0 %collective-permute-start.16 = (bf16[128,2048]{1,0:T(8,128)(2,1)S(1)}, bf16[128,2048]{1,0:T(8,128)(2,1)S(1)}, u32[]{:S(2)}, u32[]{:S(2)}) collective-permute-start(bf16[128,2048]{1,0:T(8,128)(2,1)S(1)} %get-tuple-element.44), channel_id=1, source_target_pairs={{0,16},{8,24},{16,0},{24,8},{1,17},{9,25},{17,1},{25,9},{2,18},{10... | collective-permute-start | bytes 1572872 | tf_op jit(solution)/shard_map/ppermute | solution.py:15
  607.9 13.7 %collective-permute-start.15 = (bf16[128,2048]{1,0:T(8,128)(2,1)S(1)}, bf16[128,2048]{1,0:T(8,128)(2,1)S(1)}, u32[]{:S(2)}, u32[]{:S(2)}) collective-permute-start(bf16[128,2048]{1,0:T(8,128)(2,1)S(1)} %fusion.102), channel_id=1, source_target_pairs={{0,8},{8,0},{16,24},{24,16},{1,9},{9,1},{17,25},{25,17},{2,10},{10... | collective-permute-start | bytes 1572872 | tf_op jit(solution)/shard_map/ppermute | solution.py:15
  608.0 27.3 %collective-permute-start.17 = (bf16[128,2048]{1,0:T(8,128)(2,1)}, bf16[128,2048]{1,0:T(8,128)(2,1)}, u32[]{:S(2)}, u32[]{:S(2)}) collective-permute-start(bf16[128,2048]{1,0:T(8,128)(2,1)} %get-tuple-element.45), channel_id=1, source_target_pairs={{0,8},{8,0},{16,24},{24,16},{1,9},{9,1},{17,25},{25,17},{2,10},{10... | collective-permute-start | bytes 1572872 | tf_op jit(solution)/shard_map/ppermute | solution.py:15
  623.2 12.1 %collective-permute-start.19 = (bf16[128,2048]{1,0:T(8,128)(2,1)}, bf16[128,2048]{1,0:T(8,128)(2,1)}, u32[]{:S(2)}, u32[]{:S(2)}) collective-permute-start(bf16[128,2048]{1,0:T(8,128)(2,1)} %get-tuple-element.43), channel_id=1, source_target_pairs={{0,16},{8,24},{16,0},{24,8},{1,17},{9,25},{17,1},{25,9},{2,18},{10... | collective-permute-start | bytes 1572872 | tf_op jit(solution)/shard_map/ppermute | solution.py:15
  631.1 16.7 %all-to-all-start.2 = ((bf16[4,64,3,1,512]{4,1,3,2,0:T(8,128)(2,1)}), bf16[4,64,3,1,512]{4,1,3,2,0:T(8,128)(2,1)}, u32[]{:S(2)}, u32[]{:S(2)}) async-start(bf16[4,64,3,1,512]{4,1,3,2,0:T(8,128)(2,1)} %copy.162), calls=%async_computation.3 | async-start | bytes 1572864 | tf_op jit(solution)/shard_map/all_to_all | solution.py:222
  647.8 242.7 %all-to-all-start.3 = ((bf16[4,64,1,2048]{3,1,2,0:T(8,128)(2,1)}), bf16[4,64,1,2048]{3,1,2,0:T(8,128)(2,1)}, u32[]{:S(2)}, u32[]{:S(2)}) async-start(bf16[4,64,1,2048]{3,1,2,0:T(8,128)(2,1)} %bitcast.418), calls=%async_computation.6 | async-start | bytes 2097152 | tf_op jit(solution)/shard_map/all_to_all | solution.py:221
  (63 other events, 930.7 us)
Sparse Core Ops, SparseCore 0:
  28.8 65.2 all-gather.7
  95.7 27.7 all-gather.9
  125.1 81.5 all-gather.13
  208.2 80.5 all-gather.11
  475.6 66.8 reduce-scatter.4
  544.6 88.0 reduce-scatter.8
  638.3 119.0 all-reduce.6
  760.3 36.6 reduce-scatter.6
  799.3 88.3 reduce-scatter.10

commit v2 on v1

v2 whole, which is shorter than its diff:
```python
import functools
import math

import jax
import jax.numpy as jnp
from jax import lax
from jax.experimental import pallas as pl
from jax.experimental.pallas import tpu as pltpu
from jax.sharding import PartitionSpec as P

HEAD_DIM = 128
WINDOW = 256
EPS = 1e-05
BF = jnp.bfloat16
F32 = jnp.float32
ROOT = math.sqrt(2.0 / math.pi)


def norm_stats(values):
    mean = jnp.mean(values, -1, keepdims=True)
    centred = values - mean
    rstd = lax.rsqrt(jnp.mean(centred * centred, -1, keepdims=True) + EPS)
    return centred * rstd, rstd


def norm_back(grad, normed, rstd, gain):
    dn = grad * gain
    return rstd * (
        dn - jnp.mean(dn, -1, keepdims=True) - normed * jnp.mean(dn * normed, -1, keepdims=True)
    )


def dot_t(left, right):
    return lax.dot_general(left, right, (((1,), (1,)), ((), ())), preferred_element_type=F32)


def t_dot(left, right):
    return lax.dot_general(left, right, (((0,), (0,)), ((), ())), preferred_element_type=F32)


def load_rows(ns, nb, depth, src, dst, sem):
    def one(k, carry):
        s, b = k // nb, lax.rem(k, nb)
        pltpu.make_async_copy(
            src.at[b, pl.ds(s * depth, depth), :], dst.at[pl.ds(k * depth, depth), :], sem
        ).start()
        return carry

    lax.fori_loop(0, ns * nb, one, 0)


def soft_block(query, keys, block, first, length):
    rows, count = query.shape[0], keys.shape[0]
    scores = dot_t(query, keys) * HEAD_DIM ** (-0.5)
    query_pos = block * rows + lax.broadcasted_iota(jnp.int32, (rows, count), 0)
    key_pos = first + lax.broadcasted_iota(jnp.int32, (rows, count), 1)
    back = query_pos - key_pos
    valid = (back >= 0) & (back < WINDOW) & ((key_pos < length) | (back == 0))
    scores = jnp.where(valid, scores, -1e30)
    expo = jnp.exp(scores - jnp.max(scores, -1, keepdims=True))
    return expo / jnp.sum(expo, -1, keepdims=True)


def attend_kernel(ns, nb, length, h1, wq, bias, qkv, o, w, sem):
    tokens, width = h1.shape
    share = o.shape[1]
    rows = tokens // ns
    load_rows(ns, nb, width // (ns * nb), wq, w, sem)
    pltpu.make_async_copy(w, w, sem).wait()
    wide = min(512, 3 * share)

    def project(j, carry):
        cols = pl.ds(pl.multiple_of(j * wide, wide), wide)
        for r in range(0, tokens, 256):
            part = jnp.dot(h1[r : r + 256, :], w[:, cols], preferred_element_type=F32)
            qkv[r : r + 256, cols] = (part + bias[:, cols]).astype(BF)
        return carry

    lax.fori_loop(0, 3 * share // wide, project, 0)
    limit = length[0]

    def head(h, carry):
        at = h * HEAD_DIM
        col_q = pl.ds(pl.multiple_of(at, HEAD_DIM), HEAD_DIM)
        col_k = pl.ds(pl.multiple_of(share + at, HEAD_DIM), HEAD_DIM)
        col_v = pl.ds(pl.multiple_of(2 * share + at, HEAD_DIM), HEAD_DIM)
        for n in range(ns):
            first = max(n - 1, 0) * rows
            mine, seen = slice(n * rows, n * rows + rows), slice(first, first + 2 * rows)
            probs = soft_block(qkv[mine, col_q], qkv[seen, col_k], n, first, limit)
            part = jnp.dot(probs.astype(BF), qkv[seen, col_v], preferred_element_type=F32)
            o[mine, col_q] = part.astype(BF)
        return carry

    lax.fori_loop(0, share // HEAD_DIM, head, 0)


def attend(ns, nb, lengths, h1, wq, bias):
    tokens, width = h1.shape
    share = wq.shape[2] // 3
    vm = pl.BlockSpec(memory_space=pltpu.VMEM)
    return pl.pallas_call(
        functools.partial(attend_kernel, ns, nb),
        out_shape=(
            jax.ShapeDtypeStruct((tokens, 3 * share), BF),
            jax.ShapeDtypeStruct((tokens, share), BF),
        ),
        in_specs=[pl.BlockSpec(memory_space=pltpu.SMEM), vm, pl.BlockSpec(memory_space=pl.ANY), vm],
        out_specs=(vm, vm),
        scratch_shapes=[pltpu.VMEM((width, 3 * share), BF), pltpu.SemaphoreType.DMA],
        compiler_params=pltpu.CompilerParams(vmem_limit_bytes=56 * 2**20),
        cost_estimate=pl.CostEstimate(
            flops=6 * tokens * width * share, bytes_accessed=2 * wq.size, transcendentals=tokens * 512 * share // 128
        ),
        name="attend",
    )(lengths, h1, wq, bias)


def attend_back_kernel(ns, nb, length, h1, da, wout, o, qkv, packed, dproj, gqv, h1t, do, gw, gwo, acc_k, acc_v, sems):
    tokens, width = h1.shape
    share = o.shape[1]
    rows = tokens // ns
    depth = width // (ns * nb)
    scale = HEAD_DIM ** (-0.5)
    limit = length[0]
    for r in range(0, tokens, 256):
        h1t[:, r : r + 256] = h1[r : r + 256, :].T
        do[r : r + 256, :] = dot_t(da[r : r + 256, :], wout[...]).astype(BF)
    ot = o[...].T
    for c in range(0, width, 512):
        gwo[:, c : c + 512] = jnp.dot(ot, da[:, c : c + 512], preferred_element_type=F32).astype(BF)

    def store_out(b, carry):
        for p in range(ns):
            pltpu.make_async_copy(
                gwo.at[pl.ds(b * depth, depth), p * share : (p + 1) * share],
                packed.at[b, (3 * ns + p) * depth : (3 * ns + p + 1) * depth, :],
                sems.at[0],
            ).start()
        return carry

    lax.fori_loop(0, nb, store_out, 0)

    def head(h, carry):
        at = h * HEAD_DIM
        col_q = pl.ds(pl.multiple_of(at, HEAD_DIM), HEAD_DIM)
        col_k = pl.ds(pl.multiple_of(share + at, HEAD_DIM), HEAD_DIM)
        col_v = pl.ds(pl.multiple_of(2 * share + at, HEAD_DIM), HEAD_DIM)
        acc_k[...] = jnp.zeros_like(acc_k)
        acc_v[...] = jnp.zeros_like(acc_v)
        for n in range(ns):
            first = max(n - 1, 0) * rows
            mine, seen = slice(n * rows, n * rows + rows), slice(first, first + 2 * rows)
            query, keys, grad = qkv[mine, col_q], qkv[seen, col_k], do[mine, col_q]
            probs = soft_block(query, keys, n, first, limit)
            dp = dot_t(grad, qkv[seen, col_v])
            ds = (probs * (dp - jnp.sum(dp * probs, -1, keepdims=True))).astype(BF)
            dq = jnp.dot(ds, keys, preferred_element_type=F32) * scale
            dproj[mine, col_q] = dq.astype(BF)
            acc_k[seen, :] += t_dot(ds, query)
            acc_v[seen, :] += t_dot(probs.astype(BF), grad)
        dproj[:, col_k] = (acc_k[...] * scale).astype(BF)
        dproj[:, col_v] = acc_v[...].astype(BF)
        return carry

    lax.fori_loop(0, share // HEAD_DIM, head, 0)
    wide = min(512, 3 * share)

    def weights(j, carry):
        cols = pl.ds(pl.multiple_of(j * wide, wide), wide)
        gqv[:, cols] = jnp.sum(dproj[:, cols].astype(F32), 0, keepdims=True)
        for r in range(0, width, 512):
            gw[r : r + 512, cols] = jnp.dot(
                h1t[r : r + 512, :], dproj[:, cols], preferred_element_type=F32
            ).astype(BF)
        return carry

    lax.fori_loop(0, 3 * share // wide, weights, 0)

    def store(k, c):
        s, b = k // nb, lax.rem(k, nb)
        for t in range(3):
            pltpu.make_async_copy(
                gw.at[pl.ds(k * depth, depth), t * share : (t + 1) * share],
                packed.at[b, pl.ds((t * ns + s) * depth, depth), :],
                sems.at[1],
            ).start()
        return c

    lax.fori_loop(0, ns * nb, store, 0)
    pltpu.make_async_copy(gw, gw, sems.at[1]).wait()
    pltpu.make_async_copy(gwo, gwo, sems.at[0]).wait()


def attend_back(ns, nb, lengths, h1, da, wout, o, qkv):
    tokens, width = h1.shape
    share = o.shape[1]
    vm = pl.BlockSpec(memory_space=pltpu.VMEM)
    hbm = pl.BlockSpec(memory_space=pl.ANY)
    return pl.pallas_call(
        functools.partial(attend_back_kernel, ns, nb),
        out_shape=(
            jax.ShapeDtypeStruct((nb, 4 * width // nb, share), BF),
            jax.ShapeDtypeStruct((tokens, 3 * share), BF),
            jax.ShapeDtypeStruct((1, 3 * share), F32),
        ),
        in_specs=[pl.BlockSpec(memory_space=pltpu.SMEM), vm, vm, vm, vm, vm],
        out_specs=(hbm, vm, vm),
        scratch_shapes=[
            pltpu.VMEM((width, tokens), BF),
            pltpu.VMEM((tokens, share), BF),
            pltpu.VMEM((width, 3 * share), BF),
            pltpu.VMEM((share, width), BF),
            pltpu.VMEM((tokens, HEAD_DIM), F32),
            pltpu.VMEM((tokens, HEAD_DIM), F32),
            pltpu.SemaphoreType.DMA((2,)),
        ],
        compiler_params=pltpu.CompilerParams(vmem_limit_bytes=56 * 2**20),
        cost_estimate=pl.CostEstimate(
            flops=12 * tokens * width * share, bytes_accessed=12 * width * share, transcendentals=tokens * 512 * share // 128
        ),
        name="attend_back",
    )(lengths, h1, da, wout, o, qkv)


def ff_kernel(ns, nb, h2, cot, wg, bias, gwg, g_out, du_out, gb, w1, w2, h2t, gw1, gw2, sems):
    tokens, width = h2.shape
    chunk = g_out.shape[1]
    depth = width // (ns * nb)
    part = chunk // nb
    pieces = width // chunk
    half = ns * depth
    tile = min(512, chunk)
    tiles = chunk // tile
    step = min(256, tokens)

    def load1(k, carry):
        s, b = k // nb, lax.rem(k, nb)
        pltpu.make_async_copy(
            wg.at[b, pl.ds(s * depth, depth), :], w1.at[pl.ds(k * depth, depth), :], sems.at[0]
        ).start()
        return carry

    def load2(k, carry):
        for p in range(pieces):
            pltpu.make_async_copy(
                wg.at[k, pl.ds(half + p * part, part), :],
                w2.at[pl.ds(k * part, part), p * chunk : (p + 1) * chunk],
                sems.at[1],
            ).start()
        return carry

    lax.fori_loop(0, ns * nb, load1, 0)
    lax.fori_loop(0, nb, load2, 0)
    for r in range(0, tokens, step):
        h2t[:, r : r + step] = h2[r : r + step, :].T
    pltpu.make_async_copy(w1, w1, sems.at[0]).wait()
    pltpu.make_async_copy(w2, w2, sems.at[1]).wait()

    def one_tile(j, carry):
        at = pl.multiple_of(j * tile, tile)
        cols = pl.ds(at, tile)
        total = jnp.zeros((1, tile), F32)
        for r in range(0, tokens, step):
            rows = slice(r, r + step)
            u = jnp.dot(h2[rows, :], w1[:, cols], preferred_element_type=F32) + bias[:, cols]
            dg = lax.dot_general(
                cot[rows, :], w2[cols, :], (((1,), (1,)), ((), ())), preferred_element_type=F32
            )
            sq = u * u
            th = jnp.tanh(ROOT * u * (1.0 + 0.044715 * sq))
            cdf = 0.5 * (1.0 + th)
            g_out[rows, cols] = (u * cdf).astype(BF)
            slope = cdf + 0.5 * u * (1.0 - th * th) * (ROOT * (1.0 + 3.0 * 0.044715 * sq))
            du = (dg * slope).astype(BF)
            du_out[rows, cols] = du
            total += jnp.sum(du.astype(F32), 0, keepdims=True)
        gb[:, cols] = total
        for r in range(0, width, 512):
            gw1[j, r : r + 512, :] = jnp.dot(
                h2t[r : r + 512, :], du_out[:, cols], preferred_element_type=F32
            ).astype(BF)
        gt = g_out[:, cols].T
        for r in range(0, width, 512):
            gw2[j, :, r : r + 512] = jnp.dot(
                gt, cot[:, r : r + 512], preferred_element_type=F32
            ).astype(BF)

        def store1(k, c):
            s, b = k // nb, lax.rem(k, nb)
            pltpu.make_async_copy(
                gw1.at[j, pl.ds(k * depth, depth), :],
                gwg.at[b, pl.ds(s * depth, depth), cols],
                sems.at[2],
            ).start()
            return c

        lax.fori_loop(0, ns * nb, store1, 0)
        count = tile // part

        def store2(k, c):
            for p in range(pieces):
                pltpu.make_async_copy(
                    gw2.at[j, pl.ds(k * part, part), p * chunk : (p + 1) * chunk],
                    gwg.at[j * count + k, pl.ds(half + p * part, part), :],
                    sems.at[3],
                ).start()
            return c

        lax.fori_loop(0, count, store2, 0)
        return carry

    lax.fori_loop(0, tiles, one_tile, 0)
    pltpu.make_async_copy(gw1, gw1, sems.at[2]).wait()
    pltpu.make_async_copy(gw2, gw2, sems.at[3]).wait()


def ff_chunk(ns, nb, h2, cot, wg, bias):
    tokens, width = h2.shape
    chunk = wg.shape[2]
    tile = min(512, chunk)
    vm = pl.BlockSpec(memory_space=pltpu.VMEM)
    hbm = pl.BlockSpec(memory_space=pl.ANY)
    return pl.pallas_call(
        functools.partial(ff_kernel, ns, nb),
        out_shape=(
            jax.ShapeDtypeStruct(wg.shape, BF),
            jax.ShapeDtypeStruct((tokens, chunk), BF),
            jax.ShapeDtypeStruct((tokens, chunk), BF),
            jax.ShapeDtypeStruct((1, chunk), F32),
        ),
        in_specs=[vm, vm, hbm, vm],
        out_specs=(hbm, vm, vm, vm),
        scratch_shapes=[
            pltpu.VMEM((width, chunk), BF),
            pltpu.VMEM((chunk, width), BF),
            pltpu.VMEM((width, tokens), BF),
            pltpu.VMEM((chunk // tile, width, tile), BF),
            pltpu.VMEM((chunk // tile, tile, width), BF),
            pltpu.SemaphoreType.DMA((4,)),
        ],
        compiler_params=pltpu.CompilerParams(vmem_limit_bytes=56 * 2**20),
        cost_estimate=pl.CostEstimate(
            flops=8 * tokens * width * chunk, bytes_accessed=4 * wg.size, transcendentals=tokens * chunk
        ),
        name="ff_chunk",
    )(h2, cot, wg, bias)


MESH = pl.DeviceIdType.MESH


def greet():
    me, batch = lax.axis_index("seq"), lax.axis_index("batch")
    by_x = me + 1 - 2 * lax.rem(me, 2)
    by_y = lax.rem(me + 2, 4)
    barrier = pltpu.get_barrier_semaphore()
    for other in (by_x, by_y):
        pl.semaphore_signal(barrier, inc=1, device_id=(other, batch), device_id_type=MESH)
    pl.semaphore_wait(barrier, 2)
    return me, by_x, by_y, (by_x, batch), (by_y, batch)


def scatter_sum(partial, place, buffers, send, recv):
    me, by_x, by_y, to_x, to_y = place
    out, via, from_x, from_y = buffers
    half = via.shape[1]
    top, low = slice(0, half), slice(half, 2 * half)
    far = 3 - me

    def copy(k, src, dst, to):
        one = pltpu.make_async_remote_copy(
            src_ref=src, dst_ref=dst, send_sem=send.at[k], recv_sem=recv.at[k], device_id=to, device_id_type=MESH
        )
        one.start()
        return one

    out[0, top] = partial(far, 0).astype(BF)
    c0 = copy(0, out.at[0, top], via.at[0], to_y)
    out[0, low] = partial(far, 1).astype(BF)
    c1 = copy(1, out.at[0, low], via.at[1], to_x)
    out[1, low] = partial(by_x, 1).astype(BF)
    c2 = copy(2, out.at[1, low], from_x.at[low], to_x)
    out[2, top] = partial(by_y, 0).astype(BF)
    c3 = copy(3, out.at[2, top], from_y.at[top], to_y)
    x_top = partial(by_x, 0)
    c0.wait_recv()
    out[1, top] = (x_top + via[0].astype(F32)).astype(BF)
    c4 = copy(4, out.at[1, top], from_x.at[top], to_x)
    y_low = partial(by_y, 1)
    c1.wait_recv()
    out[2, low] = (y_low + via[1].astype(F32)).astype(BF)
    c5 = copy(5, out.at[2, low], from_y.at[low], to_y)
    mine_top, mine_low = partial(me, 0), partial(me, 1)
    c3.wait_recv()
    c4.wait_recv()
    mine_top = mine_top + from_x[top].astype(F32) + from_y[top].astype(F32)
    c2.wait_recv()
    c5.wait_recv()
    mine_low = mine_low + from_x[low].astype(F32) + from_y[low].astype(F32)
    for one in (c0, c1, c2, c3, c4, c5):
        one.wait_send()
    return mine_top, mine_low


def scatter_scratch(rows, width):
    return [
        pltpu.VMEM((3, rows, width), BF),
        pltpu.VMEM((2, rows // 2, width), BF),
        pltpu.VMEM((rows, width), BF),
        pltpu.VMEM((rows, width), BF),
        pltpu.SemaphoreType.DMA((6,)),
        pltpu.SemaphoreType.DMA((6,)),
    ]


def gather_blocks(full, rows, place, send, recv):
    me, by_x, by_y, to_x, to_y = place
    half = rows // 2

    def copy(k, block, part, to):
        at = full.at[pl.ds(pl.multiple_of(block * rows + part * half, half), half)]
        one = pltpu.make_async_remote_copy(
            src_ref=at, dst_ref=at, send_sem=send.at[k], recv_sem=recv.at[k], device_id=to, device_id_type=MESH
        )
        one.start()
        return one

    c0 = copy(0, me, 0, to_x)
    c3 = copy(3, me, 1, to_y)
    c2 = copy(2, me, 0, to_y)
    c1 = copy(1, me, 1, to_x)
    c0.wait_recv()
    c4 = copy(4, by_x, 0, to_y)
    c3.wait_recv()
    c5 = copy(5, by_y, 1, to_x)
    for one in (c1, c2, c4, c5):
        one.wait_recv()
    for one in (c0, c1, c2, c3, c4, c5):
        one.wait_send()


GATHER_SEMS = [pltpu.SemaphoreType.DMA((6,)), pltpu.SemaphoreType.DMA((6,))]


def middle_kernel(o, wout, mine, obias, gain, shift, x1, h2, out, via, from_x, from_y, s1, r1, s2, r2):
    rows, width = mine.shape
    half = rows // 2
    place = greet()

    def partial(block, part):
        at = pl.multiple_of(block * rows + part * half, half)
        return jnp.dot(o[pl.ds(at, half), :], wout[...], preferred_element_type=F32)

    sums = scatter_sum(partial, place, (out, via, from_x, from_y), s1, r1)
    for part, total in enumerate(sums):
        span = slice(part * half, part * half + half)
        res = mine[span, :].astype(F32) + (total + obias[...])
        x1[span, :] = res
        normed, _ = norm_stats(res)
        at = pl.multiple_of(place[0] * rows + part * half, half)
        h2[pl.ds(at, half), :] = (normed * gain[...] + shift[...]).astype(BF)
    gather_blocks(h2, rows, place, s2, r2)


def middle(o, wout, mine, obias, gain, shift):
    tokens, share = o.shape
    rows, width = mine.shape
    vm = pl.BlockSpec(memory_space=pltpu.VMEM)
    return pl.pallas_call(
        middle_kernel,
        out_shape=(jax.ShapeDtypeStruct((rows, width), F32), jax.ShapeDtypeStruct((tokens, width), BF)),
        in_specs=[vm] * 6,
        out_specs=(vm, vm),
        scratch_shapes=scatter_scratch(rows, width) + GATHER_SEMS,
        compiler_params=pltpu.CompilerParams(collective_id=1, has_side_effects=True, vmem_limit_bytes=56 * 2**20),
        cost_estimate=pl.CostEstimate(flops=40 * 10**9, bytes_accessed=12 * tokens * width, transcendentals=0),
        name="project_out",
    )(o, wout, mine, obias, gain, shift)


def ff_back_kernel(ns, nb, count, *refs):
    dus, wgs = refs[:count], refs[count : 2 * count]
    x1, cot, gain, dx1, da, ggain, gshift, gob = refs[2 * count : 2 * count + 8]
    ws = refs[2 * count + 8 : 3 * count + 8]
    load_sem, out, via, from_x, from_y, s1, r1, s2, r2 = refs[3 * count + 8 :]
    rows, width = x1.shape
    half = rows // 2
    for c in range(count):
        load_rows(ns, nb, width // (ns * nb), wgs[c], ws[c], load_sem.at[c])
    place = greet()
    for c in range(count):
        pltpu.make_async_copy(ws[c], ws[c], load_sem.at[c]).wait()

    def partial(block, part):
        at = pl.multiple_of(block * rows + part * half, half)
        total = dot_t(dus[0][pl.ds(at, half), :], ws[0][...])
        for c in range(1, count):
            total += dot_t(dus[c][pl.ds(at, half), :], ws[c][...])
        return total

    sums = scatter_sum(partial, place, (out, via, from_x, from_y), s1, r1)
    totals = [jnp.zeros((1, width), F32)] * 3
    for part, grad in enumerate(sums):
        span = slice(part * half, part * half + half)
        normed, rstd = norm_stats(x1[span, :])
        res = cot[span, :].astype(F32) + norm_back(grad, normed, rstd, gain[...])
        dx1[span, :] = res
        low = res.astype(BF)
        at = pl.multiple_of(place[0] * rows + part * half, half)
        da[pl.ds(at, half), :] = low
        for k, term in enumerate((grad * normed, grad, low.astype(F32))):
            totals[k] += jnp.sum(term, 0, keepdims=True)
    ggain[...], gshift[...], gob[...] = totals
    gather_blocks(da, rows, place, s2, r2)


def ff_back(ns, nb, dus, wgs, x1, cot, gain):
    rows, width = x1.shape
    tokens, chunk = dus[0].shape
    count = len(dus)
    vm = pl.BlockSpec(memory_space=pltpu.VMEM)
    hbm = pl.BlockSpec(memory_space=pl.ANY)
    row = jax.ShapeDtypeStruct((1, width), F32)
    return pl.pallas_call(
        functools.partial(ff_back_kernel, ns, nb, count),
        out_shape=(
            jax.ShapeDtypeStruct((rows, width), F32),
            jax.ShapeDtypeStruct((tokens, width), BF),
            row,
            row,
            row,
        ),
        in_specs=[vm] * count + [hbm] * count + [vm] * 3,
        out_specs=(vm,) * 5,
        scratch_shapes=[pltpu.VMEM((width, chunk), BF)] * count
        + [pltpu.SemaphoreType.DMA((count,))]
        + scatter_scratch(rows, width)
        + GATHER_SEMS,
        compiler_params=pltpu.CompilerParams(collective_id=2, has_side_effects=True, vmem_limit_bytes=56 * 2**20),
        cost_estimate=pl.CostEstimate(flops=40 * 10**9, bytes_accessed=12 * tokens * width, transcendentals=0),
        name="ff_back",
    )(*dus, *wgs, x1, cot, gain)


def finish_kernel(ns, nb, dproj, wq, mine, dx1, gain, gx, ggain, gshift, w, load_sem, out, via, from_x, from_y, s1, r1):
    rows, width = mine.shape
    half = rows // 2
    load_rows(ns, nb, width // (ns * nb), wq, w, load_sem)
    place = greet()
    pltpu.make_async_copy(w, w, load_sem).wait()

    def partial(block, part):
        at = pl.multiple_of(block * rows + part * half, half)
        return dot_t(dproj[pl.ds(at, half), :], w[...])

    sums = scatter_sum(partial, place, (out, via, from_x, from_y), s1, r1)
    totals = [jnp.zeros((1, width), F32)] * 2
    for part, grad in enumerate(sums):
        span = slice(part * half, part * half + half)
        normed, rstd = norm_stats(mine[span, :].astype(F32))
        gx[span, :] = dx1[span, :] + norm_back(grad, normed, rstd, gain[...])
        for k, term in enumerate((grad * normed, grad)):
            totals[k] += jnp.sum(term, 0, keepdims=True)
    ggain[...], gshift[...] = totals


def finish(ns, nb, dproj, wq, mine, dx1, gain):
    rows, width = mine.shape
    vm = pl.BlockSpec(memory_space=pltpu.VMEM)
    row = jax.ShapeDtypeStruct((1, width), F32)
    return pl.pallas_call(
        functools.partial(finish_kernel, ns, nb),
        out_shape=(jax.ShapeDtypeStruct((rows, width), F32), row, row),
        in_specs=[vm, pl.BlockSpec(memory_space=pl.ANY), vm, vm, vm],
        out_specs=(vm,) * 3,
        scratch_shapes=[pltpu.VMEM((width, wq.shape[2]), BF), pltpu.SemaphoreType.DMA] + scatter_scratch(rows, width),
        compiler_params=pltpu.CompilerParams(collective_id=3, has_side_effects=True, vmem_limit_bytes=56 * 2**20),
        cost_estimate=pl.CostEstimate(flops=20 * 10**9, bytes_accessed=12 * rows * width, transcendentals=0),
        name="attend_input",
    )(dproj, wq, mine, dx1, gain)


def ff_out_kernel(nb, count, *refs):
    gs, wgs = refs[:count], refs[count : 2 * count]
    x1, bias, result = refs[2 * count : 2 * count + 3]
    ws = refs[2 * count + 3 : 3 * count + 3]
    load_sem, out, via, from_x, from_y, s1, r1 = refs[3 * count + 3 :]
    rows, width = x1.shape
    half = rows // 2
    chunk = gs[0].shape[1]
    part_rows, pieces, base = chunk // nb, width // chunk, width // nb
    for c in range(count):

        def load(k, carry):
            for p in range(pieces):
                pltpu.make_async_copy(
                    wgs[c].at[k, pl.ds(base + p * part_rows, part_rows), :],
                    ws[c].at[pl.ds(k * part_rows, part_rows), p * chunk : (p + 1) * chunk],
                    load_sem.at[c],
                ).start()
            return carry

        lax.fori_loop(0, nb, load, 0)
    place = greet()
    for c in range(count):
        pltpu.make_async_copy(ws[c], ws[c], load_sem.at[c]).wait()

    def partial(block, part):
        at = pl.multiple_of(block * rows + part * half, half)
        total = jnp.dot(gs[0][pl.ds(at, half), :], ws[0][...], preferred_element_type=F32)
        for c in range(1, count):
            total += jnp.dot(gs[c][pl.ds(at, half), :], ws[c][...], preferred_element_type=F32)
        return total

    sums = scatter_sum(partial, place, (out, via, from_x, from_y), s1, r1)
    for part, total in enumerate(sums):
        span = slice(part * half, part * half + half)
        result[span, :] = (x1[span, :] + (total + bias[...])).astype(BF)


def ff_out(nb, gs, wgs, x1, bias):
    rows, width = x1.shape
    chunk = gs[0].shape[1]
    count = len(gs)
    vm = pl.BlockSpec(memory_space=pltpu.VMEM)
    hbm = pl.BlockSpec(memory_space=pl.ANY)
    return pl.pallas_call(
        functools.partial(ff_out_kernel, nb, count),
        out_shape=jax.ShapeDtypeStruct((rows, width), BF),
        in_specs=[vm] * count + [hbm] * count + [vm] * 2,
        out_specs=vm,
        scratch_shapes=[pltpu.VMEM((chunk, width), BF)] * count
        + [pltpu.SemaphoreType.DMA((count,))]
        + scatter_scratch(rows, width),
        compiler_params=pltpu.CompilerParams(collective_id=4, has_side_effects=True, vmem_limit_bytes=56 * 2**20),
        cost_estimate=pl.CostEstimate(flops=20 * 10**9, bytes_accessed=12 * rows * width, transcendentals=0),
        name="ff_out",
    )(*gs, *wgs, x1, bias)


def greet_all(ns, nb):
    me, batch = lax.axis_index("seq"), lax.axis_index("batch")
    along_seq = [(lax.rem(me + d, ns), batch) for d in range(1, ns)]
    along_batch = [(me, lax.rem(batch + d, nb)) for d in range(1, nb)]
    barrier = pltpu.get_barrier_semaphore()
    for other in along_seq + along_batch:
        pl.semaphore_signal(barrier, inc=1, device_id=other, device_id_type=MESH)
    pl.semaphore_wait(barrier, ns + nb - 2)
    return me, batch, along_seq, along_batch


def send(src, dst, sends, recvs, to):
    one = pltpu.make_async_remote_copy(
        src_ref=src, dst_ref=dst, send_sem=sends, recv_sem=recvs, device_id=to, device_id_type=MESH
    )
    one.start()
    return one


def spread_kernel(ns, nb, w_qkv, vec, packed, vecs, local, s0, r0, s1, r1, s2, r2):
    depth = w_qkv.shape[0]
    share = packed.shape[1] // 3
    width = ns * share
    me, batch, along_seq, along_batch = greet_all(ns, nb)
    own = pltpu.make_async_copy(vec, vecs.at[batch, me], local.at[3])
    own.start()
    small = [send(vec, vecs.at[batch, me], s1.at[d], r1.at[d], to) for d, to in enumerate(along_seq)]
    rows = pl.ds(pl.multiple_of(me * depth, depth), depth)
    copies = []
    for t in range(3):
        keep = pl.ds(pl.multiple_of(t * width + me * share, share), share)
        here = packed.at[rows, t * share : (t + 1) * share]
        one = pltpu.make_async_copy(w_qkv.at[:, keep], here, local.at[t])
        one.start()
        copies.append(one)
        for d, to in enumerate(along_seq):
            cols = pl.ds(pl.multiple_of(t * width + to[0] * share, share), share)
            copies.append(send(w_qkv.at[:, cols], here, s0.at[t, d], r0.at[t, d], to))
    for one in small:
        one.wait_recv()
    own.wait()
    far = [send(vecs.at[batch], vecs.at[batch], s2.at[d], r2.at[d], to) for d, to in enumerate(along_batch)]
    for one in small:
        one.wait_send()
    for one in copies + far:
        one.wait()


def spread(ns, nb, w_qkv, vec):
    depth, width = w_qkv.shape
    hbm = pl.BlockSpec(memory_space=pl.ANY)
    dma = pltpu.SemaphoreType.DMA
    return pl.pallas_call(
        functools.partial(spread_kernel, ns, nb),
        out_shape=(
            jax.ShapeDtypeStruct((ns * depth, width // ns), BF),
            jax.ShapeDtypeStruct((nb, ns) + vec.shape, F32),
        ),
        in_specs=[hbm, hbm],
        out_specs=(hbm, hbm),
        scratch_shapes=[
            dma((4,)),
            dma((3, ns - 1)),
            dma((3, ns - 1)),
            dma((ns - 1,)),
            dma((ns - 1,)),
            dma((nb - 1,)),
            dma((nb - 1,)),
        ],
        compiler_params=pltpu.CompilerParams(collective_id=5, has_side_effects=True),
        cost_estimate=pl.CostEstimate(flops=5 * 10**9, bytes_accessed=2 * w_qkv.size, transcendentals=0),
        name="spread_qkv",
    )(w_qkv, vec)


def collect_kernel(ns, nb, parts, w1, w2, mine, cot, gain, shift, *refs):
    packs = refs[:parts]
    h1, cots, acts, local, s0, r0, s1, r1, s2, r2 = refs[parts:]
    depth = w1.shape[0]
    rows, width = mine.shape
    half = rows // 2
    hidden = w1.shape[1] // ns
    part = hidden // (parts * nb)
    chunk = hidden // parts
    pieces = width // chunk
    me, batch = lax.axis_index("seq"), lax.axis_index("batch")
    by_x = me + 1 - 2 * lax.rem(me, 2)
    by_y = lax.rem(me + 2, 4)
    others = [(lax.rem(me + d, ns), batch) for d in range(1, ns)]
    barrier = pltpu.get_barrier_semaphore()
    for other in others:
        pl.semaphore_signal(barrier, inc=1, device_id=other, device_id_type=MESH)
    at_me = pl.ds(pl.multiple_of(me * rows, rows), rows)
    acts[at_me, :] = mine[...]
    own = pltpu.make_async_copy(cot, cots.at[at_me], local.at[parts])
    own.start()
    for c in range(parts):
        for p in range(pieces):
            pltpu.make_async_copy(
                w2.at[c * part : (c + 1) * part, p * chunk : (p + 1) * chunk],
                packs[c].at[ns * depth + p * part : ns * depth + (p + 1) * part, :],
                local.at[c],
            ).start()
    at = pl.ds(pl.multiple_of(me * depth, depth), depth)

    def keep(b, carry):
        for c in range(parts):
            cols = pl.ds(pl.multiple_of(me * hidden + (b * parts + c) * part, part), part)
            here = packs[c].at[at, pl.ds(pl.multiple_of(b * part, part), part)]
            pltpu.make_async_copy(w1.at[:, cols], here, local.at[c]).start()
        return carry

    lax.fori_loop(0, nb, keep, 0)
    pl.semaphore_wait(barrier, ns - 1)
    to_x, to_y = (by_x, batch), (by_y, batch)

    def ship(b, carry):
        for c in range(parts):
            here = packs[c].at[at, pl.ds(pl.multiple_of(b * part, part), part)]
            for d, to in enumerate(others):
                cols = pl.ds(pl.multiple_of(to[0] * hidden + (b * parts + c) * part, part), part)
                send(w1.at[:, cols], here, s0.at[c, d], r0.at[c, d], to)
        return carry

    lax.fori_loop(0, nb, ship, 0)

    def normalise(block):
        span = pl.ds(pl.multiple_of(block * rows, rows), rows)
        normed, _ = norm_stats(acts[span, :].astype(F32))
        h1[span, :] = (normed * gain[...] + shift[...]).astype(BF)

    def copy(k, full, block, side, to, sends, recvs):
        span = full.at[pl.ds(pl.multiple_of(block * rows + side * half, half), half)]
        return send(span, span, sends.at[k], recvs.at[k], to)

    c0 = copy(0, acts, me, 0, to_x, s1, r1)
    c3 = copy(3, acts, me, 1, to_y, s1, r1)
    c2 = copy(2, acts, me, 0, to_y, s1, r1)
    c1 = copy(1, acts, me, 1, to_x, s1, r1)
    normalise(me)
    c0.wait_recv()
    c4 = copy(4, acts, by_x, 0, to_y, s1, r1)
    c3.wait_recv()
    c5 = copy(5, acts, by_y, 1, to_x, s1, r1)
    own.wait()
    d0 = copy(0, cots, me, 0, to_x, s2, r2)
    d3 = copy(3, cots, me, 1, to_y, s2, r2)
    d2 = copy(2, cots, me, 0, to_y, s2, r2)
    d1 = copy(1, cots, me, 1, to_x, s2, r2)
    c1.wait_recv()
    normalise(by_x)
    c2.wait_recv()
    normalise(by_y)
    c4.wait_recv()
    c5.wait_recv()
    normalise(3 - me)
    d0.wait_recv()
    d4 = copy(4, cots, by_x, 0, to_y, s2, r2)
    d3.wait_recv()
    d5 = copy(5, cots, by_y, 1, to_x, s2, r2)
    for one in (d1, d2, d4, d5):
        one.wait_recv()
    for one in (c0, c1, c2, c3, c4, c5, d0, d1, d2, d3, d4, d5):
        one.wait_send()
    for c in range(parts):
        pack = packs[c].at[: depth]
        for d, to in enumerate(others):
            rest = pltpu.make_async_remote_copy(
                src_ref=pack, dst_ref=pack, send_sem=s0.at[c, d], recv_sem=r0.at[c, d], device_id=to, device_id_type=MESH
            )
            rest.wait()
        whole = packs[c].at[: depth + pieces * part]
        pltpu.make_async_copy(whole, whole, local.at[c]).wait()


def collect(ns, nb, parts, w1, w2, mine, cot, gain, shift):
    depth = w1.shape[0]
    rows, width = mine.shape
    chunk = w1.shape[1] // (ns * parts)
    vm = pl.BlockSpec(memory_space=pltpu.VMEM)
    hbm = pl.BlockSpec(memory_space=pl.ANY)
    dma = pltpu.SemaphoreType.DMA
    pack = jax.ShapeDtypeStruct((2 * ns * depth, chunk), BF)
    full = jax.ShapeDtypeStruct((ns * rows, width), BF)
    return pl.pallas_call(
        functools.partial(collect_kernel, ns, nb, parts),
        out_shape=(pack,) * parts + (full, full),
        in_specs=[hbm, hbm, vm, hbm, vm, vm],
        out_specs=(hbm,) * parts + (vm, hbm),
        scratch_shapes=[
            pltpu.VMEM((ns * rows, width), BF),
            dma((parts + 1,)),
            dma((parts, ns - 1)),
            dma((parts, ns - 1)),
            dma((6,)),
            dma((6,)),
            dma((6,)),
            dma((6,)),
        ],
        compiler_params=pltpu.CompilerParams(collective_id=6, has_side_effects=True, vmem_limit_bytes=40 * 2**20),
        cost_estimate=pl.CostEstimate(flops=40 * 10**9, bytes_accessed=12 * rows * width, transcendentals=0),
        name="collect",
    )(w1, w2, mine, cot, gain, shift)


def small_kernel(ns, nb, sums, result, near, mid, far, s1, r1, s2, r2):
    me, batch, along_seq, along_batch = greet_all(ns, nb)
    copies = [send(sums.at[to[1]], near.at[d], s1.at[d], r1.at[d], to) for d, to in enumerate(along_batch)]
    total = sums[batch]
    for d, one in enumerate(copies):
        one.wait_recv()
        total += near[d]
    mid[...] = total
    more = [send(mid.at[to[0]], far.at[d], s2.at[d], r2.at[d], to) for d, to in enumerate(along_seq)]
    total = mid[me]
    for d, one in enumerate(more):
        one.wait_recv()
        total += far[d]
    result[...] = total
    for one in copies + more:
        one.wait_send()


def small_sums(ns, nb, sums):
    tail = sums.shape[2:]
    vm = pl.BlockSpec(memory_space=pltpu.VMEM)
    dma = pltpu.SemaphoreType.DMA
    return pl.pallas_call(
        functools.partial(small_kernel, ns, nb),
        out_shape=jax.ShapeDtypeStruct(tail, F32),
        in_specs=[vm],
        out_specs=vm,
        scratch_shapes=[
            pltpu.VMEM((nb - 1, ns) + tail, F32),
            pltpu.VMEM((ns,) + tail, F32),
            pltpu.VMEM((ns - 1,) + tail, F32),
            dma((nb - 1,)),
            dma((nb - 1,)),
            dma((ns - 1,)),
            dma((ns - 1,)),
        ],
        compiler_params=pltpu.CompilerParams(collective_id=7, has_side_effects=True),
        cost_estimate=pl.CostEstimate(flops=5 * 10**9, bytes_accessed=4 * sums.size, transcendentals=0),
        name="small_sums",
    )(sums)


def home_kernel(ns, summed, gqkv, gout, stage, local, s0, r0):
    depth, width = gout.shape
    share = width // ns
    me, batch = lax.axis_index("seq"), lax.axis_index("batch")
    others = [(lax.rem(me + d, ns), batch) for d in range(1, ns)]
    barrier = pltpu.get_barrier_semaphore()
    for other in others:
        pl.semaphore_signal(barrier, inc=1, device_id=other, device_id_type=MESH)
    pl.semaphore_wait(barrier, ns - 1)
    copies = []
    for t in range(3):
        cols = pl.ds(pl.multiple_of(t * width + me * share, share), share)
        for d, to in enumerate(others):
            rows = pl.ds(pl.multiple_of((t * ns + to[0]) * depth, depth), depth)
            copies.append(send(summed.at[rows], stage.at[:, cols], s0.at[t, d], r0.at[t, d], to))
        rows = pl.ds(pl.multiple_of((t * ns + me) * depth, depth), depth)
        own = pltpu.make_async_copy(summed.at[rows], stage.at[:, cols], local.at[t])
        own.start()
        copies.append(own)
    for p in range(ns):
        rows = slice((3 * ns + p) * depth, (3 * ns + p + 1) * depth)
        gout[:, p * share : (p + 1) * share] = summed[rows, :].astype(F32)
    for one in copies:
        one.wait()
    gqkv[...] = stage[...].astype(F32)


def home(ns, summed):
    rows, share = summed.shape
    depth, width = rows // (4 * ns), ns * share
    vm = pl.BlockSpec(memory_space=pltpu.VMEM)
    dma = pltpu.SemaphoreType.DMA
    return pl.pallas_call(
        functools.partial(home_kernel, ns),
        out_shape=(jax.ShapeDtypeStruct((depth, 3 * width), F32), jax.ShapeDtypeStruct((depth, width), F32)),
        in_specs=[vm],
        out_specs=(vm, vm),
        scratch_shapes=[pltpu.VMEM((depth, 3 * width), BF), dma((3,)), dma((3, ns - 1)), dma((3, ns - 1))],
        compiler_params=pltpu.CompilerParams(collective_id=8, has_side_effects=True),
        cost_estimate=pl.CostEstimate(flops=5 * 10**9, bytes_accessed=4 * summed.size, transcendentals=0),
        name="home",
    )(summed)


PARTS = 2


def gather_seq(value):
    return lax.all_gather(value, "seq", axis=0, tiled=True)


def scatter_seq(partial):
    return lax.psum_scatter(partial, "seq", scatter_dimension=0, tiled=True)


def scatter_batch(parts):
    flat = parts.reshape(-1, parts.shape[-1])
    return lax.psum_scatter(flat, "batch", scatter_dimension=0, tiled=True)


def unpermute(ns, nb, gathered):
    depth = gathered.shape[1] // ns
    return gathered.reshape(nb, ns, depth, -1).transpose(1, 0, 2, 3).reshape(ns * nb * depth, -1)


def body(
    block_input,
    lengths,
    ln1_gain,
    ln1_bias,
    w_qkv,
    qv_bias,
    w_out,
    out_bias,
    ln2_gain,
    ln2_bias,
    w_fc1,
    fc1_bias,
    w_fc2,
    fc2_bias,
    out_cotangent,
):
    ns, nb = lax.axis_size("seq"), lax.axis_size("batch")
    seq = lax.axis_index("seq")
    rows, width = block_input.shape[1:]
    share = width // ns
    depth = width // (ns * nb)
    hidden = w_fc1.shape[1] // ns
    chunk = hidden // PARTS
    part = chunk // nb
    pieces = width // chunk
    planar = ns == 4 and part % 128 == 0
    mine, cot_mine = block_input[0], out_cotangent[0]

    vectors = (ln1_gain, ln1_bias, qv_bias, out_bias, ln2_gain, ln2_bias, fc1_bias, fc2_bias)
    vector = jnp.concatenate(vectors).astype(F32)
    wout = lax.all_gather(w_out, "batch", axis=0, tiled=True)
    if planar:
        padded = jnp.pad(vector, (0, 1024 - vector.shape[0])).reshape(8, 128)
        qkv_part, packed = spread(ns, nb, w_qkv, padded)
        packed = packed.transpose(1, 0, 2, 3).reshape(ns * nb, 1024)
    else:
        qkv_part = lax.all_to_all(w_qkv.reshape(depth, 3, ns, share), "seq", 2, 0).reshape(ns * depth, 3 * share)
        packed = lax.all_gather(vector, ("seq", "batch"), axis=0, tiled=False)
    wq = lax.all_gather(qkv_part, "batch", axis=0, tiled=True).reshape(nb, ns * depth, 3 * share)
    full, at = [], 0
    for vec in vectors:
        full.append(packed[:, at : at + vec.shape[0]].reshape(1, -1))
        at += vec.shape[0]
    gain1, shift1, qv, obias, gain2, shift2, bias1, bias2 = full
    bias1 = lax.dynamic_slice_in_dim(bias1, seq * hidden, hidden, 1).reshape(nb, PARTS, part)
    qbias = lax.dynamic_slice_in_dim(qv, seq * share, share, 1)
    vbias = lax.dynamic_slice_in_dim(qv, width + seq * share, share, 1)
    bias3 = jnp.concatenate([qbias, jnp.zeros_like(qbias), vbias], 1)

    if planar:
        *packs, h1, cot = collect(ns, nb, PARTS, w_fc1, w_fc2, mine, cot_mine, gain1, shift1)
    else:
        fc1_part = lax.all_to_all(w_fc1.reshape(depth, ns, hidden), "seq", 1, 0)
        fc1_part = fc1_part.reshape(ns * depth, nb, PARTS, part)
        fc2_part = w_fc2.reshape(PARTS, part, pieces, chunk)
        packs = []
        for c in range(PARTS):
            first = fc1_part[:, :, c].reshape(ns * depth, chunk)
            second = fc2_part[c].transpose(1, 0, 2).reshape(pieces * part, chunk)
            packs.append(jnp.concatenate([first, second], 0))
        h1 = (norm_stats(gather_seq(mine).astype(F32))[0] * gain1 + shift1).astype(BF)
        cot = gather_seq(cot_mine)
    wgs = [lax.all_gather(pack, "batch", axis=0, tiled=True).reshape(nb, -1, chunk) for pack in packs]

    qkv, o = attend(ns, nb, lengths, h1, wq, bias3)
    if planar:
        x1, h2 = middle(o, wout, mine, obias, gain2, shift2)
    else:
        a = scatter_seq(jnp.dot(o, wout, preferred_element_type=F32))
        x1 = mine.astype(F32) + (a + obias)
        h2 = gather_seq((norm_stats(x1)[0] * gain2 + shift2).astype(BF))

    gws, gs, dus, gb1 = [], [], [], []
    for c in range(PARTS):
        gw, g, du, gb = ff_chunk(ns, nb, h2, cot, wgs[c], bias1[:, c].reshape(1, chunk))
        gws.append(scatter_batch(gw))
        gs.append(g)
        dus.append(du)
        gb1.append(gb.reshape(nb, 1, part))
    cot_f = cot_mine.astype(F32)
    if planar:
        dx1, da, ggain2, gshift2, gob = ff_back(ns, nb, dus, wgs, x1, cot_mine, gain2)
    else:
        dh2 = sum(dot_t(du, unpermute(ns, nb, wg[:, : ns * depth])) for du, wg in zip(dus, wgs))
        dh2 = scatter_seq(dh2)
        normed2, rstd2 = norm_stats(x1)
        ggain2 = jnp.sum(dh2 * normed2, 0)
        gshift2 = jnp.sum(dh2, 0)
        dx1 = cot_f + norm_back(dh2, normed2, rstd2, gain2)
        da_mine = dx1.astype(BF)
        gob = jnp.sum(da_mine.astype(F32), 0)
        da = gather_seq(da_mine)

    if planar:
        da, gws[0] = lax.optimization_barrier((da, gws[0]))
    gattn, dproj, gqv = attend_back(ns, nb, lengths, h1, da, wout, o, qkv)
    gattn = scatter_batch(gattn)
    if planar:
        gx, ggain1, gshift1 = finish(ns, nb, dproj, wq, mine, dx1, gain1)
        x1, gws[1] = lax.optimization_barrier((x1, gws[1]))
        out = ff_out(nb, gs, wgs, x1, bias2)
    else:
        dh1 = scatter_seq(dot_t(dproj, unpermute(ns, nb, wq)))
        normed1, rstd1 = norm_stats(mine.astype(F32))
        ggain1 = jnp.sum(dh1 * normed1, 0)
        gshift1 = jnp.sum(dh1, 0)
        gx = dx1 + norm_back(dh1, normed1, rstd1, gain1)
        y = 0.0
        for g, wg in zip(gs, wgs):
            w2 = wg[:, ns * depth :].reshape(nb, pieces, part, chunk).transpose(0, 2, 1, 3).reshape(chunk, width)
            y += jnp.dot(g, w2, preferred_element_type=F32)
        out = (x1 + (scatter_seq(y) + bias2)).astype(BF)

    gw1 = jnp.stack([gw[: ns * depth].reshape(ns, depth, nb, part) for gw in gws], 3)
    gw1 = lax.all_to_all(gw1, "seq", 0, 1).astype(F32).reshape(depth, ns * hidden)
    gw2 = jnp.stack([gw[ns * depth :].reshape(pieces, part, chunk) for gw in gws], 0)
    gw2 = gw2.astype(F32).transpose(0, 2, 1, 3).reshape(PARTS * part, width)
    if planar:
        gwqkv, gwo = home(ns, gattn)
    else:
        gwqkv = gattn[: 3 * ns * depth].reshape(3, ns, depth, share)
        gwqkv = lax.all_to_all(gwqkv, "seq", 1, 2).astype(F32).transpose(1, 0, 2, 3).reshape(depth, 3 * width)
        gwo = gattn[3 * ns * depth :].reshape(ns, depth, share).astype(F32).transpose(1, 0, 2).reshape(depth, width)

    def place(part, size):
        return lax.dynamic_update_slice_in_dim(jnp.zeros((size,), F32), part, seq * part.shape[0], 0)

    gqv = gqv[0]
    gqv = jnp.concatenate([place(gqv[:share], width), place(gqv[2 * share :], width)])
    gb1 = place(jnp.stack(gb1, 1).reshape(-1), ns * hidden)
    gb2 = jnp.sum(cot_f, 0)
    sums = (ggain1, gshift1, gqv, gob, ggain2, gshift2, gb1, gb2)
    sums = jnp.concatenate([t.reshape(ns * nb, -1) for t in sums], 1)
    if planar:
        sums = jnp.pad(sums, ((0, 0), (0, 1024 - sums.shape[1]))).reshape(ns, nb, 8, 128)
        sums = small_sums(ns, nb, sums.transpose(1, 0, 2, 3)).reshape(-1)
    else:
        sums = lax.psum_scatter(sums, ("seq", "batch"), scatter_dimension=0, tiled=True)[0]
    small, at = [], 0
    for vec in vectors:
        small.append(sums[at : at + vec.shape[0]])
        at += vec.shape[0]
    return (
        out[None],
        gx[None],
        small[0],
        small[1],
        gwqkv,
        small[2],
        gwo,
        small[3],
        small[4],
        small[5],
        gw1,
        small[6],
        gw2,
        small[7],
    )


def solution(mesh):
    shard = P(("seq", "batch"))
    shard2 = P(("seq", "batch"), None)
    acts = P("batch", "seq", None)
    return jax.shard_map(
        body,
        mesh=mesh,
        in_specs=(acts, P("batch"), shard, shard, shard2, shard, shard2, shard, shard, shard, shard2, shard, shard2, shard, acts),
        out_specs=(acts, acts, shard, shard, shard2, shard, shard2, shard, shard, shard, shard2, shard, shard2, shard),
        check_vma=False,
    )
```

time: 911 us -> 636 us (0.70)
  Pallas kernels: 0 us -> 508 us
  waiting for transfers between devices: 398 us -> 57.5 us
  matrix products: 150 us -> 0 us
  local copies, waits for them, and re-layouts: 147 us -> 38 us
  blocking collectives: 75.4 us -> 0 us
  other arithmetic: 74 us -> 8.56 us
  starting transfers between devices: 41.4 us -> 3.97 us
    pallas_call x0 -> x12, Pallas kernels: none -> 508 us  [the longest x1 90.2 us: ff_back(): pl.pallas_call(functools.partial(ff_back_kernel, ns, nb, count), out_shap...]
    ppermute x40 -> x0, waiting for transfers between devices: 167 us -> none  [swap(): return lax.ppermute(value, 'seq', [(i, i ^ bit) for i in range(count)])]
    dot_general x18 -> x0, matrix products: 150 us -> none  [the longest x1 19.4 us: body(): dg = jnp.einsum('td,fd->tf', cot, w2, preferred_element_type=F32)]
    unnamed x10 -> x7, waiting for transfers between devices: 101 us -> 1.3 us
    reduce_scatter x4 -> x3, waiting for transfers between devices: 120 us -> 19.7 us  [scatter_batch(): return lax.psum_scatter(flat, 'batch', scatter_dimension=0, tiled=True)]
    all_gather x1 -> x0, blocking collectives: 43 us -> none  [body(): lax.all_gather(jnp.concatenate(vectors), ('seq', 'batch'), axis=0, tiled=...]
    all_gather x3, waiting for transfers between devices: 0.01 us -> 36.5 us  [the longest x2 36.5 us: body(): lax.all_gather(pack, 'batch', axis=0, tiled=True).reshape(nb, -1, chunk)]
    convert_element_type x24 -> x2, local copies, waits for them, and re-layouts: 37.6 us -> 3.97 us  [body(): lax.all_to_all(gw1, 'seq', 0, 1).astype(F32).reshape(depth, ns * hidden)]
  transfers between devices with their start and end apart: 51 -> 8, of which waited for: 32 -> 2; matrix products, arithmetic and copies ran while one was open for 29% -> 5% of each run, Pallas kernels for 0% -> 76%
where the time goes in v2:
time: 636 us; the launch traced here: 632 us
  Pallas kernels  508 us (80%)
  waiting for transfers between devices  57.5 us (9%)
  local copies, waits for them, and re-layouts  38 us (6%)
  between operations  15.5 us (2%)
  other arithmetic  8.56 us (1%)
    pallas_call x1, Pallas kernels, ff_back(): pl.pallas_call(functools.partial(ff_back_kernel, ns, nb, count), out_shap...  90.2 us
    pallas_call x1, Pallas kernels, collect(): pl.pallas_call(functools.partial(collect_kernel, ns, nb, parts), out_shap...  82.3 us
    pallas_call x1, Pallas kernels, middle(): pl.pallas_call(middle_kernel, out_shape=(jax.ShapeDtypeStruct((rows, widt...  76.7 us
    pallas_call x2, Pallas kernels, ff_chunk(): pl.pallas_call(functools.partial(ff_kernel, ns, nb), out_shape=(jax.Shape...  62.9 us
    pallas_call x1, Pallas kernels, finish(): pl.pallas_call(functools.partial(finish_kernel, ns, nb), out_shape=(jax.S...  51.2 us
    pallas_call x1, Pallas kernels, ff_out(): pl.pallas_call(functools.partial(ff_out_kernel, nb, count), out_shape=jax...  45.2 us
    all_gather x2, waiting for transfers between devices, body(): lax.all_gather(pack, 'batch', axis=0, tiled=True).reshape(nb, -1, chunk)  36.5 us
    pallas_call x1, Pallas kernels, attend_back(): pl.pallas_call(functools.partial(attend_back_kernel, ns, nb), out_shape=(...  33.4 us
  transfers between devices with their start and end apart: 8, of which 2 were waited for; matrix products, arithmetic and copies ran while one was open for 5% of the time, Pallas kernels for 76%

profile of v2, /device:TPU:0, one launch (start us, length us, event | category | flops | bytes accessed | tf_op | source)
XLA Modules:
  0.0 631.7 jit_solution(13019166611510225206)
XLA Ops:
  7.2 5.4 concatenate.17
  13.3 17.0 %spread_qkv.1 = (bf16[256,1536]{1,0:T(8,128)(2,1)}, f32[8,4,8,128]{3,2,1,0:T(8,128)}) custom-call(bf16[64,6144]{1,0:T(8,128)(2,1)} %w_qkv.1, f32[8,128]{1,0:T(8,128)} %bitcast_convert_fusion.vec), custom_call_target="tpu_custom_call" | custom-call | flops 5000000000 | bytes 786432 | tf_op jit(solution)/shard_map/spread_qkv/pallas_call | solution.py:694
  30.3 0.7 all-gather.7.cloned.1.call-update
  31.1 0.9 copy_bitcast_fusion.3
  32.0 0.7 fusion.3
  32.9 1.2 copy-done.5
  34.1 82.3 %collect.1 = (bf16[512,1024]{1,0:T(8,128)(2,1)}, bf16[512,1024]{1,0:T(8,128)(2,1)}, bf16[1024,2048]{1,0:T(8,128)(2,1)S(1)}, bf16[1024,2048]{1,0:T(8,128)(2,1)}) custom-call(bf16[64,8192]{1,0:T(8,128)(2,1)S(1)} %copy-done.3, bf16[256,2048]{1,0:T(8,128)(2,1)S(1)} %copy-done.4, bf16[256,2048]{1,0:T(8,128)(2,1)S(1)} %bitcast.84, bf16[256,2048]{1,0:T(8,128)(2,1)S(1)} %bitcast.81, ...), custom_call_target="tpu_custom_call" | custom-call | flops 40000000000 | bytes 6291456 | tf_op jit(solution)/shard_map/collect/pallas_call | solution.py:826
  116.5 2.0 copy-done.6
  120.0 0.7 reshape.138.gain.refs_6_
  120.7 0.7 reshape.139.shift
  121.4 0.7 reshape.137.obias
  122.1 0.6 fusion.bias
  122.7 0.6 slice_bitcast_fusion.3
  123.3 20.5 %attend.1 = (bf16[1024,1536]{1,0:T(8,128)(2,1)}, bf16[1024,512]{1,0:T(8,128)(2,1)}) custom-call(s32[1]{0:T(128)S(6)} %copy.74.length, bf16[1024,2048]{1,0:T(8,128)(2,1)} %copy-done.6, bf16[8,256,1536]{2,1,0:T(8,128)(2,1)} %bitcast.117, f32[1,1536]{1,0:T(1,128)} %fusion.bias), custom_call_target="tpu_custom_call" | custom-call | flops 6442450944 | bytes 6291456 | tf_op jit(solution)/shard_map/attend/pallas_call | solution.py:102
  143.9 76.7 %project_out.1 = (f32[256,2048]{1,0:T(8,128)}, bf16[1024,2048]{1,0:T(8,128)(2,1)}) custom-call(bf16[1024,512]{1,0:T(8,128)(2,1)} %get-tuple-element.52.o, bf16[512,2048]{1,0:T(8,128)(2,1)} %all-gather.7.cloned.1.call-done.wout, bf16[256,2048]{1,0:T(8,128)(2,1)} %bitcast.82, f32[1,2048]{1,0:T(1,128)} %reshape.137.obias, f32[1,2048]{1,0:T(1,128)} %reshape.138.gain.refs_6_, ...), custom_call_target="tpu_custom_call" | custom-call | flops 40000000000 | bytes 25165824 | tf_op jit(solution)/shard_map/project_out/pallas_call | solution.py:470
  220.6 31.1 %ff_chunk.2 = (bf16[8,512,1024]{2,1,0:T(8,128)(2,1)}, bf16[1024,1024]{1,0:T(8,128)(2,1)}, bf16[1024,1024]{1,0:T(8,128)(2,1)}, f32[1,1024]{1,0:T(1,128)}) custom-call(bf16[1024,2048]{1,0:T(8,128)(2,1)} %get-tuple-element.53.h2, bf16[1024,2048]{1,0:T(8,128)(2,1)} %get-tuple-element.54.cot, bf16[8,512,1024]{2,1,0:T(8,128)(2,1)} %bitcast.111, ...), custom_call_target="tpu_custom_call" | custom-call | flops 17179869184 | bytes 16777216 | tf_op jit(solution)/shard_map/ff_chunk/pallas_call | solution.py:324
  251.8 36.5 %all-gather.11.cloned.1.call-done = bf16[4096,1024]{1,0:T(8,128)(2,1)} async-done(((bf16[512,1024]{1,0:T(8,128)(2,1)}), bf16[4096,1024]{1,0:T(8,128)(2,1)}) %all-gather.11.cloned.1.call-update) | async-done | bytes 8388624 | tf_op jit(solution)/shard_map/all_gather | solution.py:1017
  288.3 31.8 %ff_chunk.3 = (bf16[8,512,1024]{2,1,0:T(8,128)(2,1)}, bf16[1024,1024]{1,0:T(8,128)(2,1)}, bf16[1024,1024]{1,0:T(8,128)(2,1)}, f32[1,1024]{1,0:T(1,128)}) custom-call(bf16[1024,2048]{1,0:T(8,128)(2,1)} %get-tuple-element.53.h2, bf16[1024,2048]{1,0:T(8,128)(2,1)} %get-tuple-element.54.cot, bf16[8,512,1024]{2,1,0:T(8,128)(2,1)} %bitcast.114, ...), custom_call_target="tpu_custom_call" | custom-call | flops 17179869184 | bytes 16777216 | tf_op jit(solution)/shard_map/ff_chunk/pallas_call | solution.py:324
  320.2 90.2 %ff_back.1 = (f32[256,2048]{1,0:T(8,128)}, bf16[1024,2048]{1,0:T(8,128)(2,1)}, f32[1,2048]{1,0:T(1,128)}, f32[1,2048]{1,0:T(1,128)}, f32[1,2048]{1,0:T(1,128)}) custom-call(bf16[1024,1024]{1,0:T(8,128)(2,1)} %get-tuple-element.62.refs_0_, bf16[1024,1024]{1,0:T(8,128)(2,1)} %get-tuple-element.63.refs_1_, bf16[8,512,1024]{2,1,0:T(8,128)(2,1)} %bitcast.112, ...), custom_call_target="tpu_custom_call" | custom-call | flops 40000000000 | bytes 25165824 | tf_op jit(solution)/shard_map/ff_back/pallas_call | solution.py:525
  410.4 33.4 %attend_back.1 = (bf16[8,1024,512]{2,1,0:T(8,128)(2,1)}, bf16[1024,1536]{1,0:T(8,128)(2,1)}, f32[1,1536]{1,0:T(1,128)}) custom-call(s32[1]{0:T(128)S(6)} %copy.74.length, bf16[1024,2048]{1,0:T(8,128)(2,1)} %copy-done.6, bf16[1024,2048]{1,0:T(8,128)(2,1)} %get-tuple-element.66.da, bf16[512,2048]{1,0:T(8,128)(2,1)} %all-gather.7.cloned.1.call-done.wout, ...), custom_call_target="tpu_custom_call" | custom-call | flops 12884901888 | bytes 12582912 | tf_op jit(solution)/shard_map/attend_back/pallas_call | solution.py:200
  443.8 1.1 copy-done.1
  445.2 0.7 reshape.145.refs_5_
  446.8 0.7 reduce.17
  447.5 0.7 reduce.18
  448.2 0.7 reduce.19
  449.1 19.6 %reduce-scatter.4.cloned.1.call-done = bf16[512,1024]{1,0:T(8,128)(2,1)} async-done(((bf16[4096,1024]{1,0:T(8,128)(2,1)}), bf16[512,1024]{1,0:T(8,128)(2,1)}) %reduce-scatter.4.cloned.1.call-update) | async-done | bytes 1048592 | tf_op jit(solution)/shard_map/reduce_scatter | solution.py:946
  468.7 1.3 fusion.2
  470.1 51.2 %attend_input.1 = (f32[256,2048]{1,0:T(8,128)}, f32[1,2048]{1,0:T(1,128)}, f32[1,2048]{1,0:T(1,128)}) custom-call(bf16[1024,1536]{1,0:T(8,128)(2,1)} %get-tuple-element.68.dproj, bf16[8,256,1536]{2,1,0:T(8,128)(2,1)} %bitcast.118, bf16[256,2048]{1,0:T(8,128)(2,1)} %bitcast.83, f32[256,2048]{1,0:T(8,128)} %get-tuple-element.69.dx1, f32[1,2048]{1,0:T(1,128)} %copy-done.2), custom_call_target="tpu_custom_call" | custom-call | flops 20000000000 | bytes 6291456 | tf_op jit(solution)/shard_map/attend_input/pallas_call | solution.py:572
  521.3 1.4 reduce.15
  522.8 1.4 reduce.16
  524.5 2.8 copy.51
  527.3 3.5 all-to-all-start
  531.5 0.7 copy_bitcast_fusion.2.sums
  532.2 45.2 %ff_out.1 = bf16[256,2048]{1,0:T(8,128)(2,1)} custom-call(bf16[1024,1024]{1,0:T(8,128)(2,1)} %get-tuple-element.56.refs_0_, bf16[1024,1024]{1,0:T(8,128)(2,1)} %get-tuple-element.58.refs_1_, bf16[8,512,1024]{2,1,0:T(8,128)(2,1)} %bitcast.113, bf16[8,512,1024]{2,1,0:T(8,128)(2,1)} %bitcast.116, f32[256,2048]{1,0:T(8,128)} %get-tuple-element.61.refs_4_, ...), custom_call_target="tpu_custom_call" | custom-call | flops 20000000000 | bytes 6291456 | tf_op jit(solution)/shard_map/ff_out/pallas_call | solution.py:628
  577.4 14.7 %small_sums.1 = f32[8,128]{1,0:T(8,128)} custom-call(f32[8,4,8,128]{3,2,1,0:T(8,128)} %copy_bitcast_fusion.2.sums), custom_call_target="tpu_custom_call" | custom-call | flops 5000000000 | bytes 131072 | tf_op jit(solution)/shard_map/small_sums/pallas_call | solution.py:869
  592.7 1.3 slice.104
  594.5 1.6 maximum_convert_fusion
  596.1 2.2 copy.60
  599.4 0.7 convert_bitcast_fusion
  600.2 1.3 copy.52
  601.5 2.7 reshape.162
  604.2 14.1 %home.1 = (f32[64,6144]{1,0:T(8,128)}, f32[64,2048]{1,0:T(8,128)}) custom-call(bf16[1024,512]{1,0:T(8,128)(2,1)} %reduce-scatter.8.cloned.1.call-done.summed), custom_call_target="tpu_custom_call" | custom-call | flops 5000000000 | bytes 2097152 | tf_op jit(solution)/shard_map/home/pallas_call | solution.py:921
  618.3 1.0 copy.75
  619.2 1.0 copy-done.7
  620.2 1.3 copy.76
  621.5 0.8 copy-done.8
  622.4 1.1 copy.77
  623.8 0.8 copy.78
  (93 shorter events, 7.0 us)
Async XLA Ops:
  7.2 116.1 %all-gather.5.cloned.1.call-start = ((), (), s32[]{:S(2)}) async-start(), calls=%async_computation.4 | async-start | bytes 7077888 | tf_op jit(solution)/shard_map/all_gather | solution.py:993
  13.2 19.6 %copy-start = (bf16[1,256,2048]{2,1,0:T(8,128)(2,1)S(1)}, bf16[1,256,2048]{2,1,0:T(8,128)(2,1)}, u32[]{:S(2)}) copy-start(bf16[1,256,2048]{2,1,0:T(8,128)(2,1)} %param.29) | copy-start | bytes 3145732
  13.2 19.6 %copy-start.3 = (bf16[64,8192]{1,0:T(8,128)(2,1)S(1)}, bf16[64,8192]{1,0:T(8,128)(2,1)}, u32[]{:S(2)}) copy-start(bf16[64,8192]{1,0:T(8,128)(2,1)} %w1.1) | copy-start | bytes 3145732
  13.3 19.6 %copy-start.4 = (bf16[256,2048]{1,0:T(8,128)(2,1)S(1)}, bf16[256,2048]{1,0:T(8,128)(2,1)}, u32[]{:S(2)}) copy-start(bf16[256,2048]{1,0:T(8,128)(2,1)} %w2.1) | copy-start | bytes 3145732
  30.3 113.6 %all-gather.7.cloned.1.call-start = ((), (), s32[]{:S(2)}) async-start(), calls=%async_computation.5 | async-start | bytes 2359296 | tf_op jit(solution)/shard_map/all_gather | solution.py:985
  31.0 189.6 %all-gather.9.cloned.1.call-start = ((), (), s32[]{:S(2)}) async-start(), calls=%async_computation.6 | async-start | bytes 9437184 | tf_op jit(solution)/shard_map/all_gather | solution.py:1017
  32.8 83.7 %copy-start.2 = (f32[1,2048]{1,0:T(1,128)}, f32[1,2048]{1,0:T(1,128)S(1)}, u32[]{:S(2)}) copy-start(f32[1,2048]{1,0:T(1,128)S(1)} %reshape.133.gain) | copy-start | bytes 24580
  32.9 1.2 copy-start.5
  116.4 2.0 copy-start.6
  118.5 169.8 %all-gather.11.cloned.1.call-start = ((), (), s32[]{:S(2)}) async-start(), calls=%async_computation.7 | async-start | bytes 9437184 | tf_op jit(solution)/shard_map/all_gather | solution.py:1017
  119.0 291.3 %reduce-scatter.6.cloned.1.call-start = ((), (), s32[]{:S(2)}) async-start(), calls=%async_computation.9 | async-start | bytes 9437184 | tf_op jit(solution)/shard_map/reduce_scatter | solution.py:946
  251.7 217.0 %reduce-scatter.4.cloned.1.call-start = ((), (), s32[]{:S(2)}) async-start(), calls=%async_computation.8 | async-start | bytes 9437184 | tf_op jit(solution)/shard_map/reduce_scatter | solution.py:946
  320.1 284.0 %reduce-scatter.8.cloned.1.call-start = ((), (), s32[]{:S(2)}) async-start(), calls=%async_computation.10 | async-start | bytes 9437184 | tf_op jit(solution)/shard_map/reduce_scatter | solution.py:946
  443.7 1.2 copy-start.1
  443.8 1.5 copy-start.12
  443.8 2.1 copy-start.17
  443.8 2.1 copy-start.18
  443.8 3.0 copy-start.15
  443.8 3.7 copy-start.14
  443.8 4.4 copy-start.13
  470.1 54.1 %copy-start.9 = (bf16[512,1024]{1,0:T(8,128)(2,1)S(1)}, bf16[512,1024]{1,0:T(8,128)(2,1)}, u32[]{:S(2)}) copy-start(bf16[512,1024]{1,0:T(8,128)(2,1)} %reduce-scatter.6.cloned.1.call-done) | copy-start | bytes 3145732
  524.5 6.3 %copy-start.19 = (f32[1,1536]{1,0:T(1,128)S(1)}, f32[1,1536]{1,0:T(1,128)}, u32[]{:S(2)}) copy-start(f32[1,1536]{1,0:T(1,128)} %get-tuple-element.73) | copy-start | bytes 18436
  527.3 72.1 %all-to-all-start = ((bf16[4,64,1,8,2,128]{5,4,3,1,2,0:T(2,128)(2,1)}), bf16[4,64,1,8,2,128]{5,4,3,1,2,0:T(2,128)(2,1)S(1)}, u32[]{:S(2)}, u32[]{:S(2)}) async-start(bf16[4,64,1,8,2,128]{5,4,3,1,2,0:T(2,128)(2,1)} %copy.51), calls=%async_computation.3 | async-start | bytes 2097152 | tf_op jit(solution)/shard_map/all_to_all | solution.py:1069
  596.1 2.2 copy-start.16
  604.2 14.1 %copy-start.10 = (bf16[256,2048]{1,0:T(8,128)(2,1)S(1)}, bf16[256,2048]{1,0:T(8,128)(2,1)}, u32[]{:S(2)}) copy-start(bf16[256,2048]{1,0:T(8,128)(2,1)} %ff_out.1) | copy-start | bytes 3145732
  618.2 2.0 copy-start.7
  620.2 2.2 copy-start.8
  622.4 1.4 copy-start.11
Sparse Core Ops, SparseCore 0:
  30.4 63.1 all-gather.4
  95.2 27.7 all-gather.6
  124.6 81.5 all-gather.8
  207.6 80.5 all-gather.10
  290.4 88.1 reduce-scatter.5
  380.7 87.9 reduce-scatter.3
  471.0 87.9 reduce-scatter.7

commit v3 on v2

v3 whole, which is shorter than its diff:
```python
import functools
import math

import jax
import jax.numpy as jnp
from jax import lax
from jax.experimental import pallas as pl
from jax.experimental.pallas import tpu as pltpu
from jax.sharding import PartitionSpec as P

HEAD_DIM = 128
WINDOW = 256
EPS = 1e-05
BF = jnp.bfloat16
F32 = jnp.float32
ROOT = math.sqrt(2.0 / math.pi)


def norm_stats(values):
    mean = jnp.mean(values, -1, keepdims=True)
    centred = values - mean
    rstd = lax.rsqrt(jnp.mean(centred * centred, -1, keepdims=True) + EPS)
    return centred * rstd, rstd


def norm_back(grad, normed, rstd, gain):
    dn = grad * gain
    return rstd * (
        dn - jnp.mean(dn, -1, keepdims=True) - normed * jnp.mean(dn * normed, -1, keepdims=True)
    )


def dot_t(left, right):
    return lax.dot_general(left, right, (((1,), (1,)), ((), ())), preferred_element_type=F32)


def t_dot(left, right):
    return lax.dot_general(left, right, (((0,), (0,)), ((), ())), preferred_element_type=F32)


def load_rows(ns, nb, depth, src, dst, sem):
    def one(k, carry):
        s, b = k // nb, lax.rem(k, nb)
        pltpu.make_async_copy(
            src.at[b, pl.ds(s * depth, depth), :], dst.at[pl.ds(k * depth, depth), :], sem
        ).start()
        return carry

    lax.fori_loop(0, ns * nb, one, 0)


def load_attention(ns, nb, packed, w, sem):
    share = packed.shape[2]
    depth = packed.shape[1] // (4 * ns)

    def one(k, carry):
        s, b = k // nb, lax.rem(k, nb)
        for t in range(3):
            pltpu.make_async_copy(
                packed.at[b, pl.ds((t * ns + s) * depth, depth), :],
                w.at[pl.ds(k * depth, depth), t * share : (t + 1) * share],
                sem,
            ).start()
        return carry

    lax.fori_loop(0, ns * nb, one, 0)


def load_out(ns, nb, packed, wout, sem):
    share = packed.shape[2]
    depth = packed.shape[1] // (4 * ns)

    def one(b, carry):
        for p in range(ns):
            pltpu.make_async_copy(
                packed.at[b, (3 * ns + p) * depth : (3 * ns + p + 1) * depth, :],
                wout.at[pl.ds(b * depth, depth), p * share : (p + 1) * share],
                sem,
            ).start()
        return carry

    lax.fori_loop(0, nb, one, 0)


def soft_block(query, keys, block, first, length):
    rows, count = query.shape[0], keys.shape[0]
    scores = dot_t(query, keys) * HEAD_DIM ** (-0.5)
    query_pos = block * rows + lax.broadcasted_iota(jnp.int32, (rows, count), 0)
    key_pos = first + lax.broadcasted_iota(jnp.int32, (rows, count), 1)
    back = query_pos - key_pos
    valid = (back >= 0) & (back < WINDOW) & ((key_pos < length) | (back == 0))
    scores = jnp.where(valid, scores, -1e30)
    expo = jnp.exp(scores - jnp.max(scores, -1, keepdims=True))
    return expo / jnp.sum(expo, -1, keepdims=True)


def attend_kernel(ns, nb, length, h1, wq, bias, qkv, o, h1t, w, sem):
    tokens, width = h1.shape
    share = o.shape[1]
    rows = tokens // ns
    load_attention(ns, nb, wq, w, sem)
    for r in range(0, tokens, 256):
        h1t[:, r : r + 256] = h1[r : r + 256, :].T
    pltpu.make_async_copy(w, w, sem).wait()
    wide = min(512, 3 * share)

    def project(j, carry):
        cols = pl.ds(pl.multiple_of(j * wide, wide), wide)
        for r in range(0, tokens, 256):
            part = jnp.dot(h1[r : r + 256, :], w[:, cols], preferred_element_type=F32)
            qkv[r : r + 256, cols] = (part + bias[:, cols]).astype(BF)
        return carry

    lax.fori_loop(0, 3 * share // wide, project, 0)
    limit = length[0]

    def head(h, carry):
        at = h * HEAD_DIM
        col_q = pl.ds(pl.multiple_of(at, HEAD_DIM), HEAD_DIM)
        col_k = pl.ds(pl.multiple_of(share + at, HEAD_DIM), HEAD_DIM)
        col_v = pl.ds(pl.multiple_of(2 * share + at, HEAD_DIM), HEAD_DIM)
        for n in range(ns):
            first = max(n - 1, 0) * rows
            mine, seen = slice(n * rows, n * rows + rows), slice(first, first + 2 * rows)
            probs = soft_block(qkv[mine, col_q], qkv[seen, col_k], n, first, limit)
            part = jnp.dot(probs.astype(BF), qkv[seen, col_v], preferred_element_type=F32)
            o[mine, col_q] = part.astype(BF)
        return carry

    lax.fori_loop(0, share // HEAD_DIM, head, 0)


def attend(ns, nb, lengths, h1, wq, bias):
    tokens, width = h1.shape
    share = wq.shape[2]
    vm = pl.BlockSpec(memory_space=pltpu.VMEM)
    return pl.pallas_call(
        functools.partial(attend_kernel, ns, nb),
        out_shape=(
            jax.ShapeDtypeStruct((tokens, 3 * share), BF),
            jax.ShapeDtypeStruct((tokens, share), BF),
            jax.ShapeDtypeStruct((width, tokens), BF),
        ),
        in_specs=[pl.BlockSpec(memory_space=pltpu.SMEM), vm, pl.BlockSpec(memory_space=pl.ANY), vm],
        out_specs=(vm, vm, vm),
        scratch_shapes=[pltpu.VMEM((width, 3 * share), BF), pltpu.SemaphoreType.DMA],
        compiler_params=pltpu.CompilerParams(vmem_limit_bytes=56 * 2**20),
        cost_estimate=pl.CostEstimate(
            flops=6 * tokens * width * share, bytes_accessed=2 * wq.size, transcendentals=tokens * 512 * share // 128
        ),
        name="attend",
    )(lengths, h1, wq, bias)


def attend_back_kernel(ns, nb, length, h1t, da, wq, o, qkv, packed, dproj, gqv, do, gw, gwo, wout, acc_k, acc_v, sems):
    width, tokens = h1t.shape
    share = o.shape[1]
    rows = tokens // ns
    depth = width // (ns * nb)
    scale = HEAD_DIM ** (-0.5)
    limit = length[0]
    load_out(ns, nb, wq, wout, sems.at[2])
    pltpu.make_async_copy(wout, wout, sems.at[2]).wait()
    for r in range(0, tokens, 256):
        do[r : r + 256, :] = dot_t(da[r : r + 256, :], wout[...]).astype(BF)
    ot = o[...].T
    for c in range(0, width, 512):
        gwo[:, c : c + 512] = jnp.dot(ot, da[:, c : c + 512], preferred_element_type=F32).astype(BF)

    def store_out(b, carry):
        for p in range(ns):
            pltpu.make_async_copy(
                gwo.at[pl.ds(b * depth, depth), p * share : (p + 1) * share],
                packed.at[b, (3 * ns + p) * depth : (3 * ns + p + 1) * depth, :],
                sems.at[0],
            ).start()
        return carry

    lax.fori_loop(0, nb, store_out, 0)

    def head(h, carry):
        at = h * HEAD_DIM
        col_q = pl.ds(pl.multiple_of(at, HEAD_DIM), HEAD_DIM)
        col_k = pl.ds(pl.multiple_of(share + at, HEAD_DIM), HEAD_DIM)
        col_v = pl.ds(pl.multiple_of(2 * share + at, HEAD_DIM), HEAD_DIM)
        acc_k[...] = jnp.zeros_like(acc_k)
        acc_v[...] = jnp.zeros_like(acc_v)
        for n in range(ns):
            first = max(n - 1, 0) * rows
            mine, seen = slice(n * rows, n * rows + rows), slice(first, first + 2 * rows)
            query, keys, grad = qkv[mine, col_q], qkv[seen, col_k], do[mine, col_q]
            probs = soft_block(query, keys, n, first, limit)
            dp = dot_t(grad, qkv[seen, col_v])
            ds = (probs * (dp - jnp.sum(dp * probs, -1, keepdims=True))).astype(BF)
            dq = jnp.dot(ds, keys, preferred_element_type=F32) * scale
            dproj[mine, col_q] = dq.astype(BF)
            acc_k[seen, :] += t_dot(ds, query)
            acc_v[seen, :] += t_dot(probs.astype(BF), grad)
        dproj[:, col_k] = (acc_k[...] * scale).astype(BF)
        dproj[:, col_v] = acc_v[...].astype(BF)
        return carry

    lax.fori_loop(0, share // HEAD_DIM, head, 0)
    wide = min(512, 3 * share)

    def weights(j, carry):
        cols = pl.ds(pl.multiple_of(j * wide, wide), wide)
        gqv[:, cols] = jnp.sum(dproj[:, cols].astype(F32), 0, keepdims=True)
        for r in range(0, width, 512):
            gw[r : r + 512, cols] = jnp.dot(
                h1t[r : r + 512, :], dproj[:, cols], preferred_element_type=F32
            ).astype(BF)
        return carry

    lax.fori_loop(0, 3 * share // wide, weights, 0)

    def store(k, c):
        s, b = k // nb, lax.rem(k, nb)
        for t in range(3):
            pltpu.make_async_copy(
                gw.at[pl.ds(k * depth, depth), t * share : (t + 1) * share],
                packed.at[b, pl.ds((t * ns + s) * depth, depth), :],
                sems.at[1],
            ).start()
        return c

    lax.fori_loop(0, ns * nb, store, 0)
    pltpu.make_async_copy(gw, gw, sems.at[1]).wait()
    pltpu.make_async_copy(gwo, gwo, sems.at[0]).wait()


def attend_back(ns, nb, lengths, h1t, da, wq, o, qkv):
    width, tokens = h1t.shape
    share = o.shape[1]
    vm = pl.BlockSpec(memory_space=pltpu.VMEM)
    hbm = pl.BlockSpec(memory_space=pl.ANY)
    return pl.pallas_call(
        functools.partial(attend_back_kernel, ns, nb),
        out_shape=(
            jax.ShapeDtypeStruct((nb, 4 * width // nb, share), BF),
            jax.ShapeDtypeStruct((tokens, 3 * share), BF),
            jax.ShapeDtypeStruct((1, 3 * share), F32),
        ),
        in_specs=[pl.BlockSpec(memory_space=pltpu.SMEM), vm, vm, hbm, vm, vm],
        out_specs=(hbm, vm, vm),
        scratch_shapes=[
            pltpu.VMEM((tokens, share), BF),
            pltpu.VMEM((width, 3 * share), BF),
            pltpu.VMEM((share, width), BF),
            pltpu.VMEM((share, width), BF),
            pltpu.VMEM((tokens, HEAD_DIM), F32),
            pltpu.VMEM((tokens, HEAD_DIM), F32),
            pltpu.SemaphoreType.DMA((3,)),
        ],
        compiler_params=pltpu.CompilerParams(vmem_limit_bytes=56 * 2**20),
        cost_estimate=pl.CostEstimate(
            flops=40 * 10**9, bytes_accessed=12 * width * share, transcendentals=tokens * 512 * share // 128
        ),
        name="attend_back",
    )(lengths, h1t, da, wq, o, qkv)


MESH = pl.DeviceIdType.MESH


def send(src, dst, sends, recvs, to):
    one = pltpu.make_async_remote_copy(
        src_ref=src, dst_ref=dst, send_sem=sends, recv_sem=recvs, device_id=to, device_id_type=MESH
    )
    one.start()
    return one


class Line:
    def __init__(self, step, own, prior, got, held, load, sends, recvs):
        self.step, self.own, self.prior, self.got, self.held = step, own, prior, got, held
        self.load, self.sends, self.recvs = load, sends, recvs
        self.last = own.shape[0] - 1
        self.seq, batch = lax.axis_index("seq"), lax.axis_index("batch")
        self.chip, self.core = batch // 2, lax.rem(batch, 2)

    def ready(self):
        self.got[...] = jnp.zeros_like(self.got)
        ahead = self.last - self.step
        wanted = jnp.minimum(self.chip + ahead, self.last), jnp.maximum(self.chip - ahead, 0)
        for way, chunk in enumerate(wanted):
            pltpu.make_async_copy(self.own.at[chunk], self.held.at[way], self.load.at[way]).start()

    def neighbours(self):
        count = self.last + 1
        return [(self.seq, 2 * lax.rem(self.chip + d, count) + self.core) for d in (1, count - 1)]

    def copy(self, way):
        to = jnp.minimum(self.chip + 1, self.last) if way == 0 else jnp.maximum(self.chip - 1, 0)
        return pltpu.make_async_remote_copy(
            src_ref=self.held.at[way],
            dst_ref=self.got.at[way],
            send_sem=self.sends.at[way],
            recv_sem=self.recvs.at[way],
            device_id=(self.seq, 2 * to + self.core),
            device_id_type=MESH,
        )

    def roles(self):
        chip, last, step = self.chip, self.last, self.step
        gives = chip <= step, chip >= last - step
        takes = (chip >= 1) & (chip <= step + 1), (chip <= last - 1) & (chip >= last - 1 - step)
        return gives, takes

    def go(self):
        for way in range(2):
            here = self.held.at[way]
            pltpu.make_async_copy(here, here, self.load.at[way]).wait()
            if self.prior is not None:
                total = self.held[way].astype(F32) + self.prior[way].astype(F32)
                self.held[way] = total.astype(BF)

            @pl.when(self.roles()[0][way])
            def _():
                self.copy(way).start()

    def stop(self):
        gives, takes = self.roles()
        for way in range(2):

            @pl.when(takes[way])
            def _():
                self.copy(way).wait_recv()

            @pl.when(gives[way])
            def _():
                self.copy(way).wait_send()


def line_scratch(rows, width):
    dma = pltpu.SemaphoreType.DMA
    return [pltpu.VMEM((2, rows, width), BF), dma((2,)), dma((2,)), dma((2,))]


def ff_kernel(ns, nb, first, moving, *refs):
    line = None
    if first:
        h2, cot, wg, bias, *gwg, g_out, du_out, gb, h2t, dh2, w1, w2, gw1, gw2, sems = refs
    elif moving:
        h2, h2t, cot, wg, bias, own, *gwg, g_out, du_out, gb, got, w1, w2, gw1, gw2, sems, held, s0, s1, s2 = refs
        line = Line(0, own, None, got, held, s0, s1, s2)
    else:
        h2, h2t, cot, wg, bias, *gwg, g_out, du_out, gb, w1, w2, gw1, gw2, sems = refs
    core = lax.rem(lax.axis_index("batch"), 2)

    def store(src, b, rows, cols, sem):
        if len(gwg) == 1:
            pltpu.make_async_copy(src, gwg[0].at[b, rows, cols], sem).start()
        else:

            @pl.when(lax.rem(b, 2) == core)
            def _():
                pltpu.make_async_copy(src, gwg[0].at[b // 2, rows, cols], sem).start()

            @pl.when(lax.rem(b, 2) != core)
            def _():
                pltpu.make_async_copy(src, gwg[1].at[b // 2, rows, cols], sem).start()

    tokens, width = h2.shape
    chunk = g_out.shape[1]
    depth = width // (ns * nb)
    part = chunk // nb
    pieces = width // chunk
    half = ns * depth
    tile = min(512, chunk)
    tiles = chunk // tile
    step = min(256, tokens)

    def load1(k, carry):
        s, b = k // nb, lax.rem(k, nb)
        pltpu.make_async_copy(
            wg.at[b, pl.ds(s * depth, depth), :], w1.at[pl.ds(k * depth, depth), :], sems.at[0]
        ).start()
        return carry

    def load2(k, carry):
        for p in range(pieces):
            pltpu.make_async_copy(
                wg.at[k, pl.ds(half + p * part, part), :],
                w2.at[pl.ds(k * part, part), p * chunk : (p + 1) * chunk],
                sems.at[1],
            ).start()
        return carry

    lax.fori_loop(0, ns * nb, load1, 0)
    lax.fori_loop(0, nb, load2, 0)
    if moving:
        line.ready()
        barrier = pltpu.get_barrier_semaphore()
        for other in line.neighbours():
            pl.semaphore_signal(barrier, inc=1, device_id=other, device_id_type=MESH)
        pl.semaphore_wait(barrier, 2)
        line.go()
    if first:
        for r in range(0, tokens, step):
            h2t[:, r : r + step] = h2[r : r + step, :].T
    pltpu.make_async_copy(w1, w1, sems.at[0]).wait()
    pltpu.make_async_copy(w2, w2, sems.at[1]).wait()

    def one_tile(j, carry):
        at = pl.multiple_of(j * tile, tile)
        cols = pl.ds(at, tile)
        total = jnp.zeros((1, tile), F32)
        for r in range(0, tokens, step):
            rows = slice(r, r + step)
            u = jnp.dot(h2[rows, :], w1[:, cols], preferred_element_type=F32) + bias[:, cols]
            dg = lax.dot_general(
                cot[rows, :], w2[cols, :], (((1,), (1,)), ((), ())), preferred_element_type=F32
            )
            sq = u * u
            th = jnp.tanh(ROOT * u * (1.0 + 0.044715 * sq))
            cdf = 0.5 * (1.0 + th)
            g_out[rows, cols] = (u * cdf).astype(BF)
            slope = cdf + 0.5 * u * (1.0 - th * th) * (ROOT * (1.0 + 3.0 * 0.044715 * sq))
            du = (dg * slope).astype(BF)
            du_out[rows, cols] = du
            total += jnp.sum(du.astype(F32), 0, keepdims=True)
        gb[:, cols] = total
        for r in range(0, width, 512):
            gw1[j, r : r + 512, :] = jnp.dot(
                h2t[r : r + 512, :], du_out[:, cols], preferred_element_type=F32
            ).astype(BF)
        gt = g_out[:, cols].T
        for r in range(0, width, 512):
            gw2[j, :, r : r + 512] = jnp.dot(
                gt, cot[:, r : r + 512], preferred_element_type=F32
            ).astype(BF)

        def store1(k, c):
            s, b = k // nb, lax.rem(k, nb)
            store(gw1.at[j, pl.ds(k * depth, depth), :], b, pl.ds(s * depth, depth), cols, sems.at[2])
            return c

        lax.fori_loop(0, ns * nb, store1, 0)
        count = tile // part

        def store2(k, c):
            for p in range(pieces):
                src = gw2.at[j, pl.ds(k * part, part), p * chunk : (p + 1) * chunk]
                store(src, j * count + k, pl.ds(half + p * part, part), slice(None), sems.at[3])
            return c

        lax.fori_loop(0, count, store2, 0)
        return carry

    lax.fori_loop(0, tiles, one_tile, 0)
    if first:
        for r in range(0, tokens, step):
            for c in range(0, width, 512):
                part_sum = dot_t(du_out[r : r + step, :], w1[c : c + 512, :])
                dh2[r : r + step, c : c + 512] = part_sum.astype(BF)
    pltpu.make_async_copy(gw1, gw1, sems.at[2]).wait()
    pltpu.make_async_copy(gw2, gw2, sems.at[3]).wait()
    if moving:
        line.stop()


def ff_chunk(ns, nb, h2, h2t, cot, wg, bias, split, own=None):
    tokens, width = h2.shape
    chunk = wg.shape[2]
    tile = min(512, chunk)
    first = h2t is None
    vm = pl.BlockSpec(memory_space=pltpu.VMEM)
    hbm = pl.BlockSpec(memory_space=pl.ANY)
    grads = (jax.ShapeDtypeStruct((nb // 2,) + wg.shape[1:], BF),) * 2 if split else (jax.ShapeDtypeStruct(wg.shape, BF),)
    inner = jax.ShapeDtypeStruct((tokens, chunk), BF)
    extra = (jax.ShapeDtypeStruct((width, tokens), BF), jax.ShapeDtypeStruct((tokens, width), BF)) if first else ()
    given = (h2, cot, wg, bias) if first else (h2, h2t, cot, wg, bias)
    moving = own is not None
    more = []
    if moving:
        given += (own,)
        extra = (jax.ShapeDtypeStruct((2,) + own.shape[1:], BF),)
        more = line_scratch(*own.shape[1:])
    return pl.pallas_call(
        functools.partial(ff_kernel, ns, nb, first, moving),
        out_shape=grads + (inner, inner, jax.ShapeDtypeStruct((1, chunk), F32)) + extra,
        in_specs=[hbm if one is wg or one is own else vm for one in given],
        out_specs=(hbm,) * len(grads) + (vm,) * (3 + len(extra)),
        scratch_shapes=[
            pltpu.VMEM((width, chunk), BF),
            pltpu.VMEM((chunk, width), BF),
            pltpu.VMEM((chunk // tile, width, tile), BF),
            pltpu.VMEM((chunk // tile, tile, width), BF),
            pltpu.SemaphoreType.DMA((4,)),
        ]
        + more,
        compiler_params=pltpu.CompilerParams(
            collective_id=4 if moving else None, has_side_effects=moving, vmem_limit_bytes=60 * 2**20
        ),
        cost_estimate=pl.CostEstimate(
            flops=40 * 10**9,
            bytes_accessed=4 * wg.size,
            transcendentals=tokens * chunk,
        ),
        name="ff_first" if first else "ff_chunk",
    )(*given)


def greet(more=()):
    me, batch = lax.axis_index("seq"), lax.axis_index("batch")
    by_x = me + 1 - 2 * lax.rem(me, 2)
    by_y = lax.rem(me + 2, 4)
    barrier = pltpu.get_barrier_semaphore()
    for other in [(by_x, batch), (by_y, batch), *more]:
        pl.semaphore_signal(barrier, inc=1, device_id=other, device_id_type=MESH)
    pl.semaphore_wait(barrier, 2 + len(more))
    return me, by_x, by_y, (by_x, batch), (by_y, batch)


def scatter_steps(partial, place, buffers, send, recv):
    me, by_x, by_y, to_x, to_y = place
    out, via, from_x, from_y = buffers
    half = via.shape[1]
    top, low = slice(0, half), slice(half, 2 * half)
    far = 3 - me

    def copy(k, src, dst, to):
        one = pltpu.make_async_remote_copy(
            src_ref=src, dst_ref=dst, send_sem=send.at[k], recv_sem=recv.at[k], device_id=to, device_id_type=MESH
        )
        one.start()
        return one

    out[0] = partial(far).astype(BF)
    c0 = copy(0, out.at[0, top], via.at[0], to_y)
    c1 = copy(1, out.at[0, low], via.at[1], to_x)
    yield
    block = partial(by_x)
    out[1, low] = block[low].astype(BF)
    c2 = copy(2, out.at[1, low], from_x.at[low], to_x)
    x_top = block[top]
    yield
    block = partial(by_y)
    out[2, top] = block[top].astype(BF)
    c3 = copy(3, out.at[2, top], from_y.at[top], to_y)
    y_low = block[low]
    yield
    c0.wait_recv()
    out[1, top] = (x_top + via[0].astype(F32)).astype(BF)
    c4 = copy(4, out.at[1, top], from_x.at[top], to_x)
    c1.wait_recv()
    out[2, low] = (y_low + via[1].astype(F32)).astype(BF)
    c5 = copy(5, out.at[2, low], from_y.at[low], to_y)
    yield
    mine = partial(me)
    yield
    c3.wait_recv()
    c4.wait_recv()
    mine_top = mine[top] + from_x[top].astype(F32) + from_y[top].astype(F32)
    c2.wait_recv()
    c5.wait_recv()
    mine_low = mine[low] + from_x[low].astype(F32) + from_y[low].astype(F32)
    for one in (c0, c1, c2, c3, c4, c5):
        one.wait_send()
    yield mine_top, mine_low


def scatter_sum(partial, place, buffers, send, recv):
    return list(scatter_steps(partial, place, buffers, send, recv))[-1]


def scatter_scratch(rows, width):
    return [
        pltpu.VMEM((3, rows, width), BF),
        pltpu.VMEM((2, rows // 2, width), BF),
        pltpu.VMEM((rows, width), BF),
        pltpu.VMEM((rows, width), BF),
        pltpu.SemaphoreType.DMA((6,)),
        pltpu.SemaphoreType.DMA((6,)),
    ]


def gather_blocks(full, rows, place, send, recv):
    me, by_x, by_y, to_x, to_y = place
    half = rows // 2

    def copy(k, block, part, to):
        at = full.at[pl.ds(pl.multiple_of(block * rows + part * half, half), half)]
        one = pltpu.make_async_remote_copy(
            src_ref=at, dst_ref=at, send_sem=send.at[k], recv_sem=recv.at[k], device_id=to, device_id_type=MESH
        )
        one.start()
        return one

    c0 = copy(0, me, 0, to_x)
    c3 = copy(3, me, 1, to_y)
    c2 = copy(2, me, 0, to_y)
    c1 = copy(1, me, 1, to_x)
    c0.wait_recv()
    c4 = copy(4, by_x, 0, to_y)
    c3.wait_recv()
    c5 = copy(5, by_y, 1, to_x)
    for one in (c1, c2, c4, c5):
        one.wait_recv()
    for one in (c0, c1, c2, c3, c4, c5):
        one.wait_send()


GATHER_SEMS = [pltpu.SemaphoreType.DMA((6,)), pltpu.SemaphoreType.DMA((6,))]


def middle_kernel(ns, nb, o, wq, mine, obias, gain, shift, x1, h2, wout, load_sem, out, via, from_x, from_y, s1, r1, s2, r2):
    rows, width = mine.shape
    half = rows // 2
    load_out(ns, nb, wq, wout, load_sem)
    place = greet()
    pltpu.make_async_copy(wout, wout, load_sem).wait()

    def partial(block):
        at = pl.multiple_of(block * rows, rows)
        return jnp.dot(o[pl.ds(at, rows), :], wout[...], preferred_element_type=F32)

    sums = scatter_sum(partial, place, (out, via, from_x, from_y), s1, r1)
    for part, total in enumerate(sums):
        span = slice(part * half, part * half + half)
        res = mine[span, :].astype(F32) + (total + obias[...])
        x1[span, :] = res
        normed, _ = norm_stats(res)
        at = pl.multiple_of(place[0] * rows + part * half, half)
        h2[pl.ds(at, half), :] = (normed * gain[...] + shift[...]).astype(BF)
    gather_blocks(h2, rows, place, s2, r2)


def middle(ns, nb, o, wq, mine, obias, gain, shift):
    tokens, share = o.shape
    rows, width = mine.shape
    vm = pl.BlockSpec(memory_space=pltpu.VMEM)
    return pl.pallas_call(
        functools.partial(middle_kernel, ns, nb),
        out_shape=(jax.ShapeDtypeStruct((rows, width), F32), jax.ShapeDtypeStruct((tokens, width), BF)),
        in_specs=[vm, pl.BlockSpec(memory_space=pl.ANY)] + [vm] * 4,
        out_specs=(vm, vm),
        scratch_shapes=[pltpu.VMEM((share, width), BF), pltpu.SemaphoreType.DMA] + scatter_scratch(rows, width) + GATHER_SEMS,
        compiler_params=pltpu.CompilerParams(collective_id=1, has_side_effects=True, vmem_limit_bytes=56 * 2**20),
        cost_estimate=pl.CostEstimate(flops=40 * 10**9, bytes_accessed=12 * tokens * width, transcendentals=0),
        name="project_out",
    )(o, wq, mine, obias, gain, shift)


def ff_back_kernel(ns, nb, du, wg, before, x1, cot, gain, own, prior, *refs):
    dx1, da, ggain, gshift, gob, got, w, load_sem, out, via, from_x, from_y, s1, r1, s2, r2, *moving = refs
    line = Line(1, own, prior, got, *moving)
    rows, width = x1.shape
    half = rows // 2
    load_rows(ns, nb, width // (ns * nb), wg, w, load_sem)
    line.ready()
    place = greet(line.neighbours())
    pltpu.make_async_copy(w, w, load_sem).wait()

    def partial(block):
        at = pl.multiple_of(block * rows, rows)
        return before[pl.ds(at, rows), :].astype(F32) + dot_t(du[pl.ds(at, rows), :], w[...])

    steps = scatter_steps(partial, place, (out, via, from_x, from_y), s1, r1)
    next(steps)
    line.go()
    *_, sums = steps
    totals = [jnp.zeros((1, width), F32)] * 3
    for part, grad in enumerate(sums):
        span = slice(part * half, part * half + half)
        normed, rstd = norm_stats(x1[span, :])
        res = cot[span, :].astype(F32) + norm_back(grad, normed, rstd, gain[...])
        dx1[span, :] = res
        low = res.astype(BF)
        at = pl.multiple_of(place[0] * rows + part * half, half)
        da[pl.ds(at, half), :] = low
        for k, term in enumerate((grad * normed, grad, low.astype(F32))):
            totals[k] += jnp.sum(term, 0, keepdims=True)
    ggain[...], gshift[...], gob[...] = totals
    gather_blocks(da, rows, place, s2, r2)
    line.stop()


def ff_back(ns, nb, du, wg, before, x1, cot, gain, own, prior):
    rows, width = x1.shape
    tokens, chunk = du.shape
    vm = pl.BlockSpec(memory_space=pltpu.VMEM)
    hbm = pl.BlockSpec(memory_space=pl.ANY)
    row = jax.ShapeDtypeStruct((1, width), F32)
    return pl.pallas_call(
        functools.partial(ff_back_kernel, ns, nb),
        out_shape=(
            jax.ShapeDtypeStruct((rows, width), F32),
            jax.ShapeDtypeStruct((tokens, width), BF),
            row,
            row,
            row,
            jax.ShapeDtypeStruct(prior.shape, BF),
        ),
        in_specs=[vm, hbm] + [vm] * 4 + [hbm, vm],
        out_specs=(vm,) * 6,
        scratch_shapes=[pltpu.VMEM((width, chunk), BF), pltpu.SemaphoreType.DMA]
        + scatter_scratch(rows, width)
        + GATHER_SEMS
        + line_scratch(*prior.shape[1:]),
        compiler_params=pltpu.CompilerParams(collective_id=2, has_side_effects=True, vmem_limit_bytes=56 * 2**20),
        cost_estimate=pl.CostEstimate(flops=40 * 10**9, bytes_accessed=12 * tokens * width, transcendentals=0),
        name="ff_back",
    )(du, wg, before, x1, cot, gain, own, prior)


def finish_kernel(ns, nb, count, *refs):
    dproj, wq = refs[:2]
    gs, wgs = refs[2 : 2 + count], refs[2 + count : 2 + 2 * count]
    own_sum, prior, *later = refs[2 + 2 * count : 3 + 3 * count]
    refs = refs[3 + 3 * count :]
    mine, dx1, gain, x1, bias, gx, ggain, gshift, result, gw1, gw2, w = refs[:12]
    ws, stage = refs[12 : 12 + count], refs[12 + count]
    gw2_low, load_sem, s0, r0, got, *rest = refs[13 + count :]
    first, second, moving = rest[:6], rest[6:12], rest[12:]
    line = Line(2, own_sum, prior, got, *moving)
    total = moving[0].at[0]
    summed = [total, *later]
    rows, width = mine.shape
    half = rows // 2
    chunk = gs[0].shape[1]
    part_rows, pieces, base = chunk // nb, width // chunk, width // nb
    load_attention(ns, nb, wq, w, load_sem.at[count])
    for c in range(count):

        def load(k, carry):
            for p in range(pieces):
                pltpu.make_async_copy(
                    wgs[c].at[k, pl.ds(base + p * part_rows, part_rows), :],
                    ws[c].at[pl.ds(k * part_rows, part_rows), p * chunk : (p + 1) * chunk],
                    load_sem.at[c],
                ).start()
            return carry

        lax.fori_loop(0, nb, load, 0)
    line.ready()
    me, others, met = greet_seq(ns, line.neighbours())
    by_x, by_y, batch = me + 1 - 2 * lax.rem(me, 2), lax.rem(me + 2, 4), lax.axis_index("batch")
    place = me, by_x, by_y, (by_x, batch), (by_y, batch)
    depth, hidden = gw1.shape[0], gw1.shape[1] // ns

    def ship(chunks, b, carry):
        for c in chunks:
            cols = pl.ds(pl.multiple_of(me * hidden + (b * count + c) * part_rows, part_rows), part_rows)
            from_cols = pl.ds(pl.multiple_of(b * part_rows, part_rows), part_rows)
            own = pl.ds(pl.multiple_of(me * depth, depth), depth)
            pltpu.make_async_copy(summed[c].at[own, from_cols], stage.at[:, cols], load_sem.at[count + 1]).start()
            for d, to in enumerate(others):
                theirs = pl.ds(pl.multiple_of(to[0] * depth, depth), depth)
                send(summed[c].at[theirs, from_cols], stage.at[:, cols], s0.at[d], r0.at[d], to)
        return carry

    def bring(chunks):
        lax.fori_loop(0, nb, functools.partial(ship, chunks), 0)
        for c in chunks:
            for p in range(pieces):
                here = pltpu.make_async_copy(
                    summed[c].at[ns * depth + p * part_rows : ns * depth + (p + 1) * part_rows],
                    gw2_low.at[c * part_rows : (c + 1) * part_rows, p * chunk : (p + 1) * chunk],
                    load_sem.at[count + 2],
                )
                here.start()

    met()
    line.go()
    bring(range(1, count))

    def input_grad(block):
        at = pl.multiple_of(block * rows, rows)
        return dot_t(dproj[pl.ds(at, rows), :], w[...])

    def branch(block):
        at = pl.multiple_of(block * rows, rows)
        total = jnp.dot(gs[0][pl.ds(at, rows), :], ws[0][...], preferred_element_type=F32)
        for c in range(1, count):
            total += jnp.dot(gs[c][pl.ds(at, rows), :], ws[c][...], preferred_element_type=F32)
        return total

    pltpu.make_async_copy(w, w, load_sem.at[count]).wait()
    one = scatter_steps(input_grad, place, first[:4], *first[4:])
    two = scatter_steps(branch, place, second[:4], *second[4:])
    for _ in range(3):
        next(one)
    for c in range(count):
        pltpu.make_async_copy(ws[c], ws[c], load_sem.at[c]).wait()
    next(two)
    next(one)
    next(two)
    next(two)
    next(one)
    sums = next(one)
    next(two)
    line.stop()
    own_part = pltpu.make_async_copy(own_sum.at[line.chip], total, load_sem.at[count + 3])
    own_part.start()
    own_part.wait()
    total[...] = (total[...].astype(F32) + got[0].astype(F32) + got[1].astype(F32)).astype(BF)
    bring([0])
    totals = [jnp.zeros((1, width), F32)] * 2
    for part, grad in enumerate(sums):
        span = slice(part * half, part * half + half)
        normed, rstd = norm_stats(mine[span, :].astype(F32))
        gx[span, :] = dx1[span, :] + norm_back(grad, normed, rstd, gain[...])
        for k, term in enumerate((grad * normed, grad)):
            totals[k] += jnp.sum(term, 0, keepdims=True)
    ggain[...], gshift[...] = totals
    pltpu.make_async_copy(gw2_low, gw2_low, load_sem.at[count + 2]).wait()
    gw2[...] = gw2_low[...].astype(F32)
    next(two)
    strip = stage.at[:, :hidden]
    pltpu.make_async_copy(strip, strip, load_sem.at[count + 1]).wait()
    for d, to in enumerate(others):
        pltpu.make_async_remote_copy(
            src_ref=strip, dst_ref=strip, send_sem=s0.at[d], recv_sem=r0.at[d], device_id=to, device_id_type=MESH
        ).wait()
    gw1[...] = stage[...].astype(F32)
    for part, branch_sum in enumerate(next(two)):
        span = slice(part * half, part * half + half)
        result[span, :] = (x1[span, :] + (branch_sum + bias[...])).astype(BF)


def finish(ns, nb, dproj, wq, gs, wgs, own, prior, summed, mine, dx1, gain, x1, bias):
    rows, width = mine.shape
    count, chunk = len(gs), gs[0].shape[1]
    depth, hidden = width // (ns * nb), count * chunk
    vm = pl.BlockSpec(memory_space=pltpu.VMEM)
    hbm = pl.BlockSpec(memory_space=pl.ANY)
    row = jax.ShapeDtypeStruct((1, width), F32)
    return pl.pallas_call(
        functools.partial(finish_kernel, ns, nb, count),
        out_shape=(
            jax.ShapeDtypeStruct((rows, width), F32),
            row,
            row,
            jax.ShapeDtypeStruct((rows, width), BF),
            jax.ShapeDtypeStruct((depth, hidden * ns), F32),
            jax.ShapeDtypeStruct((hidden // nb, width), F32),
        ),
        in_specs=[vm, hbm] + [vm] * count + [hbm] * (count + 1) + [vm] + [hbm] * (count - 1) + [vm] * 5,
        out_specs=(vm,) * 6,
        scratch_shapes=[pltpu.VMEM((width, dproj.shape[1]), BF)]
        + [pltpu.VMEM((chunk, width), BF)] * count
        + [pltpu.VMEM((depth, hidden * ns), BF), pltpu.VMEM((hidden // nb, width), BF)]
        + [pltpu.SemaphoreType.DMA((count + 4,)), pltpu.SemaphoreType.DMA((ns - 1,)), pltpu.SemaphoreType.DMA((ns - 1,))]
        + [pltpu.VMEM(prior.shape, BF)]
        + scatter_scratch(rows, width) * 2
        + line_scratch(*prior.shape[1:]),
        compiler_params=pltpu.CompilerParams(collective_id=3, has_side_effects=True, vmem_limit_bytes=60 * 2**20),
        cost_estimate=pl.CostEstimate(flops=40 * 10**9, bytes_accessed=24 * rows * width, transcendentals=0),
        name="finish",
    )(dproj, wq, *gs, *wgs, own, prior, *summed, mine, dx1, gain, x1, bias)


def greet_all(ns, nb):
    me, batch = lax.axis_index("seq"), lax.axis_index("batch")
    along_seq = [(lax.rem(me + d, ns), batch) for d in range(1, ns)]
    along_batch = [(me, lax.rem(batch + d, nb)) for d in range(1, nb)]
    barrier = pltpu.get_barrier_semaphore()
    for other in along_seq + along_batch:
        pl.semaphore_signal(barrier, inc=1, device_id=other, device_id_type=MESH)
    pl.semaphore_wait(barrier, ns + nb - 2)
    return me, batch, along_seq, along_batch


def greet_seq(ns, more=()):
    me, batch = lax.axis_index("seq"), lax.axis_index("batch")
    others = [(lax.rem(me + d, ns), batch) for d in range(1, ns)]
    barrier = pltpu.get_barrier_semaphore()
    for other in [*others, *more]:
        pl.semaphore_signal(barrier, inc=1, device_id=other, device_id_type=MESH)
    return me, others, lambda: pl.semaphore_wait(barrier, ns - 1 + len(more))


def spread_kernel(ns, w_qkv, w_out, packed, local, s0, r0):
    depth, width = w_out.shape
    share = packed.shape[1]
    me, others, met = greet_seq(ns)
    copies = []
    for p in range(ns):
        rows = slice((3 * ns + p) * depth, (3 * ns + p + 1) * depth)
        copies.append(pltpu.make_async_copy(w_out.at[:, p * share : (p + 1) * share], packed.at[rows], local.at[3 + p]))
    for t in range(3):
        cols = pl.ds(pl.multiple_of(t * width + me * share, share), share)
        rows = pl.ds(pl.multiple_of((t * ns + me) * depth, depth), depth)
        copies.append(pltpu.make_async_copy(w_qkv.at[:, cols], packed.at[rows], local.at[t]))
    for one in copies:
        one.start()
    met()
    for t in range(3):
        rows = pl.ds(pl.multiple_of((t * ns + me) * depth, depth), depth)
        for d, to in enumerate(others):
            cols = pl.ds(pl.multiple_of(t * width + to[0] * share, share), share)
            copies.append(send(w_qkv.at[:, cols], packed.at[rows], s0.at[t, d], r0.at[t, d], to))
    for one in copies:
        one.wait()


def spread(ns, w_qkv, w_out):
    depth, width = w_out.shape
    hbm = pl.BlockSpec(memory_space=pl.ANY)
    dma = pltpu.SemaphoreType.DMA
    return pl.pallas_call(
        functools.partial(spread_kernel, ns),
        out_shape=jax.ShapeDtypeStruct((4 * ns * depth, width // ns), BF),
        in_specs=[hbm, hbm],
        out_specs=hbm,
        scratch_shapes=[dma((3 + ns,)), dma((3, ns - 1)), dma((3, ns - 1))],
        compiler_params=pltpu.CompilerParams(collective_id=5, has_side_effects=True),
        cost_estimate=pl.CostEstimate(flops=5 * 10**9, bytes_accessed=2 * w_qkv.size, transcendentals=0),
        name="spread_qkv",
    )(w_qkv, w_out)


def whole_row(ns, nb, vecs, row, width):
    pieces = jnp.concatenate([vecs[b, s, row : row + 1, :] for b in range(nb) for s in range(ns)], 0)
    lanes = jnp.concatenate([pieces] * (width // pieces.shape[1]), 1)
    owner = lax.broadcasted_iota(jnp.int32, lanes.shape, 0)
    owner = lax.rem(owner, ns) * nb + owner // ns
    place = lax.broadcasted_iota(jnp.int32, lanes.shape, 1) // (width // (ns * nb))
    return jnp.sum(jnp.where(owner == place, lanes, 0.0), 0, keepdims=True)


def collect_kernel(ns, nb, parts, w1, w2, mine, cot, vec, *refs):
    packs = refs[:parts]
    h1, cots, vecs, acts, local, s0, r0, s1, r1, s2, r2, s3, r3, s4, r4 = refs[parts:]
    depth = w1.shape[0]
    rows, width = mine.shape
    half = rows // 2
    hidden = w1.shape[1] // ns
    part = hidden // (parts * nb)
    chunk = hidden // parts
    pieces = width // chunk
    me, batch = lax.axis_index("seq"), lax.axis_index("batch")
    by_x = me + 1 - 2 * lax.rem(me, 2)
    by_y = lax.rem(me + 2, 4)
    others = [(lax.rem(me + d, ns), batch) for d in range(1, ns)]
    column = [(me, lax.rem(batch + d, nb)) for d in range(1, nb)]
    barrier = pltpu.get_barrier_semaphore()
    for other in others + column:
        pl.semaphore_signal(barrier, inc=1, device_id=other, device_id_type=MESH)
    vecs[batch, me] = vec[...]
    at_me = pl.ds(pl.multiple_of(me * rows, rows), rows)
    acts[at_me, :] = mine[...]
    own = pltpu.make_async_copy(cot, cots.at[at_me], local.at[parts])
    own.start()
    for c in range(parts):
        for p in range(pieces):
            pltpu.make_async_copy(
                w2.at[c * part : (c + 1) * part, p * chunk : (p + 1) * chunk],
                packs[c].at[ns * depth + p * part : ns * depth + (p + 1) * part, :],
                local.at[c],
            ).start()
    at = pl.ds(pl.multiple_of(me * depth, depth), depth)

    def keep(b, carry):
        for c in range(parts):
            cols = pl.ds(pl.multiple_of(me * hidden + (b * parts + c) * part, part), part)
            here = packs[c].at[at, pl.ds(pl.multiple_of(b * part, part), part)]
            pltpu.make_async_copy(w1.at[:, cols], here, local.at[c]).start()
        return carry

    lax.fori_loop(0, nb, keep, 0)
    pl.semaphore_wait(barrier, ns + nb - 2)
    to_x, to_y = (by_x, batch), (by_y, batch)
    small = vecs.at[batch, me]
    near = [send(small, small, s3.at[d], r3.at[d], to) for d, to in enumerate(others)]

    def ship(b, carry):
        for c in range(parts):
            here = packs[c].at[at, pl.ds(pl.multiple_of(b * part, part), part)]
            for d, to in enumerate(others):
                cols = pl.ds(pl.multiple_of(to[0] * hidden + (b * parts + c) * part, part), part)
                send(w1.at[:, cols], here, s0.at[c, d], r0.at[c, d], to)
        return carry

    def normalise(block):
        span = pl.ds(pl.multiple_of(block * rows, rows), rows)
        normed, _ = norm_stats(acts[span, :].astype(F32))
        h1[span, :] = (normed * gain + shift).astype(BF)

    def copy(k, full, block, side, to, sends, recvs):
        span = full.at[pl.ds(pl.multiple_of(block * rows + side * half, half), half)]
        return send(span, span, sends.at[k], recvs.at[k], to)

    c0 = copy(0, acts, me, 0, to_x, s1, r1)
    c3 = copy(3, acts, me, 1, to_y, s1, r1)
    c2 = copy(2, acts, me, 0, to_y, s1, r1)
    c1 = copy(1, acts, me, 1, to_x, s1, r1)
    for one in near:
        one.wait_recv()
    row = vecs.at[batch]
    wide = [send(row, row, s4.at[d], r4.at[d], to) for d, to in enumerate(column)]
    lax.fori_loop(0, nb, ship, 0)
    for one in wide:
        one.wait_recv()
    gain, shift = whole_row(ns, nb, vecs, 0, width), whole_row(ns, nb, vecs, 1, width)
    normalise(me)
    c0.wait_recv()
    c4 = copy(4, acts, by_x, 0, to_y, s1, r1)
    c3.wait_recv()
    c5 = copy(5, acts, by_y, 1, to_x, s1, r1)
    own.wait()
    d0 = copy(0, cots, me, 0, to_x, s2, r2)
    d3 = copy(3, cots, me, 1, to_y, s2, r2)
    d2 = copy(2, cots, me, 0, to_y, s2, r2)
    d1 = copy(1, cots, me, 1, to_x, s2, r2)
    c1.wait_recv()
    normalise(by_x)
    c2.wait_recv()
    normalise(by_y)
    c4.wait_recv()
    c5.wait_recv()
    normalise(3 - me)
    d0.wait_recv()
    d4 = copy(4, cots, by_x, 0, to_y, s2, r2)
    d3.wait_recv()
    d5 = copy(5, cots, by_y, 1, to_x, s2, r2)
    for one in (d1, d2, d4, d5):
        one.wait_recv()
    for one in (c0, c1, c2, c3, c4, c5, d0, d1, d2, d3, d4, d5, *near, *wide):
        one.wait_send()
    for c in range(parts):
        pack = packs[c].at[: depth]
        for d, to in enumerate(others):
            rest = pltpu.make_async_remote_copy(
                src_ref=pack, dst_ref=pack, send_sem=s0.at[c, d], recv_sem=r0.at[c, d], device_id=to, device_id_type=MESH
            )
            rest.wait()
        whole = packs[c].at[: depth + pieces * part]
        pltpu.make_async_copy(whole, whole, local.at[c]).wait()


def collect(ns, nb, parts, w1, w2, mine, cot, vec):
    depth = w1.shape[0]
    rows, width = mine.shape
    chunk = w1.shape[1] // (ns * parts)
    vm = pl.BlockSpec(memory_space=pltpu.VMEM)
    hbm = pl.BlockSpec(memory_space=pl.ANY)
    dma = pltpu.SemaphoreType.DMA
    pack = jax.ShapeDtypeStruct((2 * ns * depth, chunk), BF)
    full = jax.ShapeDtypeStruct((ns * rows, width), BF)
    return pl.pallas_call(
        functools.partial(collect_kernel, ns, nb, parts),
        out_shape=(pack,) * parts + (full, full, jax.ShapeDtypeStruct((nb, ns) + vec.shape, F32)),
        in_specs=[hbm, hbm, vm, hbm, vm],
        out_specs=(hbm,) * parts + (vm, hbm, vm),
        scratch_shapes=[
            pltpu.VMEM((ns * rows, width), BF),
            dma((parts + 1,)),
            dma((parts, ns - 1)),
            dma((parts, ns - 1)),
            dma((6,)),
            dma((6,)),
            dma((6,)),
            dma((6,)),
            dma((ns - 1,)),
            dma((ns - 1,)),
            dma((nb - 1,)),
            dma((nb - 1,)),
        ],
        compiler_params=pltpu.CompilerParams(collective_id=6, has_side_effects=True, vmem_limit_bytes=40 * 2**20),
        cost_estimate=pl.CostEstimate(flops=40 * 10**9, bytes_accessed=12 * rows * width, transcendentals=0),
        name="collect",
    )(w1, w2, mine, cot, vec)


def home_kernel(ns, nb, summed, sums, gqkv, gout, small, stage, near, mid, far, local, s0, r0, s1, r1, s2, r2):
    depth, width = gout.shape
    share = width // ns
    me, batch, others, column = greet_all(ns, nb)
    first = [send(sums.at[to[1]], near.at[d], s1.at[d], r1.at[d], to) for d, to in enumerate(column)]
    copies = []
    for t in range(3):
        cols = pl.ds(pl.multiple_of(t * width + me * share, share), share)
        for d, to in enumerate(others):
            rows = pl.ds(pl.multiple_of((t * ns + to[0]) * depth, depth), depth)
            copies.append(send(summed.at[rows], stage.at[:, cols], s0.at[t, d], r0.at[t, d], to))
        rows = pl.ds(pl.multiple_of((t * ns + me) * depth, depth), depth)
        own = pltpu.make_async_copy(summed.at[rows], stage.at[:, cols], local.at[t])
        own.start()
        copies.append(own)
    for p in range(ns):
        rows = slice((3 * ns + p) * depth, (3 * ns + p + 1) * depth)
        gout[:, p * share : (p + 1) * share] = summed[rows, :].astype(F32)
    total = sums[batch]
    for d, one in enumerate(first):
        one.wait_recv()
        total += near[d]
    mid[...] = total
    second = [send(mid.at[to[0]], far.at[d], s2.at[d], r2.at[d], to) for d, to in enumerate(others)]
    for one in copies:
        one.wait()
    gqkv[...] = stage[...].astype(F32)
    total = mid[me]
    for d, one in enumerate(second):
        one.wait_recv()
        total += far[d]
    small[...] = total
    for one in first + second:
        one.wait_send()


def home(ns, nb, summed, sums):
    rows, share = summed.shape
    depth, width = rows // (4 * ns), ns * share
    tail = sums.shape[2:]
    vm = pl.BlockSpec(memory_space=pltpu.VMEM)
    dma = pltpu.SemaphoreType.DMA
    return pl.pallas_call(
        functools.partial(home_kernel, ns, nb),
        out_shape=(
            jax.ShapeDtypeStruct((depth, 3 * width), F32),
            jax.ShapeDtypeStruct((depth, width), F32),
            jax.ShapeDtypeStruct(tail, F32),
        ),
        in_specs=[vm, vm],
        out_specs=(vm, vm, vm),
        scratch_shapes=[
            pltpu.VMEM((depth, 3 * width), BF),
            pltpu.VMEM((nb - 1, ns) + tail, F32),
            pltpu.VMEM((ns,) + tail, F32),
            pltpu.VMEM((ns - 1,) + tail, F32),
            dma((3,)),
            dma((3, ns - 1)),
            dma((3, ns - 1)),
            dma((nb - 1,)),
            dma((nb - 1,)),
            dma((ns - 1,)),
            dma((ns - 1,)),
        ],
        compiler_params=pltpu.CompilerParams(collective_id=8, has_side_effects=True),
        cost_estimate=pl.CostEstimate(flops=5 * 10**9, bytes_accessed=4 * summed.size, transcendentals=0),
        name="home",
    )(summed, sums)


PARTS = 2


def gather_seq(value):
    return lax.all_gather(value, "seq", axis=0, tiled=True)


def scatter_seq(partial):
    return lax.psum_scatter(partial, "seq", scatter_dimension=0, tiled=True)


def scatter_batch(parts):
    flat = parts.reshape(-1, parts.shape[-1])
    return lax.psum_scatter(flat, "batch", scatter_dimension=0, tiled=True)


def own_sums(keep, give):
    count = lax.axis_size("batch")
    got = lax.ppermute(give, "batch", [(i, i ^ 1) for i in range(count)])
    return (keep.astype(F32) + got.astype(F32)).astype(BF)


def unpermute(ns, nb, gathered):
    depth = gathered.shape[1] // ns
    return gathered.reshape(nb, ns, depth, -1).transpose(1, 0, 2, 3).reshape(ns * nb * depth, -1)


def unpack_attention(ns, nb, packed):
    share = packed.shape[2]
    parts = packed.reshape(nb, 4, ns, -1, share)
    qkv = parts[:, :3].transpose(2, 0, 3, 1, 4).reshape(ns * share, 3 * share)
    return qkv, parts[:, 3].transpose(0, 2, 1, 3).reshape(share, ns * share)


def body(
    block_input,
    lengths,
    ln1_gain,
    ln1_bias,
    w_qkv,
    qv_bias,
    w_out,
    out_bias,
    ln2_gain,
    ln2_bias,
    w_fc1,
    fc1_bias,
    w_fc2,
    fc2_bias,
    out_cotangent,
):
    ns, nb = lax.axis_size("seq"), lax.axis_size("batch")
    seq = lax.axis_index("seq")
    rows, width = block_input.shape[1:]
    share = width // ns
    depth = width // (ns * nb)
    hidden = w_fc1.shape[1] // ns
    chunk = hidden // PARTS
    part = chunk // nb
    pieces = width // chunk
    planar = ns == 4 and nb == 8
    mine, cot_mine = block_input[0], out_cotangent[0]

    vectors = (ln1_gain, ln1_bias, qv_bias, out_bias, ln2_gain, ln2_bias, fc1_bias, fc2_bias)
    if planar:
        attn = spread(ns, w_qkv, w_out)
        attn, vectors = lax.optimization_barrier((attn, vectors))
        spare = jnp.zeros((1024 - 2 * depth - sum(vec.shape[0] for vec in vectors),), BF)
        block = jnp.concatenate([vectors[0], vectors[0], vectors[1], vectors[1], *vectors[2:], spare])
        block = block.astype(F32).reshape(8, 128)
        *packs, h1, cot, packed = collect(ns, nb, PARTS, w_fc1, w_fc2, mine, cot_mine, block)
        packed = packed.transpose(1, 0, 2, 3).reshape(ns * nb, 1024)
        packed = jnp.concatenate([packed[:, :depth], packed[:, 2 * depth : 3 * depth], packed[:, 4 * depth :]], 1)
    else:
        attn = lax.all_to_all(w_qkv.reshape(depth, 3, ns, share), "seq", 2, 0).transpose(2, 0, 1, 3)
        attn = jnp.concatenate([attn, w_out.reshape(depth, ns, share).transpose(1, 0, 2)[None]], 0)
        attn = attn.reshape(4 * ns * depth, share)
        vector = jnp.concatenate(vectors).astype(F32)
        packed = lax.all_gather(vector, ("seq", "batch"), axis=0, tiled=False)
    attn = lax.all_gather(attn, "batch", axis=0, tiled=True).reshape(nb, 4 * ns * depth, share)
    full, at = [], 0
    for vec in vectors:
        full.append(packed[:, at : at + vec.shape[0]].reshape(1, -1))
        at += vec.shape[0]
    gain1, shift1, qv, obias, gain2, shift2, bias1, bias2 = full
    bias1 = lax.dynamic_slice_in_dim(bias1, seq * hidden, hidden, 1).reshape(nb, PARTS, part)
    qbias = lax.dynamic_slice_in_dim(qv, seq * share, share, 1)
    vbias = lax.dynamic_slice_in_dim(qv, width + seq * share, share, 1)
    bias3 = jnp.concatenate([qbias, jnp.zeros_like(qbias), vbias], 1)

    if not planar:
        fc1_part = lax.all_to_all(w_fc1.reshape(depth, ns, hidden), "seq", 1, 0)
        fc1_part = fc1_part.reshape(ns * depth, nb, PARTS, part)
        fc2_part = w_fc2.reshape(PARTS, part, pieces, chunk)
        packs = []
        for c in range(PARTS):
            first = fc1_part[:, :, c].reshape(ns * depth, chunk)
            second = fc2_part[c].transpose(1, 0, 2).reshape(pieces * part, chunk)
            packs.append(jnp.concatenate([first, second], 0))
        h1 = (norm_stats(gather_seq(mine).astype(F32))[0] * gain1 + shift1).astype(BF)
        cot = gather_seq(cot_mine)
    wgs = [lax.all_gather(pack, "batch", axis=0, tiled=True).reshape(nb, -1, chunk) for pack in packs]

    qkv, o, h1t = attend(ns, nb, lengths, h1, attn, bias3)
    if planar:
        x1, h2 = middle(ns, nb, o, attn, mine, obias, gain2, shift2)
    else:
        wq, wout = unpack_attention(ns, nb, attn)
        a = scatter_seq(jnp.dot(o, wout, preferred_element_type=F32))
        x1 = mine.astype(F32) + (a + obias)
        h2 = gather_seq((norm_stats(x1)[0] * gain2 + shift2).astype(BF))

    *gw, g, du, gb, h2t, before = ff_chunk(ns, nb, h2, None, cot, wgs[0], bias1[:, 0].reshape(1, chunk), planar)
    gws, gs, dus, gb1 = [gw], [g], [du], [gb.reshape(nb, 1, part)]
    if planar:
        own = own_sums(*gw)
    else:
        gws = [scatter_batch(gw[0])]
    for c in range(1, PARTS):
        gw, g, du, gb, *got = ff_chunk(
            ns, nb, h2, h2t, cot, wgs[c], bias1[:, c].reshape(1, chunk), False, own if planar else None
        )
        gws.append(scatter_batch(gw))
        gs.append(g)
        dus.append(du)
        gb1.append(gb.reshape(nb, 1, part))
    cot_f = cot_mine.astype(F32)
    if planar:
        dx1, da, ggain2, gshift2, gob, got = ff_back(
            ns, nb, dus[1], wgs[1], before, x1, cot_mine, gain2, own, got[0]
        )
    else:
        dh2 = before.astype(F32) + dot_t(dus[1], unpermute(ns, nb, wgs[1][:, : ns * depth]))
        dh2 = scatter_seq(dh2)
        normed2, rstd2 = norm_stats(x1)
        ggain2 = jnp.sum(dh2 * normed2, 0)
        gshift2 = jnp.sum(dh2, 0)
        dx1 = cot_f + norm_back(dh2, normed2, rstd2, gain2)
        da_mine = dx1.astype(BF)
        gob = jnp.sum(da_mine.astype(F32), 0)
        da = gather_seq(da_mine)

    gattn, dproj, gqv = attend_back(ns, nb, lengths, h1t, da, attn, o, qkv)
    gattn = scatter_batch(gattn)
    if planar:
        gx, ggain1, gshift1, out, gw1, gw2 = finish(
            ns, nb, dproj, attn, gs, wgs, own, got, gws[1:], mine, dx1, gain1, x1, bias2
        )
    else:
        dh1 = scatter_seq(dot_t(dproj, wq))
        normed1, rstd1 = norm_stats(mine.astype(F32))
        ggain1 = jnp.sum(dh1 * normed1, 0)
        gshift1 = jnp.sum(dh1, 0)
        gx = dx1 + norm_back(dh1, normed1, rstd1, gain1)
        y = 0.0
        for g, wg in zip(gs, wgs):
            w2 = wg[:, ns * depth :].reshape(nb, pieces, part, chunk).transpose(0, 2, 1, 3).reshape(chunk, width)
            y += jnp.dot(g, w2, preferred_element_type=F32)
        out = (x1 + (scatter_seq(y) + bias2)).astype(BF)

    if not planar:
        gw1 = jnp.stack([gw[: ns * depth].reshape(ns, depth, nb, part) for gw in gws], 3)
        gw1 = lax.all_to_all(gw1, "seq", 0, 1).astype(F32).reshape(depth, ns * hidden)
        gw2 = jnp.stack([gw[ns * depth :].reshape(pieces, part, chunk) for gw in gws], 0)
        gw2 = gw2.astype(F32).transpose(0, 2, 1, 3).reshape(PARTS * part, width)
        gwqkv = gattn[: 3 * ns * depth].reshape(3, ns, depth, share)
        gwqkv = lax.all_to_all(gwqkv, "seq", 1, 2).astype(F32).transpose(1, 0, 2, 3).reshape(depth, 3 * width)
        gwo = gattn[3 * ns * depth :].reshape(ns, depth, share).astype(F32).transpose(1, 0, 2).reshape(depth, width)

    def place(part, size):
        return lax.dynamic_update_slice_in_dim(jnp.zeros((size,), F32), part, seq * part.shape[0], 0)

    gqv = gqv[0]
    gqv = jnp.concatenate([place(gqv[:share], width), place(gqv[2 * share :], width)])
    gb1 = place(jnp.stack(gb1, 1).reshape(-1), ns * hidden)
    gb2 = jnp.sum(cot_f, 0)
    sums = (ggain1, gshift1, gqv, gob, ggain2, gshift2, gb1, gb2)
    sums = jnp.concatenate([t.reshape(ns * nb, -1) for t in sums], 1)
    if planar:
        sums = jnp.pad(sums, ((0, 0), (0, 1024 - sums.shape[1]))).reshape(ns, nb, 8, 128)
        gwqkv, gwo, sums = home(ns, nb, gattn, sums.transpose(1, 0, 2, 3))
        sums = sums.reshape(-1)
    else:
        sums = lax.psum_scatter(sums, ("seq", "batch"), scatter_dimension=0, tiled=True)[0]
    small, at = [], 0
    for vec in vectors:
        small.append(sums[at : at + vec.shape[0]])
        at += vec.shape[0]
    return (
        out[None],
        gx[None],
        small[0],
        small[1],
        gwqkv,
        small[2],
        gwo,
        small[3],
        small[4],
        small[5],
        gw1,
        small[6],
        gw2,
        small[7],
    )


def solution(mesh):
    shard = P(("seq", "batch"))
    shard2 = P(("seq", "batch"), None)
    acts = P("batch", "seq", None)
    return jax.shard_map(
        body,
        mesh=mesh,
        in_specs=(acts, P("batch"), shard, shard, shard2, shard, shard2, shard, shard, shard, shard2, shard, shard2, shard, acts),
        out_specs=(acts, acts, shard, shard, shard2, shard, shard2, shard, shard, shard, shard2, shard, shard2, shard),
        check_vma=False,
    )
```

time: 636 us -> 580 us (0.912)
  waiting for transfers between devices: 57.5 us -> 18 us
  local copies, waits for them, and re-layouts: 38 us -> 22.4 us
    all_gather x2, waiting for transfers between devices: 36.5 us -> 3.3 us  [body(): lax.all_gather(pack, 'batch', axis=0, tiled=True).reshape(nb, -1, chunk)]
    reduce_scatter x3 -> x2, waiting for transfers between devices: 19.7 us -> 6.59 us  [scatter_batch(): return lax.psum_scatter(flat, 'batch', scatter_dimension=0, tiled=True)]
    pallas_call x9 -> x7, Pallas kernels: 372 us -> 363 us  [the longest x1 95.9 us: finish(): pl.pallas_call(functools.partial(finish_kernel, ns, nb, count), out_shape...]
    ppermute x0 -> x1, waiting for transfers between devices: none -> 7.36 us  [own_sums(): got = lax.ppermute(give, 'batch', [(i, i ^ 1) for i in range(count)])]
    unnamed x52 -> x67, local copies, waits for them, and re-layouts: 14.1 us -> 11 us
  transfers between devices with their start and end apart: 8 -> 6, of which waited for: 2 -> 3; matrix products, arithmetic and copies ran while one was open for 5% -> 3% of each run, Pallas kernels for 76% -> 77%
where the time goes in v3:
time: 580 us; the launch traced here: 576 us
  Pallas kernels  507 us (87%)
  local copies, waits for them, and re-layouts  22.4 us (4%)
  waiting for transfers between devices  18 us (3%)
  between operations  15.5 us (3%)
  other arithmetic  12 us (2%)
    pallas_call x1, Pallas kernels, finish(): pl.pallas_call(functools.partial(finish_kernel, ns, nb, count), out_shape...  95.9 us
    pallas_call x1, Pallas kernels, collect(): pl.pallas_call(functools.partial(collect_kernel, ns, nb, parts), out_shap...  87.1 us
    pallas_call x1, Pallas kernels, ff_back(): pl.pallas_call(functools.partial(ff_back_kernel, ns, nb), out_shape=(jax....  85.7 us
    pallas_call x1, Pallas kernels, middle(): pl.pallas_call(functools.partial(middle_kernel, ns, nb), out_shape=(jax.S...  78.8 us
    pallas_call x2, Pallas kernels, ff_chunk(): pl.pallas_call(functools.partial(ff_kernel, ns, nb, first, moving), out_s...  71.8 us
    pallas_call x1, Pallas kernels, attend_back(): pl.pallas_call(functools.partial(attend_back_kernel, ns, nb), out_shape=(...  34.3 us
    pallas_call x1, Pallas kernels, attend(): pl.pallas_call(functools.partial(attend_kernel, ns, nb), out_shape=(jax.S...  22.6 us
    pallas_call x1, Pallas kernels, home(): pl.pallas_call(functools.partial(home_kernel, ns, nb), out_shape=(jax.Sha...  15.7 us
  transfers between devices with their start and end apart: 6, of which 3 were waited for; matrix products, arithmetic and copies ran while one was open for 3% of the time, Pallas kernels for 77%

profile of v3, /device:TPU:0, one launch (start us, length us, event | category | flops | bytes accessed | tf_op | source)
XLA Modules:
  0.0 575.6 jit_solution(13550265796403289086)
XLA Ops:
  7.3 15.3 %spread_qkv.1 = bf16[1024,512]{1,0:T(8,128)(2,1)} custom-call(bf16[64,6144]{1,0:T(8,128)(2,1)} %w_qkv.1, bf16[64,2048]{1,0:T(8,128)(2,1)} %w_out.1), custom_call_target="tpu_custom_call" | custom-call | flops 5000000000 | bytes 786432 | tf_op jit(solution)/shard_map/spread_qkv/pallas_call | solution.py:903
  22.9 1.2 copy-done.4
  24.2 87.1 %collect.1 = (bf16[512,1024]{1,0:T(8,128)(2,1)}, bf16[512,1024]{1,0:T(8,128)(2,1)}, bf16[1024,2048]{1,0:T(8,128)(2,1)S(1)}, bf16[1024,2048]{1,0:T(8,128)(2,1)}, f32[8,4,8,128]{3,2,1,0:T(8,128)S(1)}) custom-call(bf16[64,8192]{1,0:T(8,128)(2,1)S(1)} %copy-done.2, bf16[256,2048]{1,0:T(8,128)(2,1)S(1)} %copy-done.3, bf16[256,2048]{1,0:T(8,128)(2,1)S(1)} %bitcast.58, ...), custom_call_target="tpu_custom_call" | custom-call | flops 40000000000 | bytes 6291456 | tf_op jit(solution)/shard_map/collect/pallas_call | solution.py:1043
  111.3 2.1 copy-done.5
  113.4 0.7 all-gather.8.cloned.1.call-update
  114.1 0.3 reduce-scatter.3.cloned.1.call-start
  115.1 0.7 fusion.1
  115.8 0.7 reshape.114.gain
  116.4 0.7 reshape.113.obias
  117.1 0.7 reshape.115.shift
  118.0 0.6 fusion.bias
  118.6 0.6 slice_bitcast_fusion.1
  119.2 22.6 %attend.1 = (bf16[1024,1536]{1,0:T(8,128)(2,1)}, bf16[1024,512]{1,0:T(8,128)(2,1)}, bf16[2048,1024]{1,0:T(8,128)(2,1)}) custom-call(s32[1]{0:T(128)S(6)} %copy.51.length, bf16[1024,2048]{1,0:T(8,128)(2,1)} %copy-done.5, bf16[8,1024,512]{2,1,0:T(8,128)(2,1)} %bitcast.78, f32[1,1536]{1,0:T(1,128)} %fusion.bias), custom_call_target="tpu_custom_call" | custom-call | flops 6442450944 | bytes 8388608 | tf_op jit(solution)/shard_map/attend/pallas_call | solution.py:137
  141.8 78.8 %project_out.1 = (f32[256,2048]{1,0:T(8,128)}, bf16[1024,2048]{1,0:T(8,128)(2,1)}) custom-call(bf16[1024,512]{1,0:T(8,128)(2,1)} %get-tuple-element.74.o, bf16[8,1024,512]{2,1,0:T(8,128)(2,1)} %bitcast.79, bf16[256,2048]{1,0:T(8,128)(2,1)} %bitcast.56, f32[1,2048]{1,0:T(1,128)} %reshape.113.obias, f32[1,2048]{1,0:T(1,128)} %reshape.114.gain, ...), custom_call_target="tpu_custom_call" | custom-call | flops 40000000000 | bytes 25165824 | tf_op jit(solution)/shard_map/project_out/pallas_call | solution.py:634
  220.7 37.5 %ff_first.1 = (bf16[4,512,1024]{2,1,0:T(8,128)(2,1)}, bf16[4,512,1024]{2,1,0:T(8,128)(2,1)}, bf16[1024,1024]{1,0:T(8,128)(2,1)}, bf16[1024,1024]{1,0:T(8,128)(2,...) custom-call(bf16[1024,2048]{1,0:T(8,128)(2,1)} %get-tuple-element.75.refs_0_, ...), custom_call_target="tpu_custom_call" | custom-call | flops 40000000000 | bytes 16777216 | tf_op jit(solution)/shard_map/ff_first/pallas_call | solution.py:480
  258.3 7.4 %collective-permute-done = bf16[4,512,1024]{2,1,0:T(8,128)(2,1)S(1)} collective-permute-done((bf16[4,512,1024]{2,1,0:T(8,128)(2,1)}, bf16[4,512,1024]{2,1,0:T(8,128)(2,1)S(1)}, u32[]{:S(2)}, u32[]{:S(2)}) %collective-permute-start) | collective-permute-done | bytes 4194336 | tf_op jit(solution)/shard_map/ppermute | solution.py:1156
  265.6 6.4 %add_convert_fusion.refs_5_.own.refs_6_ = bf16[4,512,1024]{2,1,0:T(8,128)(2,1)} fusion(bf16[4,512,1024]{2,1,0:T(8,128)(2,1)S(1)} %collective-permute-done, bf16[4,512,1024]{2,1,0:T(8,128)(2,1)} %get-tuple-element.80), kind=kLoop, calls=%fused_computation | loop fusion | flops 8388608 | bytes 12582912 | tf_op jit(solution)/shard_map/convert_element_type | solution.py:1157
  272.1 3.3 all-gather.8.cloned.1.call-done
  275.4 34.3 %ff_chunk.1 = (bf16[8,512,1024]{2,1,0:T(8,128)(2,1)}, bf16[1024,1024]{1,0:T(8,128)(2,1)}, bf16[1024,1024]{1,0:T(8,128)(2,1)}, f32[1,1024]{1,0:T(1,128)}, bf16[2,512,1024]{2,1,0:T(8,128)(2,1)}) custom-call(bf16[1024,2048]{1,0:T(8,128)(2,1)} %get-tuple-element.75.refs_0_, bf16[2048,1024]{1,0:T(8,128)(2,1)} %get-tuple-element.78.refs_1_, ...), custom_call_target="tpu_custom_call" | custom-call | flops 40000000000 | bytes 16777216 | tf_op jit(solution)/shard_map/ff_chunk/pallas_call | solution.py:480
  309.8 85.7 %ff_back.1 = (f32[256,2048]{1,0:T(8,128)}, bf16[1024,2048]{1,0:T(8,128)(2,1)}, f32[1,2048]{1,0:T(1,128)}, f32[1,2048]{1,0:T(1,128)}, f32[1,2048]{1,0:T(1,128)}, /*index=5*/bf16[2,512,1024]{2,1,0:T(8,128)(2,1)}) custom-call(bf16[1024,1024]{1,0:T(8,128)(2,1)} %get-tuple-element.82.du, bf16[8,512,1024]{2,1,0:T(8,128)(2,1)} %bitcast.85, ...), custom_call_target="tpu_custom_call" | custom-call | flops 40000000000 | bytes 25165824 | tf_op jit(solution)/shard_map/ff_back/pallas_call | solution.py:686
  395.5 34.3 %attend_back.1 = (bf16[8,1024,512]{2,1,0:T(8,128)(2,1)}, bf16[1024,1536]{1,0:T(8,128)(2,1)}, f32[1,1536]{1,0:T(1,128)}) custom-call(s32[1]{0:T(128)S(6)} %copy.51.length, bf16[2048,1024]{1,0:T(8,128)(2,1)} %get-tuple-element.73.h1t, bf16[1024,2048]{1,0:T(8,128)(2,1)} %get-tuple-element.86.da, bf16[8,1024,512]{2,1,0:T(8,128)(2,1)} %bitcast.80, ...), custom_call_target="tpu_custom_call" | custom-call | flops 40000000000 | bytes 12582912 | tf_op jit(solution)/shard_map/attend_back/pallas_call | solution.py:237
  429.9 0.6 copy-done.13
  430.5 0.7 reshape.121.refs_11_
  431.2 0.7 reshape.122.refs_13_
  431.9 0.2 convert_reduce_fusion
  432.2 0.3 dynamic_update_slice.11
  432.5 0.5 broadcast.22
  433.0 0.7 reduce.17
  433.8 0.7 reduce.18
  434.5 0.7 reduce.19
  435.3 0.3 dynamic_update_slice.9
  435.5 0.3 dynamic_update_slice.10
  435.8 95.9 %finish.1 = (f32[256,2048]{1,0:T(8,128)}, f32[1,2048]{1,0:T(1,128)}, f32[1,2048]{1,0:T(1,128)}, bf16[256,2048]{1,0:T(8,128)(2,1)}, f32[64,8192]{1,0:T(8,128)}, /*index=5*/f32[256,2048]{1,0:T(8,128)}) custom-call(bf16[1024,1536]{1,0:T(8,128)(2,1)} %get-tuple-element.88.refs_0_, bf16[8,1024,512]{2,1,0:T(8,128)(2,1)} %bitcast.81, ...), custom_call_target="tpu_custom_call" | custom-call | flops 40000000000 | bytes 12582912 | tf_op jit(solution)/shard_map/finish/pallas_call | solution.py:830
  531.8 1.4 reduce.15
  533.2 1.4 reduce.16
  534.6 0.1 concatenate.22
  534.8 0.7 copy_bitcast_fusion.2.sums
  535.4 6.6 %reduce-scatter.5.cloned.1.call-done.summed = bf16[1024,512]{1,0:T(8,128)(2,1)} async-done(((bf16[8192,512]{1,0:T(8,128)(2,1)}), bf16[1024,512]{1,0:T(8,128)(2,1)}) %reduce-scatter.5.cloned.1.call-update) | async-done | bytes 1048592 | tf_op jit(solution)/shard_map/reduce_scatter | solution.py:1151
  542.0 15.7 %home.1 = (f32[64,6144]{1,0:T(8,128)}, f32[64,2048]{1,0:T(8,128)}, f32[8,128]{1,0:T(8,128)}) custom-call(bf16[1024,512]{1,0:T(8,128)(2,1)} %reduce-scatter.5.cloned.1.call-done.summed, f32[8,4,8,128]{3,2,1,0:T(8,128)} %copy_bitcast_fusion.2.sums), custom_call_target="tpu_custom_call" | custom-call | flops 5000000000 | bytes 2097152 | tf_op jit(solution)/shard_map/home/pallas_call | solution.py:1110
  557.7 1.5 fusion.3
  559.2 1.3 slice.93
  560.5 1.2 slice_bitcast_fusion.3
  561.7 1.0 copy.52
  562.7 1.3 copy.53
  564.0 1.1 copy.54
  565.2 0.8 copy.55
  566.0 1.3 copy.56
  567.3 1.3 copy.57
  (91 shorter events, 1.2 us)
Async XLA Ops:
  7.2 15.6 %copy-start.20 = (bf16[64]{0:T(256)(128)(2,1)S(1)}, bf16[64]{0:T(256)(128)(2,1)}, u32[]{:S(2)}) copy-start(bf16[64]{0:T(256)(128)(2,1)} %param.17) | copy-start | bytes 388
  7.2 15.6 %copy-start.21 = (bf16[64]{0:T(256)(128)(2,1)S(1)}, bf16[64]{0:T(256)(128)(2,1)}, u32[]{:S(2)}) copy-start(bf16[64]{0:T(256)(128)(2,1)} %param.18) | copy-start | bytes 388
  7.2 15.6 %copy-start.22 = (bf16[128]{0:T(256)(128)(2,1)S(1)}, bf16[128]{0:T(256)(128)(2,1)}, u32[]{:S(2)}) copy-start(bf16[128]{0:T(256)(128)(2,1)} %param.20) | copy-start | bytes 772
  7.2 15.6 %copy-start.23 = (bf16[64]{0:T(256)(128)(2,1)S(1)}, bf16[64]{0:T(256)(128)(2,1)}, u32[]{:S(2)}) copy-start(bf16[64]{0:T(256)(128)(2,1)} %param.22) | copy-start | bytes 388
  7.2 15.6 %copy-start.24 = (bf16[64]{0:T(256)(128)(2,1)S(1)}, bf16[64]{0:T(256)(128)(2,1)}, u32[]{:S(2)}) copy-start(bf16[64]{0:T(256)(128)(2,1)} %param.23) | copy-start | bytes 388
  7.2 15.6 %copy-start.25 = (bf16[64]{0:T(256)(128)(2,1)S(1)}, bf16[64]{0:T(256)(128)(2,1)}, u32[]{:S(2)}) copy-start(bf16[64]{0:T(256)(128)(2,1)} %param.24) | copy-start | bytes 388
  7.2 15.6 %copy-start.26 = (bf16[256]{0:T(256)(128)(2,1)S(1)}, bf16[256]{0:T(256)(128)(2,1)}, u32[]{:S(2)}) copy-start(bf16[256]{0:T(256)(128)(2,1)} %param.26) | copy-start | bytes 1540
  7.3 15.6 %copy-start.27 = (bf16[64]{0:T(256)(128)(2,1)S(1)}, bf16[64]{0:T(256)(128)(2,1)}, u32[]{:S(2)}) copy-start(bf16[64]{0:T(256)(128)(2,1)} %param.28) | copy-start | bytes 388
  7.3 15.7 %copy-start = (bf16[1,256,2048]{2,1,0:T(8,128)(2,1)S(1)}, bf16[1,256,2048]{2,1,0:T(8,128)(2,1)}, u32[]{:S(2)}) copy-start(bf16[1,256,2048]{2,1,0:T(8,128)(2,1)} %param.29) | copy-start | bytes 3145732
  7.3 15.6 %copy-start.2 = (bf16[64,8192]{1,0:T(8,128)(2,1)S(1)}, bf16[64,8192]{1,0:T(8,128)(2,1)}, u32[]{:S(2)}) copy-start(bf16[64,8192]{1,0:T(8,128)(2,1)} %w1.1) | copy-start | bytes 3145732
  7.3 15.6 %copy-start.3 = (bf16[256,2048]{1,0:T(8,128)(2,1)S(1)}, bf16[256,2048]{1,0:T(8,128)(2,1)}, u32[]{:S(2)}) copy-start(bf16[256,2048]{1,0:T(8,128)(2,1)} %w2.1) | copy-start | bytes 3145732
  7.3 111.9 %all-gather.4.cloned.1.call-start = ((), (), s32[]{:S(2)}) async-start(), calls=%async_computation.2 | async-start | bytes 9437184 | tf_op jit(solution)/shard_map/all_gather | solution.py:1217
  22.7 198.0 %all-gather.6.cloned.1.call-start = ((), (), s32[]{:S(2)}) async-start(), calls=%async_computation.3 | async-start | bytes 9437184 | tf_op jit(solution)/shard_map/all_gather | solution.py:1239
  22.9 1.2 copy-start.4
  111.3 2.1 copy-start.5
  113.4 162.0 %all-gather.8.cloned.1.call-start = ((), (), s32[]{:S(2)}) async-start(), calls=%async_computation.4 | async-start | bytes 9437184 | tf_op jit(solution)/shard_map/all_gather | solution.py:1239
  114.1 321.7 %reduce-scatter.3.cloned.1.call-start = ((), (), s32[]{:S(2)}) async-start(), calls=%async_computation.5 | async-start | bytes 9437184 | tf_op jit(solution)/shard_map/reduce_scatter | solution.py:1151
  258.2 7.4 %collective-permute-start = (bf16[4,512,1024]{2,1,0:T(8,128)(2,1)}, bf16[4,512,1024]{2,1,0:T(8,128)(2,1)S(1)}, u32[]{:S(2)}, u32[]{:S(2)}) collective-permute-start(bf16[4,512,1024]{2,1,0:T(8,128)(2,1)} %get-tuple-element.81), channel_id=1, source_target_pairs={{0,1},{1,0},{2,3},{3,2},{4,5},{5,4},{6,7},{7,6},{8,9},{9,8},{10,11... | collective-permute-start | bytes 12582920 | tf_op jit(solution)/shard_map/ppermute | solution.py:1156
  309.7 232.3 %reduce-scatter.5.cloned.1.call-start = ((), (), s32[]{:S(2)}) async-start(), calls=%async_computation.6 | async-start | bytes 9437184 | tf_op jit(solution)/shard_map/reduce_scatter | solution.py:1151
  429.8 0.7 copy-start.13
  429.8 1.4 copy-start.12
  429.8 2.1 copy-start.1
  429.8 2.3 copy-start.17
  429.8 2.3 copy-start.18
  429.9 3.2 copy-start.16
  429.9 3.9 copy-start.15
  429.9 4.6 copy-start.14
  429.9 5.4 copy-start.19
  535.4 26.3 %copy-start.10 = (bf16[256,2048]{1,0:T(8,128)(2,1)S(1)}, bf16[256,2048]{1,0:T(8,128)(2,1)}, u32[]{:S(2)}) copy-start(bf16[256,2048]{1,0:T(8,128)(2,1)} %get-tuple-element.94) | copy-start | bytes 3145732
  535.4 27.3 %copy-start.8 = (f32[256,2048]{1,0:T(8,128)S(1)}, f32[256,2048]{1,0:T(8,128)}, u32[]{:S(2)}) copy-start(f32[256,2048]{1,0:T(8,128)} %get-tuple-element.95) | copy-start | bytes 6291460
  557.7 6.3 %copy-start.9 = (f32[64,6144]{1,0:T(8,128)S(1)}, f32[64,6144]{1,0:T(8,128)}, u32[]{:S(2)}) copy-start(f32[64,6144]{1,0:T(8,128)} %get-tuple-element.145) | copy-start | bytes 4718596
  561.7 3.4 copy-start.11
  562.7 3.3 copy-start.7
  564.0 3.3 copy-start.6
Sparse Core Ops, SparseCore 0:
  22.8 84.7 all-gather.3
  113.5 79.6 all-gather.5
  194.7 80.5 all-gather.7
  309.9 112.1 reduce-scatter.2
  430.0 111.9 reduce-scatter.4

commit v4 on v3

--- a/solution.py
+++ b/solution.py
@@ -30,6 +30,83 @@
     )
 
 
+MESH = pl.DeviceIdType.MESH
+
+
+def send(src, dst, sends, recvs, to):
+    one = pltpu.make_async_remote_copy(
+        src_ref=src, dst_ref=dst, send_sem=sends, recv_sem=recvs, device_id=to, device_id_type=MESH
+    )
+    one.start()
+    return one
+
+
+class Line:
+    def __init__(self, step, own, prior, got, held, load, sends, recvs):
+        self.step, self.own, self.prior, self.got, self.held = step, own, prior, got, held
+        self.load, self.sends, self.recvs = load, sends, recvs
+        self.last = own.shape[0] - 1
+        self.seq, batch = lax.axis_index("seq"), lax.axis_index("batch")
+        self.chip, self.core = batch // 2, lax.rem(batch, 2)
+
+    def ready(self):
+        self.got[...] = jnp.zeros_like(self.got)
+        ahead = self.last - self.step
+        wanted = jnp.minimum(self.chip + ahead, self.last), jnp.maximum(self.chip - ahead, 0)
+        for way, chunk in enumerate(wanted):
+            pltpu.make_async_copy(self.own.at[chunk], self.held.at[way], self.load.at[way]).start()
+
+    def neighbours(self):
+        count = self.last + 1
+        return [(self.seq, 2 * lax.rem(self.chip + d, count) + self.core) for d in (1, count - 1)]
+
+    def copy(self, way):
+        to = jnp.minimum(self.chip + 1, self.last) if way == 0 else jnp.maximum(self.chip - 1, 0)
+        return pltpu.make_async_remote_copy(
+            src_ref=self.held.at[way],
+            dst_ref=self.got.at[way],
+            send_sem=self.sends.at[way],
+            recv_sem=self.recvs.at[way],
+            device_id=(self.seq, 2 * to + self.core),
+            device_id_type=MESH,
+        )
+
+    def roles(self):
+        chip, last, step = self.chip, self.last, self.step
+        gives = chip <= step, chip >= last - step
+        takes = (chip >= 1) & (chip <= step + 1), (chip <= last - 1) & (chip >= last - 1 - step)
+        return gives, takes
+
+    def go(self):
+        for way in range(2):
+            here = self.held.at[way]
+            pltpu.make_async_copy(here, here, self.load.at[way]).wait()
+            if self.prior is not None:
+                total = self.held[way].astype(F32) + self.prior[way].astype(F32)
+                self.held[way] = total.astype(BF)
+
+            @pl.when(self.roles()[0][way])
+            def _():
+                self.copy(way).start()
+
+    def stop(self):
+        gives, takes = self.roles()
+        for way in range(2):
+
+            @pl.when(takes[way])
+            def _():
+                self.copy(way).wait_recv()
+
+            @pl.when(gives[way])
+            def _():
+                self.copy(way).wait_send()
+
+
+def line_scratch(rows, width):
+    dma = pltpu.SemaphoreType.DMA
+    return [pltpu.VMEM((2, rows, width), BF), dma((2,)), dma((2,)), dma((2,))]
+
+
 def dot_t(left, right):
     return lax.dot_general(left, right, (((1,), (1,)), ((), ())), preferred_element_type=F32)
 
@@ -51,7 +128,7 @@
 
 def load_attention(ns, nb, packed, w, sem):
     share = packed.shape[2]
-    depth = packed.shape[1] // (4 * ns)
+    depth = packed.shape[1] // (3 * ns)
 
     def one(k, carry):
         s, b = k // nb, lax.rem(k, nb)
@@ -66,15 +143,15 @@
     lax.fori_loop(0, ns * nb, one, 0)
 
 
-def load_out(ns, nb, packed, wout, sem):
-    share = packed.shape[2]
-    depth = packed.shape[1] // (4 * ns)
-
-    def one(b, carry):
-        for p in range(ns):
+def load_second(nb, packed, w, sem):
+    chunk, width = w.shape
+    part, pieces, base = chunk // nb, width // chunk, width // nb
+
+    def one(k, carry):
+        for p in range(pieces):
             pltpu.make_async_copy(
-                packed.at[b, (3 * ns + p) * depth : (3 * ns + p + 1) * depth, :],
-                wout.at[pl.ds(b * depth, depth), p * share : (p + 1) * share],
+                packed.at[k, pl.ds(base + p * part, part), :],
+                w.at[pl.ds(k * part, part), p * chunk : (p + 1) * chunk],
                 sem,
             ).start()
         return carry
@@ -145,22 +222,45 @@
         out_specs=(vm, vm, vm),
         scratch_shapes=[pltpu.VMEM((width, 3 * share), BF), pltpu.SemaphoreType.DMA],
         compiler_params=pltpu.CompilerParams(vmem_limit_bytes=56 * 2**20),
-        cost_estimate=pl.CostEstimate(
-            flops=6 * tokens * width * share, bytes_accessed=2 * wq.size, transcendentals=tokens * 512 * share // 128
-        ),
+        cost_estimate=pl.CostEstimate(flops=10**6, bytes_accessed=10**4, transcendentals=0),
         name="attend",
     )(lengths, h1, wq, bias)
 
 
-def attend_back_kernel(ns, nb, length, h1t, da, wq, o, qkv, packed, dproj, gqv, do, gw, gwo, wout, acc_k, acc_v, sems):
+def attend_back_kernel(ns, nb, moving, length, h1t, da, wout, o, qkv, *refs):
+    line = None
+    if moving:
+        own, prior, g0, g1, wg0, wg1, packed, dproj, gqv, sums, branch_sum, do, gw, gwo, acc_k, acc_v, sems, *rest = refs
+        out, via, from_x, from_y, s1, r1, got, *rest = rest
+        line = Line(2, own, prior, got, *rest)
+    else:
+        packed, dproj, gqv, do, gw, gwo, acc_k, acc_v, sems = refs
     width, tokens = h1t.shape
     share = o.shape[1]
     rows = tokens // ns
     depth = width // (ns * nb)
     scale = HEAD_DIM ** (-0.5)
     limit = length[0]
-    load_out(ns, nb, wq, wout, sems.at[2])
-    pltpu.make_async_copy(wout, wout, sems.at[2]).wait()
+    steps = None
+    if moving:
+        chunk = g0.shape[1]
+        halves = gw.at[:chunk], gw.at[chunk:]
+        for k, wg in enumerate((wg0, wg1)):
+            load_second(nb, wg, halves[k], sems.at[2 + k])
+        line.ready()
+        place = greet(line.neighbours())
+        line.go()
+
+        def branch(block):
+            at = pl.ds(pl.multiple_of(block * rows, rows), rows // 2)
+            total = jnp.dot(g0[at, :], halves[0][...], preferred_element_type=F32)
+            return total + jnp.dot(g1[at, :], halves[1][...], preferred_element_type=F32)
+
+        for k in range(2):
+            pltpu.make_async_copy(halves[k], halves[k], sems.at[2 + k]).wait()
+        steps = scatter_steps(branch, place, (out, via, from_x, from_y), s1, r1)
+        for _ in range(3):
+            next(steps)
     for r in range(0, tokens, 256):
         do[r : r + 256, :] = dot_t(da[r : r + 256, :], wout[...]).astype(BF)
     ot = o[...].T
@@ -177,6 +277,8 @@
         return carry
 
     lax.fori_loop(0, nb, store_out, 0)
+    if moving:
+        next(steps)
 
     def head(h, carry):
         at = h * HEAD_DIM
@@ -201,6 +303,11 @@
         return carry
 
     lax.fori_loop(0, share // HEAD_DIM, head, 0)
+    if moving:
+        next(steps)
+        fourth = rows // 4
+        for part, total in enumerate(next(steps)):
+            branch_sum[part * fourth : (part + 1) * fourth, :] = total
     wide = min(512, 3 * share)
 
     def weights(j, carry):
@@ -225,142 +332,223 @@
         return c
 
     lax.fori_loop(0, ns * nb, store, 0)
-    pltpu.make_async_copy(gw, gw, sems.at[1]).wait()
+    if moving:
+        line.stop()
+        mine = pltpu.make_async_copy(own.at[line.chip], line.held.at[0], sems.at[2])
+        mine.start()
+        mine.wait()
+        sums[...] = (line.held[0].astype(F32) + got[0].astype(F32) + got[1].astype(F32)).astype(BF)
+    stored = gw.at[:, : 3 * share]
+    pltpu.make_async_copy(stored, stored, sems.at[1]).wait()
     pltpu.make_async_copy(gwo, gwo, sems.at[0]).wait()
 
 
-def attend_back(ns, nb, lengths, h1t, da, wq, o, qkv):
+def attend_back(ns, nb, lengths, h1t, da, wout, o, qkv, *more):
     width, tokens = h1t.shape
     share = o.shape[1]
+    rows = tokens // ns
     vm = pl.BlockSpec(memory_space=pltpu.VMEM)
     hbm = pl.BlockSpec(memory_space=pl.ANY)
+    moving = len(more) > 0
+    extra, scratch = (), []
+    if moving:
+        prior = more[1]
+        extra = jax.ShapeDtypeStruct(prior.shape[1:], BF), jax.ShapeDtypeStruct((rows // 2, width), F32)
+        scratch = scatter_scratch(rows // 2, width) + [pltpu.VMEM(prior.shape, BF)] + line_scratch(*prior.shape[1:])
     return pl.pallas_call(
-        functools.partial(attend_back_kernel, ns, nb),
+        functools.partial(attend_back_kernel, ns, nb, moving),
         out_shape=(
             jax.ShapeDtypeStruct((nb, 4 * width // nb, share), BF),
             jax.ShapeDtypeStruct((tokens, 3 * share), BF),
             jax.ShapeDtypeStruct((1, 3 * share), F32),
-        ),
-        in_specs=[pl.BlockSpec(memory_space=pltpu.SMEM), vm, vm, hbm, vm, vm],
-        out_specs=(hbm, vm, vm),
+        )
+        + extra,
+        in_specs=[pl.BlockSpec(memory_space=pltpu.SMEM), vm, vm, vm, vm, vm] + [hbm, vm, vm, vm, hbm, hbm][: len(more)],
+        out_specs=(hbm, vm, vm) + (vm,) * len(extra),
         scratch_shapes=[
             pltpu.VMEM((tokens, share), BF),
-            pltpu.VMEM((width, 3 * share), BF),
-            pltpu.VMEM((share, width), BF),
+            pltpu.VMEM((width, width if moving else 3 * share), BF),
             pltpu.VMEM((share, width), BF),
             pltpu.VMEM((tokens, HEAD_DIM), F32),
             pltpu.VMEM((tokens, HEAD_DIM), F32),
-            pltpu.SemaphoreType.DMA((3,)),
-        ],
-        compiler_params=pltpu.CompilerParams(vmem_limit_bytes=56 * 2**20),
+            pltpu.SemaphoreType.DMA((4,)),
+        ]
+        + scratch,
+        compiler_params=pltpu.CompilerParams(
+            collective_id=9 if moving else None, has_side_effects=moving, vmem_limit_bytes=60 * 2**20
+        ),
         cost_estimate=pl.CostEstimate(
             flops=40 * 10**9, bytes_accessed=12 * width * share, transcendentals=tokens * 512 * share // 128
         ),
         name="attend_back",
-    )(lengths, h1t, da, wq, o, qkv)
-
-
-MESH = pl.DeviceIdType.MESH
-
-
-def send(src, dst, sends, recvs, to):
-    one = pltpu.make_async_remote_copy(
-        src_ref=src, dst_ref=dst, send_sem=sends, recv_sem=recvs, device_id=to, device_id_type=MESH
-    )
-    one.start()
-    return one
-
-
-class Line:
-    def __init__(self, step, own, prior, got, held, load, sends, recvs):
-        self.step, self.own, self.prior, self.got, self.held = step, own, prior, got, held
-        self.load, self.sends, self.recvs = load, sends, recvs
-        self.last = own.shape[0] - 1
-        self.seq, batch = lax.axis_index("seq"), lax.axis_index("batch")
-        self.chip, self.core = batch // 2, lax.rem(batch, 2)
-
-    def ready(self):
-        self.got[...] = jnp.zeros_like(self.got)
-        ahead = self.last - self.step
-        wanted = jnp.minimum(self.chip + ahead, self.last), jnp.maximum(self.chip - ahead, 0)
-        for way, chunk in enumerate(wanted):
-            pltpu.make_async_copy(self.own.at[chunk], self.held.at[way], self.load.at[way]).start()
-
-    def neighbours(self):
-        count = self.last + 1
-        return [(self.seq, 2 * lax.rem(self.chip + d, count) + self.core) for d in (1, count - 1)]
-
-    def copy(self, way):
-        to = jnp.minimum(self.chip + 1, self.last) if way == 0 else jnp.maximum(self.chip - 1, 0)
+    )(lengths, h1t, da, wout, o, qkv, *more)
+
+
+def slopes(u, dg):
+    sq = u * u
+    th = jnp.tanh(ROOT * u * (1.0 + 0.044715 * sq))
+    cdf = 0.5 * (1.0 + th)
+    slope = cdf + 0.5 * u * (1.0 - th * th) * (ROOT * (1.0 + 3.0 * 0.044715 * sq))
+    return (u * cdf).astype(BF), (dg * slope).astype(BF)
+
+
+def ff_first_kernel(ns, nb, h2, cot, wg, bias, own, g_out, du_out, gb, h2t, dh2, w1, w2, gw1, gw2, near2, near1, *sems):
+    load, to2, from2, to1, from1 = sems
+    tokens, width = h2.shape
+    chunk = g_out.shape[1]
+    depth = width // (ns * nb)
+    part = chunk // nb
+    pieces = width // chunk
+    half = ns * depth
+    chips = nb // 2
+    tile = min(512, chunk)
+    step = min(256, tokens)
+    seq, batch = lax.axis_index("seq"), lax.axis_index("batch")
+    chip, core = batch // 2, lax.rem(batch, 2)
+    twin = (seq, 2 * chip + 1 - core)
+    load_rows(ns, nb, depth, wg, w1, load.at[0])
+
+    def load2(k, carry):
+        for p in range(pieces):
+            pltpu.make_async_copy(
+                wg.at[k, pl.ds(half + p * part, part), :],
+                w2.at[pl.ds(k * part, part), p * chunk : (p + 1) * chunk],
+                load.at[1],
+            ).start()
+        return carry
+
+    lax.fori_loop(0, nb, load2, 0)
+    barrier = pltpu.get_barrier_semaphore()
+    pl.semaphore_signal(barrier, inc=1, device_id=twin, device_id_type=MESH)
+    for r in range(0, tokens, step):
+        h2t[:, r : r + step] = h2[r : r + step, :].T
+    pltpu.make_async_copy(w1, w1, load.at[0]).wait()
+    pltpu.make_async_copy(w2, w2, load.at[1]).wait()
+
+    def one_tile(j, carry):
+        cols = pl.ds(pl.multiple_of(j * tile, tile), tile)
+        total = jnp.zeros((1, tile), F32)
+        for r in range(0, tokens, step):
+            rows = slice(r, r + step)
+            u = jnp.dot(h2[rows, :], w1[:, cols], preferred_element_type=F32) + bias[:, cols]
+            g, du = slopes(u, dot_t(cot[rows, :], w2[cols, :]))
+            g_out[rows, cols] = g
+            du_out[rows, cols] = du
+            total += jnp.sum(du.astype(F32), 0, keepdims=True)
+        gb[:, cols] = total
+        return carry
+
+    lax.fori_loop(0, chunk // tile, one_tile, 0)
+
+    def second(j, carry):
+        cols = pl.ds(pl.multiple_of(j * tile, tile), tile)
+        gt = g_out[:, cols].T
+        for r in range(0, width, 512):
+            gw2[cols, r : r + 512] = jnp.dot(gt, cot[:, r : r + 512], preferred_element_type=F32).astype(BF)
+        return carry
+
+    lax.fori_loop(0, chunk // tile, second, 0)
+    pl.semaphore_wait(barrier, 1)
+
+    def rows2(c, kept):
+        return pl.ds(pl.multiple_of((2 * c + (core if kept else 1 - core)) * part, part), part)
+
+    def rows1(c, s, kept):
+        return pl.ds(pl.multiple_of((s * nb + 2 * c + (core if kept else 1 - core)) * depth, depth), depth)
+
+    for c in range(chips):
+        for p in range(pieces):
+            span = slice(p * part, (p + 1) * part)
+            send(gw2.at[rows2(c, False), p * chunk : (p + 1) * chunk], near2.at[c, span], to2, from2, twin)
+
+    def first(j, carry):
+        cols = pl.ds(pl.multiple_of(j * tile, tile), tile)
+        for r in range(0, width, 512):
+            gw1[r : r + 512, cols] = jnp.dot(
+                h2t[r : r + 512, :], du_out[:, cols], preferred_element_type=F32
+            ).astype(BF)
+        return carry
+
+    lax.fori_loop(0, chunk // tile, first, 0)
+    for c in range(chips):
+        for s in range(ns):
+            send(gw1.at[rows1(c, s, False)], near1.at[c, s * depth : (s + 1) * depth], to1, from1, twin)
+
+    def whole(near, send_sem, recv_sem):
         return pltpu.make_async_remote_copy(
-            src_ref=self.held.at[way],
-            dst_ref=self.got.at[way],
-            send_sem=self.sends.at[way],
-            recv_sem=self.recvs.at[way],
-            device_id=(self.seq, 2 * to + self.core),
-            device_id_type=MESH,
+            src_ref=near, dst_ref=near, send_sem=send_sem, recv_sem=recv_sem, device_id=twin, device_id_type=MESH
         )
 
-    def roles(self):
-        chip, last, step = self.chip, self.last, self.step
-        gives = chip <= step, chip >= last - step
-        takes = (chip >= 1) & (chip <= step + 1), (chip <= last - 1) & (chip >= last - 1 - step)
-        return gives, takes
-
-    def go(self):
-        for way in range(2):
-            here = self.held.at[way]
-            pltpu.make_async_copy(here, here, self.load.at[way]).wait()
-            if self.prior is not None:
-                total = self.held[way].astype(F32) + self.prior[way].astype(F32)
-                self.held[way] = total.astype(BF)
-
-            @pl.when(self.roles()[0][way])
-            def _():
-                self.copy(way).start()
-
-    def stop(self):
-        gives, takes = self.roles()
-        for way in range(2):
-
-            @pl.when(takes[way])
-            def _():
-                self.copy(way).wait_recv()
-
-            @pl.when(gives[way])
-            def _():
-                self.copy(way).wait_send()
-
-
-def line_scratch(rows, width):
+    def back(k, carry):
+        rows = pl.ds(pl.multiple_of(k * step, step), step)
+        for c in range(0, width, 512):
+            dh2[rows, c : c + 512] = dot_t(du_out[rows, :], w1[c : c + 512, :]).astype(BF)
+        return carry
+
+    lax.fori_loop(0, tokens // step, back, 0)
+    whole(near2, to2, from2).wait_recv()
+    for c in range(chips):
+        for p in range(pieces):
+            mine = gw2[rows2(c, True), p * chunk : (p + 1) * chunk]
+            total = mine.astype(F32) + near2[c, p * part : (p + 1) * part].astype(F32)
+            own[c, half + p * part : half + (p + 1) * part] = total.astype(BF)
+    whole(near1, to1, from1).wait_recv()
+    for c in range(chips):
+        for s in range(ns):
+            total = gw1[rows1(c, s, True), :].astype(F32) + near1[c, s * depth : (s + 1) * depth].astype(F32)
+            own[c, s * depth : (s + 1) * depth] = total.astype(BF)
+    whole(near2, to2, from2).wait_send()
+    whole(near1, to1, from1).wait_send()
+
+
+def ff_first(ns, nb, h2, cot, wg, bias):
+    tokens, width = h2.shape
+    chunk = wg.shape[2]
+    half = width // nb
+    vm = pl.BlockSpec(memory_space=pltpu.VMEM)
     dma = pltpu.SemaphoreType.DMA
-    return [pltpu.VMEM((2, rows, width), BF), dma((2,)), dma((2,)), dma((2,))]
+    inner = jax.ShapeDtypeStruct((tokens, chunk), BF)
+    near = pltpu.VMEM((nb // 2, half, chunk), BF)
+    return pl.pallas_call(
+        functools.partial(ff_first_kernel, ns, nb),
+        out_shape=(
+            jax.ShapeDtypeStruct((nb // 2, 2 * half, chunk), BF),
+            inner,
+            inner,
+            jax.ShapeDtypeStruct((1, chunk), F32),
+            jax.ShapeDtypeStruct((width, tokens), BF),
+            jax.ShapeDtypeStruct((tokens, width), BF),
+        ),
+        in_specs=[vm, vm, pl.BlockSpec(memory_space=pl.ANY), vm],
+        out_specs=(vm,) * 6,
+        scratch_shapes=[
+            pltpu.VMEM((width, chunk), BF),
+            pltpu.VMEM((chunk, width), BF),
+            pltpu.VMEM((width, chunk), BF),
+            pltpu.VMEM((chunk, width), BF),
+            near,
+            near,
+            dma((2,)),
+            dma,
+            dma,
+            dma,
+            dma,
+        ],
+        compiler_params=pltpu.CompilerParams(collective_id=7, has_side_effects=True, vmem_limit_bytes=60 * 2**20),
+        cost_estimate=pl.CostEstimate(flops=40 * 10**9, bytes_accessed=8 * wg.size, transcendentals=tokens * chunk),
+        name="ff_first",
+    )(h2, cot, wg, bias)
 
 
 def ff_kernel(ns, nb, first, moving, *refs):
     line = None
     if first:
-        h2, cot, wg, bias, *gwg, g_out, du_out, gb, h2t, dh2, w1, w2, gw1, gw2, sems = refs
+        h2, cot, wg, bias, gwg, g_out, du_out, gb, h2t, dh2, w1, w2, gw1, gw2, sems = refs
     elif moving:
-        h2, h2t, cot, wg, bias, own, *gwg, g_out, du_out, gb, got, w1, w2, gw1, gw2, sems, held, s0, s1, s2 = refs
+        h2, h2t, cot, wg, bias, own, gwg, g_out, du_out, gb, got, w1, w2, gw1, gw2, sems, held, s0, s1, s2 = refs
         line = Line(0, own, None, got, held, s0, s1, s2)
     else:
-        h2, h2t, cot, wg, bias, *gwg, g_out, du_out, gb, w1, w2, gw1, gw2, sems = refs
-    core = lax.rem(lax.axis_index("batch"), 2)
-
-    def store(src, b, rows, cols, sem):
-        if len(gwg) == 1:
-            pltpu.make_async_copy(src, gwg[0].at[b, rows, cols], sem).start()
-        else:
-
-            @pl.when(lax.rem(b, 2) == core)
-            def _():
-                pltpu.make_async_copy(src, gwg[0].at[b // 2, rows, cols], sem).start()
-
-            @pl.when(lax.rem(b, 2) != core)
-            def _():
-                pltpu.make_async_copy(src, gwg[1].at[b // 2, rows, cols], sem).start()
-
+        h2, h2t, cot, wg, bias, gwg, g_out, du_out, gb, w1, w2, gw1, gw2, sems = refs
     tokens, width = h2.shape
     chunk = g_out.shape[1]
     depth = width // (ns * nb)
@@ -412,12 +600,8 @@
             dg = lax.dot_general(
                 cot[rows, :], w2[cols, :], (((1,), (1,)), ((), ())), preferred_element_type=F32
             )
-            sq = u * u
-            th = jnp.tanh(ROOT * u * (1.0 + 0.044715 * sq))
-            cdf = 0.5 * (1.0 + th)
-            g_out[rows, cols] = (u * cdf).astype(BF)
-            slope = cdf + 0.5 * u * (1.0 - th * th) * (ROOT * (1.0 + 3.0 * 0.044715 * sq))
-            du = (dg * slope).astype(BF)
+            g, du = slopes(u, dg)
+            g_out[rows, cols] = g
             du_out[rows, cols] = du
             total += jnp.sum(du.astype(F32), 0, keepdims=True)
         gb[:, cols] = total
@@ -433,7 +617,11 @@
 
         def store1(k, c):
             s, b = k // nb, lax.rem(k, nb)
-            store(gw1.at[j, pl.ds(k * depth, depth), :], b, pl.ds(s * depth, depth), cols, sems.at[2])
+            pltpu.make_async_copy(
+                gw1.at[j, pl.ds(k * depth, depth), :],
+                gwg.at[b, pl.ds(s * depth, depth), cols],
+                sems.at[2],
+            ).start()
             return c
 
         lax.fori_loop(0, ns * nb, store1, 0)
@@ -441,8 +629,11 @@
 
         def store2(k, c):
             for p in range(pieces):
-                src = gw2.at[j, pl.ds(k * part, part), p * chunk : (p + 1) * chunk]
-                store(src, j * count + k, pl.ds(half + p * part, part), slice(None), sems.at[3])
+                pltpu.make_async_copy(
+                    gw2.at[j, pl.ds(k * part, part), p * chunk : (p + 1) * chunk],
+                    gwg.at[j * count + k, pl.ds(half + p * part, part), :],
+                    sems.at[3],
+                ).start()
             return c
 
         lax.fori_loop(0, count, store2, 0)
@@ -460,14 +651,13 @@
         line.stop()
 
 
-def ff_chunk(ns, nb, h2, h2t, cot, wg, bias, split, own=None):
+def ff_chunk(ns, nb, h2, h2t, cot, wg, bias, own=None):
     tokens, width = h2.shape
     chunk = wg.shape[2]
     tile = min(512, chunk)
     first = h2t is None
     vm = pl.BlockSpec(memory_space=pltpu.VMEM)
     hbm = pl.BlockSpec(memory_space=pl.ANY)
-    grads = (jax.ShapeDtypeStruct((nb // 2,) + wg.shape[1:], BF),) * 2 if split else (jax.ShapeDtypeStruct(wg.shape, BF),)
     inner = jax.ShapeDtypeStruct((tokens, chunk), BF)
     extra = (jax.ShapeDtypeStruct((width, tokens), BF), jax.ShapeDtypeStruct((tokens, width), BF)) if first else ()
     given = (h2, cot, wg, bias) if first else (h2, h2t, cot, wg, bias)
@@ -479,9 +669,9 @@
         more = line_scratch(*own.shape[1:])
     return pl.pallas_call(
         functools.partial(ff_kernel, ns, nb, first, moving),
-        out_shape=grads + (inner, inner, jax.ShapeDtypeStruct((1, chunk), F32)) + extra,
+        out_shape=(jax.ShapeDtypeStruct(wg.shape, BF), inner, inner, jax.ShapeDtypeStruct((1, chunk), F32)) + extra,
         in_specs=[hbm if one is wg or one is own else vm for one in given],
-        out_specs=(hbm,) * len(grads) + (vm,) * (3 + len(extra)),
+        out_specs=(hbm,) + (vm,) * (3 + len(extra)),
         scratch_shapes=[
             pltpu.VMEM((width, chunk), BF),
             pltpu.VMEM((chunk, width), BF),
@@ -498,7 +688,7 @@
             bytes_accessed=4 * wg.size,
             transcendentals=tokens * chunk,
         ),
-        name="ff_first" if first else "ff_chunk",
+        name="ff_chunk",
     )(*given)
 
 
@@ -576,41 +766,42 @@
     ]
 
 
-def gather_blocks(full, rows, place, send, recv):
+def gather_steps(full, rows, place, send_sems, recv_sems):
     me, by_x, by_y, to_x, to_y = place
     half = rows // 2
 
     def copy(k, block, part, to):
         at = full.at[pl.ds(pl.multiple_of(block * rows + part * half, half), half)]
-        one = pltpu.make_async_remote_copy(
-            src_ref=at, dst_ref=at, send_sem=send.at[k], recv_sem=recv.at[k], device_id=to, device_id_type=MESH
-        )
-        one.start()
-        return one
+        return send(at, at, send_sems.at[k], recv_sems.at[k], to)
 
     c0 = copy(0, me, 0, to_x)
     c3 = copy(3, me, 1, to_y)
     c2 = copy(2, me, 0, to_y)
     c1 = copy(1, me, 1, to_x)
+    yield
     c0.wait_recv()
     c4 = copy(4, by_x, 0, to_y)
     c3.wait_recv()
     c5 = copy(5, by_y, 1, to_x)
+    yield
     for one in (c1, c2, c4, c5):
         one.wait_recv()
     for one in (c0, c1, c2, c3, c4, c5):
         one.wait_send()
 
 
+def gather_blocks(full, rows, place, send_sems, recv_sems):
+    for _ in gather_steps(full, rows, place, send_sems, recv_sems):
+        pass
+
+
 GATHER_SEMS = [pltpu.SemaphoreType.DMA((6,)), pltpu.SemaphoreType.DMA((6,))]
 
 
-def middle_kernel(ns, nb, o, wq, mine, obias, gain, shift, x1, h2, wout, load_sem, out, via, from_x, from_y, s1, r1, s2, r2):
+def middle_kernel(o, wout, mine, obias, gain, shift, x1, h2, out, via, from_x, from_y, s1, r1, s2, r2):
     rows, width = mine.shape
     half = rows // 2
-    load_out(ns, nb, wq, wout, load_sem)
     place = greet()
-    pltpu.make_async_copy(wout, wout, load_sem).wait()
 
     def partial(block):
         at = pl.multiple_of(block * rows, rows)
@@ -627,24 +818,24 @@
     gather_blocks(h2, rows, place, s2, r2)
 
 
-def middle(ns, nb, o, wq, mine, obias, gain, shift):
-    tokens, share = o.shape
+def middle(o, wout, mine, obias, gain, shift):
+    tokens = o.shape[0]
     rows, width = mine.shape
     vm = pl.BlockSpec(memory_space=pltpu.VMEM)
     return pl.pallas_call(
-        functools.partial(middle_kernel, ns, nb),
+        middle_kernel,
         out_shape=(jax.ShapeDtypeStruct((rows, width), F32), jax.ShapeDtypeStruct((tokens, width), BF)),
-        in_specs=[vm, pl.BlockSpec(memory_space=pl.ANY)] + [vm] * 4,
+        in_specs=[vm] * 6,
         out_specs=(vm, vm),
-        scratch_shapes=[pltpu.VMEM((share, width), BF), pltpu.SemaphoreType.DMA] + scatter_scratch(rows, width) + GATHER_SEMS,
+        scratch_shapes=scatter_scratch(rows, width) + GATHER_SEMS,
         compiler_params=pltpu.CompilerParams(collective_id=1, has_side_effects=True, vmem_limit_bytes=56 * 2**20),
         cost_estimate=pl.CostEstimate(flops=40 * 10**9, bytes_accessed=12 * tokens * width, transcendentals=0),
         name="project_out",
-    )(o, wq, mine, obias, gain, shift)
+    )(o, wout, mine, obias, gain, shift)
 
 
 def ff_back_kernel(ns, nb, du, wg, before, x1, cot, gain, own, prior, *refs):
-    dx1, da, ggain, gshift, gob, got, w, load_sem, out, via, from_x, from_y, s1, r1, s2, r2, *moving = refs
+    dx1, da, sums, got, w, load_sem, out, via, from_x, from_y, s1, r1, s2, r2, *moving = refs
     line = Line(1, own, prior, got, *moving)
     rows, width = x1.shape
     half = rows // 2
@@ -660,9 +851,9 @@
     steps = scatter_steps(partial, place, (out, via, from_x, from_y), s1, r1)
     next(steps)
     line.go()
-    *_, sums = steps
+    *_, halves = steps
     totals = [jnp.zeros((1, width), F32)] * 3
-    for part, grad in enumerate(sums):
+    for part, grad in enumerate(halves):
         span = slice(part * half, part * half + half)
         normed, rstd = norm_stats(x1[span, :])
         res = cot[span, :].astype(F32) + norm_back(grad, normed, rstd, gain[...])
@@ -670,10 +861,14 @@
         low = res.astype(BF)
         at = pl.multiple_of(place[0] * rows + part * half, half)
         da[pl.ds(at, half), :] = low
-        for k, term in enumerate((grad * normed, grad, low.astype(F32))):
+        for k, term in enumerate((low.astype(F32), grad * normed, grad)):
             totals[k] += jnp.sum(term, 0, keepdims=True)
-    ggain[...], gshift[...], gob[...] = totals
-    gather_blocks(da, rows, place, s2, r2)
+    gather = gather_steps(da, rows, place, s2, r2)
+    next(gather)
+    for k in range(3):
+        sums[k : k + 1, :] = totals[k]
+    for _ in gather:
+        pass
     line.stop()
 
 
@@ -682,19 +877,16 @@
     tokens, chunk = du.shape
     vm = pl.BlockSpec(memory_space=pltpu.VMEM)
     hbm = pl.BlockSpec(memory_space=pl.ANY)
-    row = jax.ShapeDtypeStruct((1, width), F32)
     return pl.pallas_call(
         functools.partial(ff_back_kernel, ns, nb),
         out_shape=(
             jax.ShapeDtypeStruct((rows, width), F32),
             jax.ShapeDtypeStruct((tokens, width), BF),
-            row,
-            row,
-            row,
+            jax.ShapeDtypeStruct((3, width), F32),
             jax.ShapeDtypeStruct(prior.shape, BF),
         ),
         in_specs=[vm, hbm] + [vm] * 4 + [hbm, vm],
-        out_specs=(vm,) * 6,
+        out_specs=(vm,) * 4,
         scratch_shapes=[pltpu.VMEM((width, chunk), BF), pltpu.SemaphoreType.DMA]
         + scatter_scratch(rows, width)
         + GATHER_SEMS
@@ -705,151 +897,116 @@
     )(du, wg, before, x1, cot, gain, own, prior)
 
 
-def finish_kernel(ns, nb, count, *refs):
-    dproj, wq = refs[:2]
-    gs, wgs = refs[2 : 2 + count], refs[2 + count : 2 + 2 * count]
-    own_sum, prior, *later = refs[2 + 2 * count : 3 + 3 * count]
-    refs = refs[3 + 3 * count :]
-    mine, dx1, gain, x1, bias, gx, ggain, gshift, result, gw1, gw2, w = refs[:12]
-    ws, stage = refs[12 : 12 + count], refs[12 + count]
-    gw2_low, load_sem, s0, r0, got, *rest = refs[13 + count :]
-    first, second, moving = rest[:6], rest[6:12], rest[12:]
-    line = Line(2, own_sum, prior, got, *moving)
-    total = moving[0].at[0]
-    summed = [total, *later]
+def finish_kernel(ns, nb, count, dproj, wq, *refs):
+    summed, gs, wgs = refs[:count], refs[count : 2 * count], refs[2 * count : 3 * count]
+    mine, gain, part_grad, gains, stage, gw2, low_sum, w = refs[3 * count : 3 * count + 8]
+    ws = refs[3 * count + 8 : 4 * count + 8]
+    load, s0, r0, *buffers = refs[4 * count + 8 :]
+    buffers, more = buffers[:6], buffers[6:]
     rows, width = mine.shape
     half = rows // 2
-    chunk = gs[0].shape[1]
-    part_rows, pieces, base = chunk // nb, width // chunk, width // nb
-    load_attention(ns, nb, wq, w, load_sem.at[count])
+    chunk = summed[0].shape[1]
+    part_rows, pieces = chunk // nb, width // chunk
+    load_attention(ns, nb, wq, w, load.at[0])
     for c in range(count):
-
-        def load(k, carry):
-            for p in range(pieces):
-                pltpu.make_async_copy(
-                    wgs[c].at[k, pl.ds(base + p * part_rows, part_rows), :],
-                    ws[c].at[pl.ds(k * part_rows, part_rows), p * chunk : (p + 1) * chunk],
-                    load_sem.at[c],
-                ).start()
-            return carry
-
-        lax.fori_loop(0, nb, load, 0)
-    line.ready()
-    me, others, met = greet_seq(ns, line.neighbours())
+        load_second(nb, wgs[c], ws[c], load.at[3 + c])
+    me, others, met = greet_seq(ns)
     by_x, by_y, batch = me + 1 - 2 * lax.rem(me, 2), lax.rem(me + 2, 4), lax.axis_index("batch")
     place = me, by_x, by_y, (by_x, batch), (by_y, batch)
-    depth, hidden = gw1.shape[0], gw1.shape[1] // ns
-
-    def ship(chunks, b, carry):
-        for c in chunks:
+    depth, hidden = stage.shape[0], stage.shape[1] // ns
+
+    def ship(b, carry):
+        for c in range(count):
             cols = pl.ds(pl.multiple_of(me * hidden + (b * count + c) * part_rows, part_rows), part_rows)
             from_cols = pl.ds(pl.multiple_of(b * part_rows, part_rows), part_rows)
             own = pl.ds(pl.multiple_of(me * depth, depth), depth)
-            pltpu.make_async_copy(summed[c].at[own, from_cols], stage.at[:, cols], load_sem.at[count + 1]).start()
+            pltpu.make_async_copy(summed[c].at[own, from_cols], stage.at[:, cols], load.at[1]).start()
             for d, to in enumerate(others):
                 theirs = pl.ds(pl.multiple_of(to[0] * depth, depth), depth)
                 send(summed[c].at[theirs, from_cols], stage.at[:, cols], s0.at[d], r0.at[d], to)
         return carry
 
-    def bring(chunks):
-        lax.fori_loop(0, nb, functools.partial(ship, chunks), 0)
-        for c in chunks:
-            for p in range(pieces):
-                here = pltpu.make_async_copy(
-                    summed[c].at[ns * depth + p * part_rows : ns * depth + (p + 1) * part_rows],
-                    gw2_low.at[c * part_rows : (c + 1) * part_rows, p * chunk : (p + 1) * chunk],
-                    load_sem.at[count + 2],
-                )
-                here.start()
-
-    met()
-    line.go()
-    bring(range(1, count))
+    for c in range(count):
+        for p in range(pieces):
+            pltpu.make_async_copy(
+                summed[c].at[ns * depth + p * part_rows : ns * depth + (p + 1) * part_rows],
+                gw2.at[c * part_rows : (c + 1) * part_rows, p * chunk : (p + 1) * chunk],
+                load.at[2],
+            ).start()
 
     def input_grad(block):
         at = pl.multiple_of(block * rows, rows)
         return dot_t(dproj[pl.ds(at, rows), :], w[...])
 
     def branch(block):
-        at = pl.multiple_of(block * rows, rows)
-        total = jnp.dot(gs[0][pl.ds(at, rows), :], ws[0][...], preferred_element_type=F32)
+        at = pl.ds(pl.multiple_of(block * rows + half, half), half)
+        total = jnp.dot(gs[0][at, :], ws[0][...], preferred_element_type=F32)
         for c in range(1, count):
-            total += jnp.dot(gs[c][pl.ds(at, rows), :], ws[c][...], preferred_element_type=F32)
+            total += jnp.dot(gs[c][at, :], ws[c][...], preferred_element_type=F32)
         return total
 
-    pltpu.make_async_copy(w, w, load_sem.at[count]).wait()
-    one = scatter_steps(input_grad, place, first[:4], *first[4:])
-    two = scatter_steps(branch, place, second[:4], *second[4:])
+    met()
+    pltpu.make_async_copy(w, w, load.at[0]).wait()
+    steps = scatter_steps(input_grad, place, buffers[:4], *buffers[4:])
     for _ in range(3):
-        next(one)
+        next(steps)
     for c in range(count):
-        pltpu.make_async_copy(ws[c], ws[c], load_sem.at[c]).wait()
-    next(two)
-    next(one)
-    next(two)
-    next(two)
-    next(one)
-    sums = next(one)
-    next(two)
-    line.stop()
-    own_part = pltpu.make_async_copy(own_sum.at[line.chip], total, load_sem.at[count + 3])
-    own_part.start()
-    own_part.wait()
-    total[...] = (total[...].astype(F32) + got[0].astype(F32) + got[1].astype(F32)).astype(BF)
-    bring([0])
+        pltpu.make_async_copy(ws[c], ws[c], load.at[3 + c]).wait()
+    others_steps = scatter_steps(branch, place, more[:4], *more[4:])
+    next(others_steps)
+    next(steps)
+    next(others_steps)
+    next(others_steps)
+    lax.fori_loop(0, nb, ship, 0)
+    *_, sums = steps
     totals = [jnp.zeros((1, width), F32)] * 2
     for part, grad in enumerate(sums):
         span = slice(part * half, part * half + half)
         normed, rstd = norm_stats(mine[span, :].astype(F32))
-        gx[span, :] = dx1[span, :] + norm_back(grad, normed, rstd, gain[...])
+        part_grad[span, :] = norm_back(grad, normed, rstd, gain[...])
         for k, term in enumerate((grad * normed, grad)):
             totals[k] += jnp.sum(term, 0, keepdims=True)
-    ggain[...], gshift[...] = totals
-    pltpu.make_async_copy(gw2_low, gw2_low, load_sem.at[count + 2]).wait()
-    gw2[...] = gw2_low[...].astype(F32)
-    next(two)
+    for k in range(2):
+        gains[k : k + 1, :] = totals[k]
+    *_, lows = others_steps
+    for part, total in enumerate(lows):
+        low_sum[part * half // 2 : (part + 1) * half // 2, :] = total
+    pltpu.make_async_copy(gw2, gw2, load.at[2]).wait()
     strip = stage.at[:, :hidden]
-    pltpu.make_async_copy(strip, strip, load_sem.at[count + 1]).wait()
+    pltpu.make_async_copy(strip, strip, load.at[1]).wait()
     for d, to in enumerate(others):
         pltpu.make_async_remote_copy(
             src_ref=strip, dst_ref=strip, send_sem=s0.at[d], recv_sem=r0.at[d], device_id=to, device_id_type=MESH
         ).wait()
-    gw1[...] = stage[...].astype(F32)
-    for part, branch_sum in enumerate(next(two)):
-        span = slice(part * half, part * half + half)
-        result[span, :] = (x1[span, :] + (branch_sum + bias[...])).astype(BF)
-
-
-def finish(ns, nb, dproj, wq, gs, wgs, own, prior, summed, mine, dx1, gain, x1, bias):
+
+
+def finish(ns, nb, dproj, wq, summed, gs, wgs, mine, gain):
     rows, width = mine.shape
-    count, chunk = len(gs), gs[0].shape[1]
+    count, chunk = len(summed), summed[0].shape[1]
     depth, hidden = width // (ns * nb), count * chunk
     vm = pl.BlockSpec(memory_space=pltpu.VMEM)
     hbm = pl.BlockSpec(memory_space=pl.ANY)
-    row = jax.ShapeDtypeStruct((1, width), F32)
+    dma = pltpu.SemaphoreType.DMA
     return pl.pallas_call(
         functools.partial(finish_kernel, ns, nb, count),
         out_shape=(
             jax.ShapeDtypeStruct((rows, width), F32),
-            row,
-            row,
-            jax.ShapeDtypeStruct((rows, width), BF),
-            jax.ShapeDtypeStruct((depth, hidden * ns), F32),
-            jax.ShapeDtypeStruct((hidden // nb, width), F32),
+            jax.ShapeDtypeStruct((2, width), F32),
+            jax.ShapeDtypeStruct((depth, hidden * ns), BF),
+            jax.ShapeDtypeStruct((hidden // nb, width), BF),
+            jax.ShapeDtypeStruct((rows // 2, width), F32),
         ),
-        in_specs=[vm, hbm] + [vm] * count + [hbm] * (count + 1) + [vm] + [hbm] * (count - 1) + [vm] * 5,
-        out_specs=(vm,) * 6,
+        in_specs=[vm, hbm] + [hbm] * count + [vm] * count + [hbm] * count + [vm] * 2,
+        out_specs=(vm,) * 5,
         scratch_shapes=[pltpu.VMEM((width, dproj.shape[1]), BF)]
         + [pltpu.VMEM((chunk, width), BF)] * count
-        + [pltpu.VMEM((depth, hidden * ns), BF), pltpu.VMEM((hidden // nb, width), BF)]
-        + [pltpu.SemaphoreType.DMA((count + 4,)), pltpu.SemaphoreType.DMA((ns - 1,)), pltpu.SemaphoreType.DMA((ns - 1,))]
-        + [pltpu.VMEM(prior.shape, BF)]
-        + scatter_scratch(rows, width) * 2
-        + line_scratch(*prior.shape[1:]),
-        compiler_params=pltpu.CompilerParams(collective_id=3, has_side_effects=True, vmem_limit_bytes=60 * 2**20),
+        + [dma((3 + count,)), dma((ns - 1,)), dma((ns - 1,))]
+        + scatter_scratch(rows, width)
+        + scatter_scratch(rows // 2, width),
+        compiler_params=pltpu.CompilerParams(collective_id=3, has_side_effects=True, vmem_limit_bytes=56 * 2**20),
         cost_estimate=pl.CostEstimate(flops=40 * 10**9, bytes_accessed=24 * rows * width, transcendentals=0),
         name="finish",
-    )(dproj, wq, *gs, *wgs, own, prior, *summed, mine, dx1, gain, x1, bias)
+    )(dproj, wq, *summed, *gs, *wgs, mine, gain)
 
 
 def greet_all(ns, nb):
@@ -872,44 +1029,87 @@
     return me, others, lambda: pl.semaphore_wait(barrier, ns - 1 + len(more))
 
 
-def spread_kernel(ns, w_qkv, w_out, packed, local, s0, r0):
-    depth, width = w_out.shape
-    share = packed.shape[1]
+def spread_kernel(ns, w_qkv, qkv, local, s0, r0):
+    depth = w_qkv.shape[0]
+    share = qkv.shape[1]
+    width = ns * share
     me, others, met = greet_seq(ns)
     copies = []
-    for p in range(ns):
-        rows = slice((3 * ns + p) * depth, (3 * ns + p + 1) * depth)
-        copies.append(pltpu.make_async_copy(w_out.at[:, p * share : (p + 1) * share], packed.at[rows], local.at[3 + p]))
     for t in range(3):
         cols = pl.ds(pl.multiple_of(t * width + me * share, share), share)
         rows = pl.ds(pl.multiple_of((t * ns + me) * depth, depth), depth)
-        copies.append(pltpu.make_async_copy(w_qkv.at[:, cols], packed.at[rows], local.at[t]))
-    for one in copies:
+        one = pltpu.make_async_copy(w_qkv.at[:, cols], qkv.at[rows], local.at[t])
         one.start()
+        copies.append(one)
     met()
     for t in range(3):
         rows = pl.ds(pl.multiple_of((t * ns + me) * depth, depth), depth)
         for d, to in enumerate(others):
             cols = pl.ds(pl.multiple_of(t * width + to[0] * share, share), share)
-            copies.append(send(w_qkv.at[:, cols], packed.at[rows], s0.at[t, d], r0.at[t, d], to))
+            copies.append(send(w_qkv.at[:, cols], qkv.at[rows], s0.at[t, d], r0.at[t, d], to))
     for one in copies:
         one.wait()
 
 
-def spread(ns, w_qkv, w_out):
-    depth, width = w_out.shape
+def spread(ns, w_qkv):
+    depth, width = w_qkv.shape[0], w_qkv.shape[1] // 3
     hbm = pl.BlockSpec(memory_space=pl.ANY)
     dma = pltpu.SemaphoreType.DMA
     return pl.pallas_call(
         functools.partial(spread_kernel, ns),
-        out_shape=jax.ShapeDtypeStruct((4 * ns * depth, width // ns), BF),
-        in_specs=[hbm, hbm],
+        out_shape=jax.ShapeDtypeStruct((3 * ns * depth, width // ns), BF),
+        in_specs=[hbm],
         out_specs=hbm,
-        scratch_shapes=[dma((3 + ns,)), dma((3, ns - 1)), dma((3, ns - 1))],
+        scratch_shapes=[dma((3,)), dma((3, ns - 1)), dma((3, ns - 1))],
         compiler_params=pltpu.CompilerParams(collective_id=5, has_side_effects=True),
-        cost_estimate=pl.CostEstimate(flops=5 * 10**9, bytes_accessed=2 * w_qkv.size, transcendentals=0),
-        name="spread_qkv",
-    )(w_qkv, w_out)
+        cost_estimate=pl.CostEstimate(flops=10**6, bytes_accessed=10**4, transcendentals=0),
+        name="spread",
+    )(w_qkv)
+
+
+def spread_ff_kernel(ns, nb, parts, w1, w2, *refs):
+    packs, (stage, local, s1, r1) = refs[:parts], refs[parts:]
+    depth, rows2, width = w1.shape[0], w2.shape[0], w2.shape[1]
+    hidden = w1.shape[1] // ns
+    part, chunk = rows2 // parts, hidden // parts
+    pieces = width // chunk
+    me, others, met = greet_seq(ns)
+    at = pl.ds(pl.multiple_of(me * depth, depth), depth)
+    cols = pl.ds(pl.multiple_of(me * hidden, hidden), hidden)
+    own = pltpu.make_async_copy(w1.at[:, cols], stage.at[at], local)
+    own.start()
+    met()
+    copies = [own]
+    for d, to in enumerate(others):
+        cols = pl.ds(pl.multiple_of(to[0] * hidden, hidden), hidden)
+        copies.append(send(w1.at[:, cols], stage.at[at], s1.at[d], r1.at[d], to))
+    for c in range(parts):
+        for p in range(pieces):
+            span = slice(ns * depth + p * part, ns * depth + (p + 1) * part)
+            packs[c][span, :] = w2[c * part : (c + 1) * part, p * chunk : (p + 1) * chunk]
+    for one in copies:
+        one.wait()
+    for c in range(parts):
+        for b in range(nb):
+            source = (b * parts + c) * part
+            packs[c][: ns * depth, b * part : (b + 1) * part] = stage[:, source : source + part]
+
+
+def spread_ff(ns, nb, parts, w1, w2):
+    depth, hidden = w1.shape[0], w1.shape[1] // ns
+    vm = pl.BlockSpec(memory_space=pltpu.VMEM)
+    dma = pltpu.SemaphoreType.DMA
+    pack = jax.ShapeDtypeStruct((2 * ns * depth, hidden // parts), BF)
+    return pl.pallas_call(
+        functools.partial(spread_ff_kernel, ns, nb, parts),
+        out_shape=(pack,) * parts,
+        in_specs=[pl.BlockSpec(memory_space=pl.ANY), vm],
+        out_specs=(vm,) * parts,
+        scratch_shapes=[pltpu.VMEM((ns * depth, hidden), BF), dma, dma((ns - 1,)), dma((ns - 1,))],
+        compiler_params=pltpu.CompilerParams(collective_id=11, has_side_effects=True),
+        cost_estimate=pl.CostEstimate(flops=10**6, bytes_accessed=10**4, transcendentals=0),
+        name="spread_ff",
+    )(w1, w2)
 
 
 def whole_row(ns, nb, vecs, row, width):
@@ -921,16 +1121,9 @@
     return jnp.sum(jnp.where(owner == place, lanes, 0.0), 0, keepdims=True)
 
 
-def collect_kernel(ns, nb, parts, w1, w2, mine, cot, vec, *refs):
-    packs = refs[:parts]
-    h1, cots, vecs, acts, local, s0, r0, s1, r1, s2, r2, s3, r3, s4, r4 = refs[parts:]
-    depth = w1.shape[0]
+def collect_kernel(ns, nb, mine, cot, vec, h1, cots, vecs, acts, local, s1, r1, s2, r2, s3, r3, s4, r4):
     rows, width = mine.shape
     half = rows // 2
-    hidden = w1.shape[1] // ns
-    part = hidden // (parts * nb)
-    chunk = hidden // parts
-    pieces = width // chunk
     me, batch = lax.axis_index("seq"), lax.axis_index("batch")
     by_x = me + 1 - 2 * lax.rem(me, 2)
     by_y = lax.rem(me + 2, 4)
@@ -942,37 +1135,12 @@
     vecs[batch, me] = vec[...]
     at_me = pl.ds(pl.multiple_of(me * rows, rows), rows)
     acts[at_me, :] = mine[...]
-    own = pltpu.make_async_copy(cot, cots.at[at_me], local.at[parts])
+    own = pltpu.make_async_copy(cot, cots.at[at_me], local)
     own.start()
-    for c in range(parts):
-        for p in range(pieces):
-            pltpu.make_async_copy(
-                w2.at[c * part : (c + 1) * part, p * chunk : (p + 1) * chunk],
-                packs[c].at[ns * depth + p * part : ns * depth + (p + 1) * part, :],
-                local.at[c],
-            ).start()
-    at = pl.ds(pl.multiple_of(me * depth, depth), depth)
-
-    def keep(b, carry):
-        for c in range(parts):
-            cols = pl.ds(pl.multiple_of(me * hidden + (b * parts + c) * part, part), part)
-            here = packs[c].at[at, pl.ds(pl.multiple_of(b * part, part), part)]
-            pltpu.make_async_copy(w1.at[:, cols], here, local.at[c]).start()
-        return carry
-
-    lax.fori_loop(0, nb, keep, 0)
     pl.semaphore_wait(barrier, ns + nb - 2)
     to_x, to_y = (by_x, batch), (by_y, batch)
     small = vecs.at[batch, me]
     near = [send(small, small, s3.at[d], r3.at[d], to) for d, to in enumerate(others)]
-
-    def ship(b, carry):
-        for c in range(parts):
-            here = packs[c].at[at, pl.ds(pl.multiple_of(b * part, part), part)]
-            for d, to in enumerate(others):
-                cols = pl.ds(pl.multiple_of(to[0] * hidden + (b * parts + c) * part, part), part)
-                send(w1.at[:, cols], here, s0.at[c, d], r0.at[c, d], to)
-        return carry
 
     def normalise(block):
         span = pl.ds(pl.multiple_of(block * rows, rows), rows)
@@ -991,7 +1159,6 @@
         one.wait_recv()
     row = vecs.at[batch]
     wide = [send(row, row, s4.at[d], r4.at[d], to) for d, to in enumerate(column)]
-    lax.fori_loop(0, nb, ship, 0)
     for one in wide:
         one.wait_recv()
     gain, shift = whole_row(ns, nb, vecs, 0, width), whole_row(ns, nb, vecs, 1, width)
@@ -1020,49 +1187,27 @@
         one.wait_recv()
     for one in (c0, c1, c2, c3, c4, c5, d0, d1, d2, d3, d4, d5, *near, *wide):
         one.wait_send()
-    for c in range(parts):
-        pack = packs[c].at[: depth]
-        for d, to in enumerate(others):
-            rest = pltpu.make_async_remote_copy(
-                src_ref=pack, dst_ref=pack, send_sem=s0.at[c, d], recv_sem=r0.at[c, d], device_id=to, device_id_type=MESH
-            )
-            rest.wait()
-        whole = packs[c].at[: depth + pieces * part]
-        pltpu.make_async_copy(whole, whole, local.at[c]).wait()
-
-
-def collect(ns, nb, parts, w1, w2, mine, cot, vec):
-    depth = w1.shape[0]
+
+
+def collect(ns, nb, mine, cot, vec):
     rows, width = mine.shape
-    chunk = w1.shape[1] // (ns * parts)
     vm = pl.BlockSpec(memory_space=pltpu.VMEM)
     hbm = pl.BlockSpec(memory_space=pl.ANY)
     dma = pltpu.SemaphoreType.DMA
-    pack = jax.ShapeDtypeStruct((2 * ns * depth, chunk), BF)
     full = jax.ShapeDtypeStruct((ns * rows, width), BF)
     return pl.pallas_call(
-        functools.partial(collect_kernel, ns, nb, parts),
-        out_shape=(pack,) * parts + (full, full, jax.ShapeDtypeStruct((nb, ns) + vec.shape, F32)),
-        in_specs=[hbm, hbm, vm, hbm, vm],
-        out_specs=(hbm,) * parts + (vm, hbm, vm),
-        scratch_shapes=[
-            pltpu.VMEM((ns * rows, width), BF),
-            dma((parts + 1,)),
-            dma((parts, ns - 1)),
-            dma((parts, ns - 1)),
-            dma((6,)),
-            dma((6,)),
-            dma((6,)),
-            dma((6,)),
-            dma((ns - 1,)),
-            dma((ns - 1,)),
-            dma((nb - 1,)),
-            dma((nb - 1,)),
-        ],
+        functools.partial(collect_kernel, ns, nb),
+        out_shape=(full, full, jax.ShapeDtypeStruct((nb, ns) + vec.shape, F32)),
+        in_specs=[vm, hbm, vm],
+        out_specs=(vm, hbm, vm),
+        scratch_shapes=[pltpu.VMEM((ns * rows, width), BF), dma]
+        + [dma((6,))] * 4
+        + [dma((ns - 1,))] * 2
+        + [dma((nb - 1,))] * 2,
         compiler_params=pltpu.CompilerParams(collective_id=6, has_side_effects=True, vmem_limit_bytes=40 * 2**20),
-        cost_estimate=pl.CostEstimate(flops=40 * 10**9, bytes_accessed=12 * rows * width, transcendentals=0),
+        cost_estimate=pl.CostEstimate(flops=10**6, bytes_accessed=10**4, transcendentals=0),
         name="collect",
-    )(w1, w2, mine, cot, vec)
+    )(mine, cot, vec)
 
 
 def home_kernel(ns, nb, summed, sums, gqkv, gout, small, stage, near, mid, far, local, s0, r0, s1, r1, s2, r2):
@@ -1151,12 +1296,6 @@
     return lax.psum_scatter(flat, "batch", scatter_dimension=0, tiled=True)
 
 
-def own_sums(keep, give):
-    count = lax.axis_size("batch")
-    got = lax.ppermute(give, "batch", [(i, i ^ 1) for i in range(count)])
-    return (keep.astype(F32) + got.astype(F32)).astype(BF)
-
-
 def unpermute(ns, nb, gathered):
     depth = gathered.shape[1] // ns
     return gathered.reshape(nb, ns, depth, -1).transpose(1, 0, 2, 3).reshape(ns * nb * depth, -1)
@@ -1164,9 +1303,8 @@
 
 def unpack_attention(ns, nb, packed):
     share = packed.shape[2]
-    parts = packed.reshape(nb, 4, ns, -1, share)
-    qkv = parts[:, :3].transpose(2, 0, 3, 1, 4).reshape(ns * share, 3 * share)
-    return qkv, parts[:, 3].transpose(0, 2, 1, 3).reshape(share, ns * share)
+    parts = packed.reshape(nb, 3, ns, -1, share)
+    return parts.transpose(2, 0, 3, 1, 4).reshape(ns * share, 3 * share)
 
 
 def body(
@@ -1199,22 +1337,24 @@
     mine, cot_mine = block_input[0], out_cotangent[0]
 
     vectors = (ln1_gain, ln1_bias, qv_bias, out_bias, ln2_gain, ln2_bias, fc1_bias, fc2_bias)
+    wout = lax.all_gather(w_out, "batch", axis=0, tiled=True)
     if planar:
-        attn = spread(ns, w_qkv, w_out)
-        attn, vectors = lax.optimization_barrier((attn, vectors))
+        wq = spread(ns, w_qkv)
+        wq, w_fc1 = lax.optimization_barrier((wq, w_fc1))
+        packs = spread_ff(ns, nb, PARTS, w_fc1, w_fc2)
+        packs, vectors, wout = lax.optimization_barrier((packs, vectors, wout))
         spare = jnp.zeros((1024 - 2 * depth - sum(vec.shape[0] for vec in vectors),), BF)
         block = jnp.concatenate([vectors[0], vectors[0], vectors[1], vectors[1], *vectors[2:], spare])
         block = block.astype(F32).reshape(8, 128)
-        *packs, h1, cot, packed = collect(ns, nb, PARTS, w_fc1, w_fc2, mine, cot_mine, block)
+        h1, cot, packed = collect(ns, nb, mine, cot_mine, block)
         packed = packed.transpose(1, 0, 2, 3).reshape(ns * nb, 1024)
         packed = jnp.concatenate([packed[:, :depth], packed[:, 2 * depth : 3 * depth], packed[:, 4 * depth :]], 1)
     else:
-        attn = lax.all_to_all(w_qkv.reshape(depth, 3, ns, share), "seq", 2, 0).transpose(2, 0, 1, 3)
-        attn = jnp.concatenate([attn, w_out.reshape(depth, ns, share).transpose(1, 0, 2)[None]], 0)
-        attn = attn.reshape(4 * ns * depth, share)
+        wq = lax.all_to_all(w_qkv.reshape(depth, 3, ns, share), "seq", 2, 0).transpose(2, 0, 1, 3)
+        wq = wq.reshape(3 * ns * depth, share)
         vector = jnp.concatenate(vectors).astype(F32)
         packed = lax.all_gather(vector, ("seq", "batch"), axis=0, tiled=False)
-    attn = lax.all_gather(attn, "batch", axis=0, tiled=True).reshape(nb, 4 * ns * depth, share)
+    wq = lax.all_gather(wq, "batch", axis=0, tiled=True).reshape(nb, 3 * ns * depth, share)
     full, at = [], 0
     for vec in vectors:
         full.append(packed[:, at : at + vec.shape[0]].reshape(1, -1))
@@ -1238,56 +1378,56 @@
         cot = gather_seq(cot_mine)
     wgs = [lax.all_gather(pack, "batch", axis=0, tiled=True).reshape(nb, -1, chunk) for pack in packs]
 
-    qkv, o, h1t = attend(ns, nb, lengths, h1, attn, bias3)
+    qkv, o, h1t = attend(ns, nb, lengths, h1, wq, bias3)
     if planar:
-        x1, h2 = middle(ns, nb, o, attn, mine, obias, gain2, shift2)
+        x1, h2 = middle(o, wout, mine, obias, gain2, shift2)
     else:
-        wq, wout = unpack_attention(ns, nb, attn)
         a = scatter_seq(jnp.dot(o, wout, preferred_element_type=F32))
         x1 = mine.astype(F32) + (a + obias)
         h2 = gather_seq((norm_stats(x1)[0] * gain2 + shift2).astype(BF))
 
-    *gw, g, du, gb, h2t, before = ff_chunk(ns, nb, h2, None, cot, wgs[0], bias1[:, 0].reshape(1, chunk), planar)
-    gws, gs, dus, gb1 = [gw], [g], [du], [gb.reshape(nb, 1, part)]
+    line = ()
     if planar:
-        own = own_sums(*gw)
+        own, g, du, gb, h2t, before = ff_first(ns, nb, h2, cot, wgs[0], bias1[:, 0].reshape(1, chunk))
+        line = (own,)
+        h2t, gain1, gain2, bias2 = lax.optimization_barrier((h2t, gain1, gain2, bias2))
+        gws = [None]
     else:
-        gws = [scatter_batch(gw[0])]
+        gw, g, du, gb, h2t, before = ff_chunk(ns, nb, h2, None, cot, wgs[0], bias1[:, 0].reshape(1, chunk))
+        gws = [scatter_batch(gw)]
+    gs, dus, gb1 = [g], [du], [gb.reshape(nb, 1, part)]
     for c in range(1, PARTS):
-        gw, g, du, gb, *got = ff_chunk(
-            ns, nb, h2, h2t, cot, wgs[c], bias1[:, c].reshape(1, chunk), False, own if planar else None
-        )
+        gw, g, du, gb, *got = ff_chunk(ns, nb, h2, h2t, cot, wgs[c], bias1[:, c].reshape(1, chunk), *line)
         gws.append(scatter_batch(gw))
         gs.append(g)
         dus.append(du)
         gb1.append(gb.reshape(nb, 1, part))
-    cot_f = cot_mine.astype(F32)
     if planar:
-        dx1, da, ggain2, gshift2, gob, got = ff_back(
-            ns, nb, dus[1], wgs[1], before, x1, cot_mine, gain2, own, got[0]
-        )
+        dx1, da, rows2, got = ff_back(ns, nb, dus[1], wgs[1], before, x1, cot_mine, gain2, own, got[0])
+        line = own, got, *gs, *wgs
     else:
         dh2 = before.astype(F32) + dot_t(dus[1], unpermute(ns, nb, wgs[1][:, : ns * depth]))
         dh2 = scatter_seq(dh2)
         normed2, rstd2 = norm_stats(x1)
-        ggain2 = jnp.sum(dh2 * normed2, 0)
-        gshift2 = jnp.sum(dh2, 0)
-        dx1 = cot_f + norm_back(dh2, normed2, rstd2, gain2)
+        dx1 = cot_mine.astype(F32) + norm_back(dh2, normed2, rstd2, gain2)
         da_mine = dx1.astype(BF)
-        gob = jnp.sum(da_mine.astype(F32), 0)
+        rows2 = jnp.stack([jnp.sum(term, 0) for term in (da_mine.astype(F32), dh2 * normed2, dh2)])
         da = gather_seq(da_mine)
 
-    gattn, dproj, gqv = attend_back(ns, nb, lengths, h1t, da, attn, o, qkv)
+    gattn, dproj, gqv, *more = attend_back(ns, nb, lengths, h1t, da, wout, o, qkv, *line)
+    if planar:
+        gws[0], y = more
     gattn = scatter_batch(gattn)
     if planar:
-        gx, ggain1, gshift1, out, gw1, gw2 = finish(
-            ns, nb, dproj, attn, gs, wgs, own, got, gws[1:], mine, dx1, gain1, x1, bias2
-        )
+        gx, rows1, gw1, gw2, lower = finish(ns, nb, dproj, wq, gws, gs, wgs, mine, gain1)
+        gx, rows2, gqv, gb1, cot_mine, y = lax.optimization_barrier((gx, rows2, gqv, gb1, cot_mine, y))
+        gx = dx1 + gx
+        out = (x1 + (jnp.concatenate([y, lower], 0) + bias2)).astype(BF)
+        gw1, gw2 = gw1.astype(F32), gw2.astype(F32)
     else:
-        dh1 = scatter_seq(dot_t(dproj, wq))
+        dh1 = scatter_seq(dot_t(dproj, unpack_attention(ns, nb, wq)))
         normed1, rstd1 = norm_stats(mine.astype(F32))
-        ggain1 = jnp.sum(dh1 * normed1, 0)
-        gshift1 = jnp.sum(dh1, 0)
+        rows1 = jnp.stack([jnp.sum(dh1 * normed1, 0), jnp.sum(dh1, 0)])
         gx = dx1 + norm_back(dh1, normed1, rstd1, gain1)
         y = 0.0
         for g, wg in zip(gs, wgs):
@@ -1310,12 +1450,17 @@
     gqv = gqv[0]
     gqv = jnp.concatenate([place(gqv[:share], width), place(gqv[2 * share :], width)])
     gb1 = place(jnp.stack(gb1, 1).reshape(-1), ns * hidden)
-    gb2 = jnp.sum(cot_f, 0)
-    sums = (ggain1, gshift1, gqv, gob, ggain2, gshift2, gb1, gb2)
-    sums = jnp.concatenate([t.reshape(ns * nb, -1) for t in sums], 1)
+    gb2 = jnp.sum(cot_mine.astype(F32), 0)
+
+    def shards(grads):
+        return grads.reshape(grads.shape[0], ns * nb, -1).transpose(1, 0, 2).reshape(ns * nb, -1)
+
+    sums = [shards(rows1), gqv.reshape(ns * nb, -1), shards(rows2), gb1.reshape(ns * nb, -1), gb2.reshape(ns * nb, -1)]
+    sums = jnp.concatenate(sums, 1)
     if planar:
         sums = jnp.pad(sums, ((0, 0), (0, 1024 - sums.shape[1]))).reshape(ns, nb, 8, 128)
-        gwqkv, gwo, sums = home(ns, nb, gattn, sums.transpose(1, 0, 2, 3))
+        sums, gx, out, gw1, gw2 = lax.optimization_barrier((sums.transpose(1, 0, 2, 3), gx, out, gw1, gw2))
+        gwqkv, gwo, sums = home(ns, nb, gattn, sums)
         sums = sums.reshape(-1)
     else:
         sums = lax.psum_scatter(sums, ("seq", "batch"), scatter_dimension=0, tiled=True)[0]

time: 580 us -> 572 us (0.986)
    pallas_call x3 -> x5, Pallas kernels: 200 us -> 255 us  [the longest x1 77.9 us: middle(): pl.pallas_call(middle_kernel, out_shape=(jax.ShapeDtypeStruct((rows, widt...]
    pallas_call x2 -> x1, Pallas kernels: 71.8 us -> 34.4 us  [ff_chunk(): pl.pallas_call(functools.partial(ff_kernel, ns, nb, first, moving), out_s...]
    pallas_call x1, Pallas kernels: 95.9 us -> 74.9 us  [finish(): pl.pallas_call(functools.partial(finish_kernel, ns, nb, count), out_shape...]
    ppermute x1 -> x0, waiting for transfers between devices: 7.36 us -> none  [own_sums(): got = lax.ppermute(give, 'batch', [(i, i ^ 1) for i in range(count)])]
  transfers between devices with their start and end apart: 6 -> 6, of which waited for: 3 -> 3; matrix products, arithmetic and copies ran while one was open for 3% -> 3% of each run, Pallas kernels for 77% -> 80%
where the time goes in v4:
time: 572 us; the launch traced here: 562 us
  Pallas kernels  502 us (88%)
  local copies, waits for them, and re-layouts  19 us (3%)
  waiting for transfers between devices  16.2 us (3%)
  between operations  15.7 us (3%)
  other arithmetic  9.63 us (2%)
    pallas_call x1, Pallas kernels, ff_back(): pl.pallas_call(functools.partial(ff_back_kernel, ns, nb), out_shape=(jax....  85.6 us
    pallas_call x1, Pallas kernels, middle(): pl.pallas_call(middle_kernel, out_shape=(jax.ShapeDtypeStruct((rows, widt...  77.9 us
    pallas_call x1, Pallas kernels, finish(): pl.pallas_call(functools.partial(finish_kernel, ns, nb, count), out_shape...  74.9 us
    pallas_call x1, Pallas kernels, collect(): pl.pallas_call(functools.partial(collect_kernel, ns, nb), out_shape=(full...  72.5 us
    pallas_call x1, Pallas kernels, attend_back(): pl.pallas_call(functools.partial(attend_back_kernel, ns, nb, moving), out...  48.3 us
    pallas_call x1, Pallas kernels, ff_first(): pl.pallas_call(functools.partial(ff_first_kernel, ns, nb), out_shape=(jax...  38.9 us
    pallas_call x1, Pallas kernels, ff_chunk(): pl.pallas_call(functools.partial(ff_kernel, ns, nb, first, moving), out_s...  34.4 us
    pallas_call x1, Pallas kernels, attend(): pl.pallas_call(functools.partial(attend_kernel, ns, nb), out_shape=(jax.S...  22.1 us
  transfers between devices with their start and end apart: 6, of which 3 were waited for; matrix products, arithmetic and copies ran while one was open for 3% of the time, Pallas kernels for 80%

profile of v4, /device:TPU:0, one launch (start us, length us, event | category | flops | bytes accessed | tf_op | source)
XLA Modules:
  0.0 562.4 jit_solution(12606873970881297930)
XLA Ops:
  7.2 0.7 all-gather.5.cloned.1.call-update
  8.0 13.8 %spread.1 = bf16[768,512]{1,0:T(8,128)(2,1)} custom-call(bf16[64,6144]{1,0:T(8,128)(2,1)} %w_qkv.1), custom_call_target="tpu_custom_call" | custom-call | flops 1000000 | bytes 10000 | tf_op jit(solution)/shard_map/spread/pallas_call | solution.py:1058
  22.0 17.6 %spread_ff.1 = (bf16[512,1024]{1,0:T(8,128)(2,1)}, bf16[512,1024]{1,0:T(8,128)(2,1)}) custom-call(bf16[64,8192]{1,0:T(8,128)(2,1)} %w1, bf16[256,2048]{1,0:T(8,128)(2,1)} %w2.1), custom_call_target="tpu_custom_call" | custom-call | flops 1000000 | bytes 10000 | tf_op jit(solution)/shard_map/spread_ff/pallas_call | solution.py:1103
  39.6 1.9 all-gather.5.cloned.1.call-done.wout
  41.5 0.5 all-gather.11.cloned.1.call-update
  42.9 0.1 concatenate.20
  43.0 72.5 %collect.1 = (bf16[1024,2048]{1,0:T(8,128)(2,1)S(1)}, bf16[1024,2048]{1,0:T(8,128)(2,1)S(1)}, f32[8,4,8,128]{3,2,1,0:T(8,128)S(1)}) custom-call(bf16[256,2048]{1,0:T(8,128)(2,1)S(1)} %bitcast.63, bf16[256,2048]{1,0:T(8,128)(2,1)S(1)} %bitcast.59, f32[8,128]{1,0:T(8,128)S(1)} %bitcast_convert_fusion.vec), custom_call_target="tpu_custom_call" | custom-call | flops 1000000 | bytes 10000 | tf_op jit(solution)/shard_map/collect/pallas_call | solution.py:1198
  115.5 2.1 copy-done
  117.6 2.0 copy-done.4
  119.6 0.1 fusion.3
  119.7 0.7 reshape.123
  120.4 0.1 slice_bitcast_fusion
  120.5 0.7 reshape.117.gain
  121.2 0.7 reshape.122.refs_7_
  121.9 0.7 reshape.118.shift
  122.6 0.7 reshape.116.obias
  123.2 0.6 fusion.2.bias
  123.9 0.6 slice_bitcast_fusion.1
  124.5 22.1 %attend.1 = (bf16[1024,1536]{1,0:T(8,128)(2,1)}, bf16[1024,512]{1,0:T(8,128)(2,1)}, bf16[2048,1024]{1,0:T(8,128)(2,1)}) custom-call(s32[1]{0:T(128)S(6)} %copy.51.length, bf16[1024,2048]{1,0:T(8,128)(2,1)} %copy-done, bf16[8,768,512]{2,1,0:T(8,128)(2,1)} %bitcast.66, f32[1,1536]{1,0:T(1,128)} %fusion.2.bias), custom_call_target="tpu_custom_call" | custom-call | flops 1000000 | bytes 10000 | tf_op jit(solution)/shard_map/attend/pallas_call | solution.py:214
  146.5 77.9 %project_out.1 = (f32[256,2048]{1,0:T(8,128)}, bf16[1024,2048]{1,0:T(8,128)(2,1)}) custom-call(bf16[1024,512]{1,0:T(8,128)(2,1)} %get-tuple-element.95.o, bf16[512,2048]{1,0:T(8,128)(2,1)} %all-gather.5.cloned.1.call-done.wout, bf16[256,2048]{1,0:T(8,128)(2,1)} %bitcast.61, f32[1,2048]{1,0:T(1,128)} %reshape.116.obias, f32[1,2048]{1,0:T(1,128)} %reshape.117.gain, ...), custom_call_target="tpu_custom_call" | custom-call | flops 40000000000 | bytes 25165824 | tf_op jit(solution)/shard_map/project_out/pallas_call | solution.py:825
  224.5 38.9 %ff_first.1 = (bf16[4,512,1024]{2,1,0:T(8,128)(2,1)}, bf16[1024,1024]{1,0:T(8,128)(2,1)}, bf16[1024,1024]{1,0:T(8,128)(2,1)}, f32[1,1024]{1,0:T(1,128)}, bf16[20...) custom-call(bf16[1024,2048]{1,0:T(8,128)(2,1)} %get-tuple-element.97.h2.refs_0_, bf16[1024,2048]{1,0:T(8,128)(2,1)} %copy-done.4, ...), custom_call_target="tpu_custom_call" | custom-call | flops 40000000000 | bytes 33554432 | tf_op jit(solution)/shard_map/ff_first/pallas_call | solution.py:512
  263.4 8.4 %all-gather.11.cloned.1.call-done = bf16[4096,1024]{1,0:T(8,128)(2,1)} async-done(((bf16[512,1024]{1,0:T(8,128)(2,1)}), bf16[4096,1024]{1,0:T(8,128)(2,1)}) %all-gather.11.cloned.1.call-update) | async-done | bytes 8388624 | tf_op jit(solution)/shard_map/all_gather | solution.py:1379
  271.8 34.4 %ff_chunk.1 = (bf16[8,512,1024]{2,1,0:T(8,128)(2,1)}, bf16[1024,1024]{1,0:T(8,128)(2,1)}, bf16[1024,1024]{1,0:T(8,128)(2,1)}, f32[1,1024]{1,0:T(1,128)}, bf16[2,512,1024]{2,1,0:T(8,128)(2,1)}) custom-call(bf16[1024,2048]{1,0:T(8,128)(2,1)} %get-tuple-element.97.h2.refs_0_, bf16[2048,1024]{1,0:T(8,128)(2,1)} %get-tuple-element.101.refs_1_, ...), custom_call_target="tpu_custom_call" | custom-call | flops 40000000000 | bytes 16777216 | tf_op jit(solution)/shard_map/ff_chunk/pallas_call | solution.py:670
  306.2 85.6 %ff_back.1 = (f32[256,2048]{1,0:T(8,128)}, bf16[1024,2048]{1,0:T(8,128)(2,1)}, f32[3,2048]{1,0:T(4,128)}, bf16[2,512,1024]{2,1,0:T(8,128)(2,1)}) custom-call(bf16[1024,1024]{1,0:T(8,128)(2,1)} %get-tuple-element.104.du, bf16[8,512,1024]{2,1,0:T(8,128)(2,1)} %bitcast.92, bf16[1024,2048]{1,0:T(8,128)(2,1)} %get-tuple-element.105.before, ...), custom_call_target="tpu_custom_call" | custom-call | flops 40000000000 | bytes 25165824 | tf_op jit(solution)/shard_map/ff_back/pallas_call | solution.py:880
  391.9 48.3 %attend_back.1 = (bf16[8,1024,512]{2,1,0:T(8,128)(2,1)}, bf16[1024,1536]{1,0:T(8,128)(2,1)}, f32[1,1536]{1,0:T(1,128)}, bf16[512,1024]{1,0:T(8,128)(2,1)}, f32[128,2048]{1,0:T(8,128)}) custom-call(s32[1]{0:T(128)S(6)} %copy.51.length, bf16[2048,1024]{1,0:T(8,128)(2,1)} %get-tuple-element.94.h1t, bf16[1024,2048]{1,0:T(8,128)(2,1)} %get-tuple-element.109.da, ...), custom_call_target="tpu_custom_call" | custom-call | flops 40000000000 | bytes 12582912 | tf_op jit(solution)/shard_map/attend_back/pallas_call | solution.py:358
  440.3 74.9 %finish.1 = (f32[256,2048]{1,0:T(8,128)}, f32[2,2048]{1,0:T(2,128)}, bf16[64,8192]{1,0:T(8,128)(2,1)}, bf16[256,2048]{1,0:T(8,128)(2,1)}, f32[128,2048]{1,0:T(8,128)}) custom-call(bf16[1024,1536]{1,0:T(8,128)(2,1)} %get-tuple-element.114.dproj, bf16[8,768,512]{2,1,0:T(8,128)(2,1)} %bitcast.67, bf16[512,1024]{1,0:T(8,128)(2,1)} %get-tuple-element.115.refs_0_, ...), custom_call_target="tpu_custom_call" | custom-call | flops 40000000000 | bytes 12582912 | tf_op jit(solution)/shard_map/finish/pallas_call | solution.py:990
  515.3 0.3 dynamic_update_slice.11
  515.6 3.0 fusion.1
  518.7 0.1 reshape.134
  518.8 0.1 reshape.126
  518.9 0.1 reshape.127
  519.0 0.1 reshape.130
  519.1 0.1 reshape.131
  519.2 2.8 convert_element_type.25
  522.0 1.6 convert_element_type.26
  523.6 0.8 copy-done.6
  524.4 1.6 add.43
  526.0 0.3 dynamic_update_slice.9
  526.2 0.3 dynamic_update_slice.10
  526.5 0.1 concatenate.25
  526.6 0.7 copy_bitcast_fusion.2.sums
  527.3 4.6 reduce-scatter.5.cloned.1.call-done.summed
  531.9 15.7 %home.1 = (f32[64,6144]{1,0:T(8,128)}, f32[64,2048]{1,0:T(8,128)}, f32[8,128]{1,0:T(8,128)}) custom-call(bf16[1024,512]{1,0:T(8,128)(2,1)} %reduce-scatter.5.cloned.1.call-done.summed, f32[8,4,8,128]{3,2,1,0:T(8,128)} %copy_bitcast_fusion.2.sums), custom_call_target="tpu_custom_call" | custom-call | flops 5000000000 | bytes 2097152 | tf_op jit(solution)/shard_map/home/pallas_call | solution.py:1255
  547.6 1.3 slice_bitcast_fusion.3
  548.8 1.3 slice.93
  550.2 1.5 fusion.5
  551.7 2.7 copy.52
  554.3 0.8 copy.53
  (78 shorter events, 0.7 us)
Async XLA Ops:
  7.2 34.3 %all-gather.5.cloned.1.call-start = ((), (), s32[]{:S(2)}) async-start(), calls=%async_computation.2 | async-start | bytes 2359296 | tf_op jit(solution)/shard_map/all_gather | solution.py:1340
  7.9 116.5 %all-gather.7.cloned.1.call-start = ((), (), s32[]{:S(2)}) async-start(), calls=%async_computation.3 | async-start | bytes 7077888 | tf_op jit(solution)/shard_map/all_gather | solution.py:1357
  21.8 21.0 %copy-start.16 = (bf16[64]{0:T(256)(128)(2,1)S(1)}, bf16[64]{0:T(256)(128)(2,1)}, u32[]{:S(2)}) copy-start(bf16[64]{0:T(256)(128)(2,1)} %param.17) | copy-start | bytes 388
  21.8 21.0 %copy-start.17 = (bf16[64]{0:T(256)(128)(2,1)S(1)}, bf16[64]{0:T(256)(128)(2,1)}, u32[]{:S(2)}) copy-start(bf16[64]{0:T(256)(128)(2,1)} %param.18) | copy-start | bytes 388
  21.9 21.0 %copy-start.18 = (bf16[128]{0:T(256)(128)(2,1)S(1)}, bf16[128]{0:T(256)(128)(2,1)}, u32[]{:S(2)}) copy-start(bf16[128]{0:T(256)(128)(2,1)} %param.20) | copy-start | bytes 772
  21.9 21.0 %copy-start.19 = (bf16[64]{0:T(256)(128)(2,1)S(1)}, bf16[64]{0:T(256)(128)(2,1)}, u32[]{:S(2)}) copy-start(bf16[64]{0:T(256)(128)(2,1)} %param.22) | copy-start | bytes 388
  21.9 21.0 %copy-start.20 = (bf16[64]{0:T(256)(128)(2,1)S(1)}, bf16[64]{0:T(256)(128)(2,1)}, u32[]{:S(2)}) copy-start(bf16[64]{0:T(256)(128)(2,1)} %param.23) | copy-start | bytes 388
  21.9 20.9 %copy-start.21 = (bf16[64]{0:T(256)(128)(2,1)S(1)}, bf16[64]{0:T(256)(128)(2,1)}, u32[]{:S(2)}) copy-start(bf16[64]{0:T(256)(128)(2,1)} %param.24) | copy-start | bytes 388
  21.9 20.9 %copy-start.22 = (bf16[256]{0:T(256)(128)(2,1)S(1)}, bf16[256]{0:T(256)(128)(2,1)}, u32[]{:S(2)}) copy-start(bf16[256]{0:T(256)(128)(2,1)} %param.26) | copy-start | bytes 1540
  21.9 20.9 %copy-start.23 = (bf16[64]{0:T(256)(128)(2,1)S(1)}, bf16[64]{0:T(256)(128)(2,1)}, u32[]{:S(2)}) copy-start(bf16[64]{0:T(256)(128)(2,1)} %param.28) | copy-start | bytes 388
  21.9 21.0 %copy-start.1 = (bf16[1,256,2048]{2,1,0:T(8,128)(2,1)S(1)}, bf16[1,256,2048]{2,1,0:T(8,128)(2,1)}, u32[]{:S(2)}) copy-start(bf16[1,256,2048]{2,1,0:T(8,128)(2,1)} %param.29) | copy-start | bytes 3145732
  21.9 21.0 %copy-start.3 = (bf16[1,256,2048]{2,1,0:T(8,128)(2,1)S(1)}, bf16[1,256,2048]{2,1,0:T(8,128)(2,1)}, u32[]{:S(2)}) copy-start(bf16[1,256,2048]{2,1,0:T(8,128)(2,1)} %param.15) | copy-start | bytes 3145732
  21.9 202.5 %all-gather.9.cloned.1.call-start = ((), (), s32[]{:S(2)}) async-start(), calls=%async_computation.4 | async-start | bytes 9437184 | tf_op jit(solution)/shard_map/all_gather | solution.py:1379
  41.5 230.3 %all-gather.11.cloned.1.call-start = ((), (), s32[]{:S(2)}) async-start(), calls=%async_computation.5 | async-start | bytes 9437184 | tf_op jit(solution)/shard_map/all_gather | solution.py:1379
  42.0 398.2 %reduce-scatter.3.cloned.1.call-start = ((), (), s32[]{:S(2)}) async-start(), calls=%async_computation.6 | async-start | bytes 9437184 | tf_op jit(solution)/shard_map/reduce_scatter | solution.py:1296
  115.5 2.1 copy-start
  117.6 2.0 copy-start.4
  306.2 225.7 %reduce-scatter.5.cloned.1.call-start = ((), (), s32[]{:S(2)}) async-start(), calls=%async_computation.7 | async-start | bytes 9437184 | tf_op jit(solution)/shard_map/reduce_scatter | solution.py:1296
  440.2 75.0 %copy-start.13 = (f32[1,1024]{1,0:T(1,128)S(1)}, f32[1,1024]{1,0:T(1,128)}, u32[]{:S(2)}) copy-start(f32[1,1024]{1,0:T(1,128)} %get-tuple-element.122) | copy-start | bytes 12292
  440.2 75.0 %copy-start.14 = (f32[1,1024]{1,0:T(1,128)S(1)}, f32[1,1024]{1,0:T(1,128)}, u32[]{:S(2)}) copy-start(f32[1,1024]{1,0:T(1,128)} %get-tuple-element.123) | copy-start | bytes 12292
  440.2 75.4 %copy-start.2 = (bf16[1,256,2048]{2,1,0:T(8,128)(2,1)S(1)}, bf16[1,256,2048]{2,1,0:T(8,128)(2,1)}, u32[]{:S(2)}) copy-start(bf16[1,256,2048]{2,1,0:T(8,128)(2,1)} %param.29) | copy-start | bytes 3145732
  440.2 75.4 %copy-start.5 = (f32[256,2048]{1,0:T(8,128)S(1)}, f32[256,2048]{1,0:T(8,128)}, u32[]{:S(2)}) copy-start(f32[256,2048]{1,0:T(8,128)} %get-tuple-element.106.x1) | copy-start | bytes 6291460
  440.3 75.4 %copy-start.10 = (f32[1,2048]{1,0:T(1,128)S(1)}, f32[1,2048]{1,0:T(1,128)}, u32[]{:S(2)}) copy-start(f32[1,2048]{1,0:T(1,128)} %reshape.123) | copy-start | bytes 24580
  515.6 3.1 copy-start.12
  515.6 3.3 copy-start.11
  518.7 3.4 copy-start.8
  519.2 4.4 copy-start.7
  522.0 2.4 copy-start.6
  524.4 1.6 copy-start.15
  547.6 6.7 %copy-start.9 = (f32[64,2048]{1,0:T(8,128)S(1)}, f32[64,2048]{1,0:T(8,128)}, u32[]{:S(2)}) copy-start(f32[64,2048]{1,0:T(8,128)} %get-tuple-element.185) | copy-start | bytes 1572868
Sparse Core Ops, SparseCore 0:
  9.6 31.7 all-gather.4
  43.1 64.2 all-gather.6
  109.0 80.6 all-gather.8
  191.2 80.5 all-gather.10
  306.3 124.3 reduce-scatter.2
  440.3 91.5 reduce-scatter.4

commit v5 on v4

--- a/solution.py
+++ b/solution.py
@@ -227,14 +227,19 @@
     )(lengths, h1, wq, bias)
 
 
-def attend_back_kernel(ns, nb, moving, length, h1t, da, wout, o, qkv, *refs):
+def upper_rows(rows):
+    return 3 * rows // 4
+
+
+def attend_back_kernel(ns, nb, moving, length, h1t_in, da, wout, o, qkv_in, *refs):
     line = None
     if moving:
-        own, prior, g0, g1, wg0, wg1, packed, dproj, gqv, sums, branch_sum, do, gw, gwo, acc_k, acc_v, sems, *rest = refs
+        own, prior, g0_in, g1_in, wg0, wg1, pair, dproj, gqv, sums, branch_sum, *rest = refs
+        do, gw, gwo, acc_k, acc_v, sems, h1t, qkv, g0, g1, near, to_twin, from_twin, *rest = rest
         out, via, from_x, from_y, s1, r1, got, *rest = rest
         line = Line(2, own, prior, got, *rest)
     else:
-        packed, dproj, gqv, do, gw, gwo, acc_k, acc_v, sems = refs
+        packed, dproj, gqv, do, gw, gwo, acc_k, acc_v, sems, h1t, qkv = refs
     width, tokens = h1t.shape
     share = o.shape[1]
     rows = tokens // ns
@@ -242,25 +247,65 @@
     scale = HEAD_DIM ** (-0.5)
     limit = length[0]
     steps = None
+    loads = [pltpu.make_async_copy(qkv_in, qkv, sems.at[4]), pltpu.make_async_copy(h1t_in, h1t, sems.at[5])]
     if moving:
         chunk = g0.shape[1]
         halves = gw.at[:chunk], gw.at[chunk:]
-        for k, wg in enumerate((wg0, wg1)):
+        line.ready()
+        for k, (wg, src, dst) in enumerate(((wg0, g0_in, g0), (wg1, g1_in, g1))):
+            loads.append(pltpu.make_async_copy(src, dst, sems.at[6 + k]))
+            loads[-1].start()
             load_second(nb, wg, halves[k], sems.at[2 + k])
-        line.ready()
-        place = greet(line.neighbours())
+        loads[0].start()
+        loads[1].start()
+        chips = nb // 2
+        twin = (line.seq, 2 * line.chip + 1 - line.core)
+        place = greet([*line.neighbours(), twin])
         line.go()
 
+        def strip(row, core):
+            return pl.ds(pl.multiple_of((row + core) * depth, depth), depth)
+
+        def exchange(t, source):
+            for c in range(chips):
+                for k in range(ns):
+                    ref, row, cols = source(c, k)
+                    there = near.at[c, (t * ns + k) * depth : (t * ns + k + 1) * depth]
+                    send(ref.at[strip(row, 1 - line.core), cols], there, to_twin.at[t], from_twin.at[t], twin)
+
+        def combine(t, source):
+            got_piece = near.at[:, t * ns * depth : (t + 1) * ns * depth]
+            whole = pltpu.make_async_remote_copy(
+                src_ref=got_piece,
+                dst_ref=got_piece,
+                send_sem=to_twin.at[t],
+                recv_sem=from_twin.at[t],
+                device_id=twin,
+                device_id_type=MESH,
+            )
+            whole.wait()
+            for c in range(chips):
+                for k in range(ns):
+                    ref, row, cols = source(c, k)
+                    here = slice((t * ns + k) * depth, (t * ns + k + 1) * depth)
+                    total = ref[strip(row, line.core), cols].astype(F32) + near[c, here].astype(F32)
+                    pair[c, here] = total.astype(BF)
+
+        def piece_out(c, k):
+            return gwo, 2 * c, slice(k * share, (k + 1) * share)
+
+        def piece_qkv(t):
+            return lambda c, k: (gw, k * nb + 2 * c, slice(t * share, (t + 1) * share))
+
         def branch(block):
-            at = pl.ds(pl.multiple_of(block * rows, rows), rows // 2)
+            at = pl.ds(pl.multiple_of(block * rows, rows), upper_rows(rows))
             total = jnp.dot(g0[at, :], halves[0][...], preferred_element_type=F32)
             return total + jnp.dot(g1[at, :], halves[1][...], preferred_element_type=F32)
 
-        for k in range(2):
-            pltpu.make_async_copy(halves[k], halves[k], sems.at[2 + k]).wait()
         steps = scatter_steps(branch, place, (out, via, from_x, from_y), s1, r1)
-        for _ in range(3):
-            next(steps)
+    else:
+        loads[0].start()
+        loads[1].start()
     for r in range(0, tokens, 256):
         do[r : r + 256, :] = dot_t(da[r : r + 256, :], wout[...]).astype(BF)
     ot = o[...].T
@@ -276,9 +321,16 @@
             ).start()
         return carry
 
-    lax.fori_loop(0, nb, store_out, 0)
+    if not moving:
+        lax.fori_loop(0, nb, store_out, 0)
     if moving:
-        next(steps)
+        exchange(3, piece_out)
+        for k in range(2):
+            loads[2 + k].wait()
+            pltpu.make_async_copy(halves[k], halves[k], sems.at[2 + k]).wait()
+        for _ in range(3):
+            next(steps)
+    loads[0].wait()
 
     def head(h, carry):
         at = h * HEAD_DIM
@@ -303,11 +355,10 @@
         return carry
 
     lax.fori_loop(0, share // HEAD_DIM, head, 0)
+    loads[1].wait()
     if moving:
         next(steps)
-        fourth = rows // 4
-        for part, total in enumerate(next(steps)):
-            branch_sum[part * fourth : (part + 1) * fourth, :] = total
+        next(steps)
     wide = min(512, 3 * share)
 
     def weights(j, carry):
@@ -319,6 +370,22 @@
             ).astype(BF)
         return carry
 
+    if moving:
+        for t in range(3):
+            weights(t, 0)
+            exchange(t, piece_qkv(t))
+        combine(3, piece_out)
+        size = upper_rows(rows) // 2
+        for part, total in enumerate(next(steps)):
+            branch_sum[part * size : (part + 1) * size, :] = total
+        for t in range(3):
+            combine(t, piece_qkv(t))
+        line.stop()
+        mine = pltpu.make_async_copy(own.at[line.chip], line.held.at[0], sems.at[2])
+        mine.start()
+        mine.wait()
+        sums[...] = (line.held[0].astype(F32) + got[0].astype(F32) + got[1].astype(F32)).astype(BF)
+        return
     lax.fori_loop(0, 3 * share // wide, weights, 0)
 
     def store(k, c):
@@ -332,14 +399,7 @@
         return c
 
     lax.fori_loop(0, ns * nb, store, 0)
-    if moving:
-        line.stop()
-        mine = pltpu.make_async_copy(own.at[line.chip], line.held.at[0], sems.at[2])
-        mine.start()
-        mine.wait()
-        sums[...] = (line.held[0].astype(F32) + got[0].astype(F32) + got[1].astype(F32)).astype(BF)
-    stored = gw.at[:, : 3 * share]
-    pltpu.make_async_copy(stored, stored, sems.at[1]).wait()
+    pltpu.make_async_copy(gw, gw, sems.at[1]).wait()
     pltpu.make_async_copy(gwo, gwo, sems.at[0]).wait()
 
 
@@ -353,25 +413,29 @@
     extra, scratch = (), []
     if moving:
         prior = more[1]
-        extra = jax.ShapeDtypeStruct(prior.shape[1:], BF), jax.ShapeDtypeStruct((rows // 2, width), F32)
-        scratch = scatter_scratch(rows // 2, width) + [pltpu.VMEM(prior.shape, BF)] + line_scratch(*prior.shape[1:])
+        extra = jax.ShapeDtypeStruct(prior.shape[1:], BF), jax.ShapeDtypeStruct((upper_rows(rows), width), F32)
+        scratch = [pltpu.VMEM(one.shape, BF) for one in more[2:4]]
+        scratch += [pltpu.VMEM((nb // 2, 4 * width // nb, share), BF)] + [pltpu.SemaphoreType.DMA((4,))] * 2
+        scratch += scatter_scratch(upper_rows(rows), width) + [pltpu.VMEM(prior.shape, BF)] + line_scratch(*prior.shape[1:])
     return pl.pallas_call(
         functools.partial(attend_back_kernel, ns, nb, moving),
         out_shape=(
-            jax.ShapeDtypeStruct((nb, 4 * width // nb, share), BF),
+            jax.ShapeDtypeStruct((nb // 2 if moving else nb, 4 * width // nb, share), BF),
             jax.ShapeDtypeStruct((tokens, 3 * share), BF),
             jax.ShapeDtypeStruct((1, 3 * share), F32),
         )
         + extra,
-        in_specs=[pl.BlockSpec(memory_space=pltpu.SMEM), vm, vm, vm, vm, vm] + [hbm, vm, vm, vm, hbm, hbm][: len(more)],
-        out_specs=(hbm, vm, vm) + (vm,) * len(extra),
+        in_specs=[pl.BlockSpec(memory_space=pltpu.SMEM), hbm, vm, vm, vm, hbm] + [hbm, vm, hbm, hbm, hbm, hbm][: len(more)],
+        out_specs=(vm if moving else hbm, vm, vm) + (vm,) * len(extra),
         scratch_shapes=[
             pltpu.VMEM((tokens, share), BF),
             pltpu.VMEM((width, width if moving else 3 * share), BF),
             pltpu.VMEM((share, width), BF),
             pltpu.VMEM((tokens, HEAD_DIM), F32),
             pltpu.VMEM((tokens, HEAD_DIM), F32),
-            pltpu.SemaphoreType.DMA((4,)),
+            pltpu.SemaphoreType.DMA((8,)),
+            pltpu.VMEM((width, tokens), BF),
+            pltpu.VMEM((tokens, 3 * share), BF),
         ]
         + scratch,
         compiler_params=pltpu.CompilerParams(
@@ -543,13 +607,15 @@
 def ff_kernel(ns, nb, first, moving, *refs):
     line = None
     if first:
-        h2, cot, wg, bias, gwg, g_out, du_out, gb, h2t, dh2, w1, w2, gw1, gw2, sems = refs
+        h2_in, cot_in, wg, bias, gwg, g_out, du_out, gb, h2t, dh2, w1, w2, gw1, gw2, h2, cot, u_part, sems = refs
     elif moving:
-        h2, h2t, cot, wg, bias, own, gwg, g_out, du_out, gb, got, w1, w2, gw1, gw2, sems, held, s0, s1, s2 = refs
+        h2_in, h2t_in, cot_in, wg, bias, own, gwg, g_out, du_out, gb, got, *refs = refs
+        w1, w2, gw1, gw2, h2, cot, u_part, sems, h2t, held, s0, s1, s2 = refs
         line = Line(0, own, None, got, held, s0, s1, s2)
     else:
-        h2, h2t, cot, wg, bias, gwg, g_out, du_out, gb, w1, w2, gw1, gw2, sems = refs
-    tokens, width = h2.shape
+        h2_in, h2t_in, cot_in, wg, bias, gwg, g_out, du_out, gb, *refs = refs
+        w1, w2, gw1, gw2, h2, cot, u_part, sems, h2t = refs
+    tokens, width = h2_in.shape
     chunk = g_out.shape[1]
     depth = width // (ns * nb)
     part = chunk // nb
@@ -575,8 +641,15 @@
             ).start()
         return carry
 
+    first_load = pltpu.make_async_copy(h2_in, h2, sems.at[4])
+    first_load.start()
     lax.fori_loop(0, ns * nb, load1, 0)
+    second_load = pltpu.make_async_copy(cot_in, cot, sems.at[5])
+    second_load.start()
     lax.fori_loop(0, nb, load2, 0)
+    if not first:
+        third_load = pltpu.make_async_copy(h2t_in, h2t, sems.at[6])
+        third_load.start()
     if moving:
         line.ready()
         barrier = pltpu.get_barrier_semaphore()
@@ -584,11 +657,11 @@
             pl.semaphore_signal(barrier, inc=1, device_id=other, device_id_type=MESH)
         pl.semaphore_wait(barrier, 2)
         line.go()
+    first_load.wait()
     if first:
         for r in range(0, tokens, step):
             h2t[:, r : r + step] = h2[r : r + step, :].T
     pltpu.make_async_copy(w1, w1, sems.at[0]).wait()
-    pltpu.make_async_copy(w2, w2, sems.at[1]).wait()
 
     def one_tile(j, carry):
         at = pl.multiple_of(j * tile, tile)
@@ -596,11 +669,18 @@
         total = jnp.zeros((1, tile), F32)
         for r in range(0, tokens, step):
             rows = slice(r, r + step)
-            u = jnp.dot(h2[rows, :], w1[:, cols], preferred_element_type=F32) + bias[:, cols]
-            dg = lax.dot_general(
-                cot[rows, :], w2[cols, :], (((1,), (1,)), ((), ())), preferred_element_type=F32
-            )
-            g, du = slopes(u, dg)
+            u_part[rows, :] = jnp.dot(h2[rows, :], w1[:, cols], preferred_element_type=F32) + bias[:, cols]
+
+        @pl.when(j == 0)
+        def _():
+            second_load.wait()
+            pltpu.make_async_copy(w2, w2, sems.at[1]).wait()
+            if not first:
+                third_load.wait()
+
+        for r in range(0, tokens, step):
+            rows = slice(r, r + step)
+            g, du = slopes(u_part[rows, :], dot_t(cot[rows, :], w2[cols, :]))
             g_out[rows, cols] = g
             du_out[rows, cols] = du
             total += jnp.sum(du.astype(F32), 0, keepdims=True)
@@ -667,17 +747,22 @@
         given += (own,)
         extra = (jax.ShapeDtypeStruct((2,) + own.shape[1:], BF),)
         more = line_scratch(*own.shape[1:])
+    if not first:
+        more = [pltpu.VMEM((width, tokens), BF)] + more
     return pl.pallas_call(
         functools.partial(ff_kernel, ns, nb, first, moving),
         out_shape=(jax.ShapeDtypeStruct(wg.shape, BF), inner, inner, jax.ShapeDtypeStruct((1, chunk), F32)) + extra,
-        in_specs=[hbm if one is wg or one is own else vm for one in given],
+        in_specs=[vm if one is bias else hbm for one in given],
         out_specs=(hbm,) + (vm,) * (3 + len(extra)),
         scratch_shapes=[
             pltpu.VMEM((width, chunk), BF),
             pltpu.VMEM((chunk, width), BF),
             pltpu.VMEM((chunk // tile, width, tile), BF),
             pltpu.VMEM((chunk // tile, tile, width), BF),
-            pltpu.SemaphoreType.DMA((4,)),
+            pltpu.VMEM((tokens, width), BF),
+            pltpu.VMEM((tokens, width), BF),
+            pltpu.VMEM((tokens, tile), F32),
+            pltpu.SemaphoreType.DMA((7,)),
         ]
         + more,
         compiler_params=pltpu.CompilerParams(
@@ -834,15 +919,20 @@
     )(o, wout, mine, obias, gain, shift)
 
 
-def ff_back_kernel(ns, nb, du, wg, before, x1, cot, gain, own, prior, *refs):
-    dx1, da, sums, got, w, load_sem, out, via, from_x, from_y, s1, r1, s2, r2, *moving = refs
+def ff_back_kernel(ns, nb, du, wg, before_in, x1_in, cot_in, gain, own, prior, *refs):
+    dx1, da, sums, got, before, x1, cot, loads, w, load_sem, out, via, from_x, from_y, s1, r1, s2, r2, *moving = refs
     line = Line(1, own, prior, got, *moving)
     rows, width = x1.shape
     half = rows // 2
     load_rows(ns, nb, width // (ns * nb), wg, w, load_sem)
+    pairs = (before_in, before), (x1_in, x1), (cot_in, cot)
+    copies = [pltpu.make_async_copy(src, dst, loads.at[k]) for k, (src, dst) in enumerate(pairs)]
+    for one in copies:
+        one.start()
     line.ready()
     place = greet(line.neighbours())
     pltpu.make_async_copy(w, w, load_sem).wait()
+    copies[0].wait()
 
     def partial(block):
         at = pl.multiple_of(block * rows, rows)
@@ -852,6 +942,8 @@
     next(steps)
     line.go()
     *_, halves = steps
+    copies[1].wait()
+    copies[2].wait()
     totals = [jnp.zeros((1, width), F32)] * 3
     for part, grad in enumerate(halves):
         span = slice(part * half, part * half + half)
@@ -885,9 +977,10 @@
             jax.ShapeDtypeStruct((3, width), F32),
             jax.ShapeDtypeStruct(prior.shape, BF),
         ),
-        in_specs=[vm, hbm] + [vm] * 4 + [hbm, vm],
+        in_specs=[vm] + [hbm] * 4 + [vm, hbm, vm],
         out_specs=(vm,) * 4,
-        scratch_shapes=[pltpu.VMEM((width, chunk), BF), pltpu.SemaphoreType.DMA]
+        scratch_shapes=[pltpu.VMEM(before.shape, BF), pltpu.VMEM((rows, width), F32), pltpu.VMEM((rows, width), BF)]
+        + [pltpu.SemaphoreType.DMA((3,)), pltpu.VMEM((width, chunk), BF), pltpu.SemaphoreType.DMA]
         + scatter_scratch(rows, width)
         + GATHER_SEMS
         + line_scratch(*prior.shape[1:]),
@@ -904,7 +997,7 @@
     load, s0, r0, *buffers = refs[4 * count + 8 :]
     buffers, more = buffers[:6], buffers[6:]
     rows, width = mine.shape
-    half = rows // 2
+    half, cut = rows // 2, upper_rows(rows)
     chunk = summed[0].shape[1]
     part_rows, pieces = chunk // nb, width // chunk
     load_attention(ns, nb, wq, w, load.at[0])
@@ -939,7 +1032,7 @@
         return dot_t(dproj[pl.ds(at, rows), :], w[...])
 
     def branch(block):
-        at = pl.ds(pl.multiple_of(block * rows + half, half), half)
+        at = pl.ds(pl.multiple_of(block * rows + cut, rows - cut), rows - cut)
         total = jnp.dot(gs[0][at, :], ws[0][...], preferred_element_type=F32)
         for c in range(1, count):
             total += jnp.dot(gs[c][at, :], ws[c][...], preferred_element_type=F32)
@@ -970,7 +1063,8 @@
         gains[k : k + 1, :] = totals[k]
     *_, lows = others_steps
     for part, total in enumerate(lows):
-        low_sum[part * half // 2 : (part + 1) * half // 2, :] = total
+        size = (rows - cut) // 2
+        low_sum[part * size : (part + 1) * size, :] = total
     pltpu.make_async_copy(gw2, gw2, load.at[2]).wait()
     strip = stage.at[:, :hidden]
     pltpu.make_async_copy(strip, strip, load.at[1]).wait()
@@ -994,7 +1088,7 @@
             jax.ShapeDtypeStruct((2, width), F32),
             jax.ShapeDtypeStruct((depth, hidden * ns), BF),
             jax.ShapeDtypeStruct((hidden // nb, width), BF),
-            jax.ShapeDtypeStruct((rows // 2, width), F32),
+            jax.ShapeDtypeStruct((rows - upper_rows(rows), width), F32),
         ),
         in_specs=[vm, hbm] + [hbm] * count + [vm] * count + [hbm] * count + [vm] * 2,
         out_specs=(vm,) * 5,
@@ -1002,7 +1096,7 @@
         + [pltpu.VMEM((chunk, width), BF)] * count
         + [dma((3 + count,)), dma((ns - 1,)), dma((ns - 1,))]
         + scatter_scratch(rows, width)
-        + scatter_scratch(rows // 2, width),
+        + scatter_scratch(rows - upper_rows(rows), width),
         compiler_params=pltpu.CompilerParams(collective_id=3, has_side_effects=True, vmem_limit_bytes=56 * 2**20),
         cost_estimate=pl.CostEstimate(flops=40 * 10**9, bytes_accessed=24 * rows * width, transcendentals=0),
         name="finish",
@@ -1296,6 +1390,13 @@
     return lax.psum_scatter(flat, "batch", scatter_dimension=0, tiled=True)
 
 
+def scatter_chips(parts):
+    count = lax.axis_size("batch")
+    groups = [list(range(core, count, 2)) for core in range(2)]
+    flat = parts.reshape(-1, parts.shape[-1])
+    return lax.psum_scatter(flat, "batch", scatter_dimension=0, tiled=True, axis_index_groups=groups)
+
+
 def unpermute(ns, nb, gathered):
     depth = gathered.shape[1] // ns
     return gathered.reshape(nb, ns, depth, -1).transpose(1, 0, 2, 3).reshape(ns * nb * depth, -1)
@@ -1417,7 +1518,7 @@
     gattn, dproj, gqv, *more = attend_back(ns, nb, lengths, h1t, da, wout, o, qkv, *line)
     if planar:
         gws[0], y = more
-    gattn = scatter_batch(gattn)
+    gattn = scatter_chips(gattn) if planar else scatter_batch(gattn)
     if planar:
         gx, rows1, gw1, gw2, lower = finish(ns, nb, dproj, wq, gws, gs, wgs, mine, gain1)
         gx, rows2, gqv, gb1, cot_mine, y = lax.optimization_barrier((gx, rows2, gqv, gb1, cot_mine, y))

time: 572 us -> 561 us (0.981)
  Pallas kernels: 502 us -> 496 us
    pallas_call x1, Pallas kernels: 74.9 us -> 66.4 us  [finish(): pl.pallas_call(functools.partial(finish_kernel, ns, nb, count), out_shape...]
where the time goes in v5:
time: 561 us; the launch traced here: 552 us
  Pallas kernels  496 us (88%)
  local copies, waits for them, and re-layouts  19.2 us (3%)
  between operations  15.7 us (3%)
  waiting for transfers between devices  11.8 us (2%)
  other arithmetic  9.71 us (2%)
    pallas_call x1, Pallas kernels, ff_back(): pl.pallas_call(functools.partial(ff_back_kernel, ns, nb), out_shape=(jax....  86.2 us
    pallas_call x1, Pallas kernels, middle(): pl.pallas_call(middle_kernel, out_shape=(jax.ShapeDtypeStruct((rows, widt...  77.8 us
    pallas_call x1, Pallas kernels, collect(): pl.pallas_call(functools.partial(collect_kernel, ns, nb), out_shape=(full...  72.5 us
    pallas_call x1, Pallas kernels, finish(): pl.pallas_call(functools.partial(finish_kernel, ns, nb, count), out_shape...  66.4 us
    pallas_call x1, Pallas kernels, attend_back(): pl.pallas_call(functools.partial(attend_back_kernel, ns, nb, moving), out...  48 us
    pallas_call x1, Pallas kernels, ff_first(): pl.pallas_call(functools.partial(ff_first_kernel, ns, nb), out_shape=(jax...  38.9 us
    pallas_call x1, Pallas kernels, ff_chunk(): pl.pallas_call(functools.partial(ff_kernel, ns, nb, first, moving), out_s...  34.1 us
    pallas_call x1, Pallas kernels, attend(): pl.pallas_call(functools.partial(attend_kernel, ns, nb), out_shape=(jax.S...  22 us
  transfers between devices with their start and end apart: 6, of which 3 were waited for; matrix products, arithmetic and copies ran while one was open for 3% of the time, Pallas kernels for 80%

profile of v5, /device:TPU:0, one launch (start us, length us, event | category | flops | bytes accessed | tf_op | source)
XLA Modules:
  0.0 552.3 jit_solution(14078293803423614786)
XLA Ops:
  7.2 0.7 all-gather.5.cloned.1.call-update
  8.0 13.8 %spread.1 = bf16[768,512]{1,0:T(8,128)(2,1)} custom-call(bf16[64,6144]{1,0:T(8,128)(2,1)} %w_qkv.1), custom_call_target="tpu_custom_call" | custom-call | flops 1000000 | bytes 10000 | tf_op jit(solution)/shard_map/spread/pallas_call | solution.py:1152
  22.0 17.6 %spread_ff.1 = (bf16[512,1024]{1,0:T(8,128)(2,1)}, bf16[512,1024]{1,0:T(8,128)(2,1)}) custom-call(bf16[64,8192]{1,0:T(8,128)(2,1)} %w1, bf16[256,2048]{1,0:T(8,128)(2,1)} %w2.1), custom_call_target="tpu_custom_call" | custom-call | flops 1000000 | bytes 10000 | tf_op jit(solution)/shard_map/spread_ff/pallas_call | solution.py:1197
  39.6 1.8 all-gather.5.cloned.1.call-done.wout
  41.5 0.5 all-gather.11.cloned.1.call-update
  42.9 0.1 concatenate.20
  43.0 72.5 %collect.1 = (bf16[1024,2048]{1,0:T(8,128)(2,1)S(1)}, bf16[1024,2048]{1,0:T(8,128)(2,1)S(1)}, f32[8,4,8,128]{3,2,1,0:T(8,128)S(1)}) custom-call(bf16[256,2048]{1,0:T(8,128)(2,1)S(1)} %bitcast.63, bf16[256,2048]{1,0:T(8,128)(2,1)S(1)} %bitcast.59, f32[8,128]{1,0:T(8,128)S(1)} %bitcast_convert_fusion.vec), custom_call_target="tpu_custom_call" | custom-call | flops 1000000 | bytes 10000 | tf_op jit(solution)/shard_map/collect/pallas_call | solution.py:1292
  115.5 2.1 copy-done
  117.6 2.0 copy-done.4
  119.7 0.1 fusion.3
  119.7 0.7 reshape.117.gain
  120.4 0.7 reshape.116.obias
  121.1 0.7 reshape.118.shift
  121.8 0.1 slice_bitcast_fusion
  121.9 0.7 reshape.122.refs_7_
  122.6 0.7 reshape.123
  123.3 0.6 fusion.2.bias
  123.9 0.6 slice_bitcast_fusion.1
  124.5 22.0 %attend.1 = (bf16[1024,1536]{1,0:T(8,128)(2,1)}, bf16[1024,512]{1,0:T(8,128)(2,1)}, bf16[2048,1024]{1,0:T(8,128)(2,1)}) custom-call(s32[1]{0:T(128)S(6)} %copy.51.length, bf16[1024,2048]{1,0:T(8,128)(2,1)} %copy-done, bf16[8,768,512]{2,1,0:T(8,128)(2,1)} %bitcast.65, f32[1,1536]{1,0:T(1,128)} %fusion.2.bias), custom_call_target="tpu_custom_call" | custom-call | flops 1000000 | bytes 10000 | tf_op jit(solution)/shard_map/attend/pallas_call | solution.py:214
  146.5 77.8 %project_out.1 = (f32[256,2048]{1,0:T(8,128)}, bf16[1024,2048]{1,0:T(8,128)(2,1)}) custom-call(bf16[1024,512]{1,0:T(8,128)(2,1)} %get-tuple-element.95.o, bf16[512,2048]{1,0:T(8,128)(2,1)} %all-gather.5.cloned.1.call-done.wout, bf16[256,2048]{1,0:T(8,128)(2,1)} %bitcast.61, f32[1,2048]{1,0:T(1,128)} %reshape.116.obias, f32[1,2048]{1,0:T(1,128)} %reshape.117.gain, ...), custom_call_target="tpu_custom_call" | custom-call | flops 40000000000 | bytes 25165824 | tf_op jit(solution)/shard_map/project_out/pallas_call | solution.py:910
  224.4 38.9 %ff_first.1 = (bf16[4,512,1024]{2,1,0:T(8,128)(2,1)}, bf16[1024,1024]{1,0:T(8,128)(2,1)}, bf16[1024,1024]{1,0:T(8,128)(2,1)}, f32[1,1024]{1,0:T(1,128)}, bf16[20...) custom-call(bf16[1024,2048]{1,0:T(8,128)(2,1)} %get-tuple-element.97.h2.refs_0_, bf16[1024,2048]{1,0:T(8,128)(2,1)} %copy-done.4, ...), custom_call_target="tpu_custom_call" | custom-call | flops 40000000000 | bytes 33554432 | tf_op jit(solution)/shard_map/ff_first/pallas_call | solution.py:576
  263.3 8.5 %all-gather.11.cloned.1.call-done = bf16[4096,1024]{1,0:T(8,128)(2,1)} async-done(((bf16[512,1024]{1,0:T(8,128)(2,1)}), bf16[4096,1024]{1,0:T(8,128)(2,1)}) %all-gather.11.cloned.1.call-update) | async-done | bytes 8388624 | tf_op jit(solution)/shard_map/all_gather | solution.py:1480
  271.8 34.1 %ff_chunk.1 = (bf16[8,512,1024]{2,1,0:T(8,128)(2,1)}, bf16[1024,1024]{1,0:T(8,128)(2,1)}, bf16[1024,1024]{1,0:T(8,128)(2,1)}, f32[1,1024]{1,0:T(1,128)}, bf16[2,512,1024]{2,1,0:T(8,128)(2,1)}) custom-call(bf16[1024,2048]{1,0:T(8,128)(2,1)} %get-tuple-element.97.h2.refs_0_, bf16[2048,1024]{1,0:T(8,128)(2,1)} %get-tuple-element.101.refs_1_, ...), custom_call_target="tpu_custom_call" | custom-call | flops 40000000000 | bytes 16777216 | tf_op jit(solution)/shard_map/ff_chunk/pallas_call | solution.py:752
  306.0 86.2 %ff_back.1 = (f32[256,2048]{1,0:T(8,128)}, bf16[1024,2048]{1,0:T(8,128)(2,1)}, f32[3,2048]{1,0:T(4,128)}, bf16[2,512,1024]{2,1,0:T(8,128)(2,1)}) custom-call(bf16[1024,1024]{1,0:T(8,128)(2,1)} %get-tuple-element.104.du, bf16[8,512,1024]{2,1,0:T(8,128)(2,1)} %bitcast.92, bf16[1024,2048]{1,0:T(8,128)(2,1)} %get-tuple-element.105.before_in, ...), custom_call_target="tpu_custom_call" | custom-call | flops 40000000000 | bytes 25165824 | tf_op jit(solution)/shard_map/ff_back/pallas_call | solution.py:972
  392.3 48.0 %attend_back.1 = (bf16[4,1024,512]{2,1,0:T(8,128)(2,1)}, bf16[1024,1536]{1,0:T(8,128)(2,1)}, f32[1,1536]{1,0:T(1,128)}, bf16[512,1024]{1,0:T(8,128)(2,1)}, f32[192,2048]{1,0:T(8,128)}) custom-call(s32[1]{0:T(128)S(6)} %copy.51.length, bf16[2048,1024]{1,0:T(8,128)(2,1)} %get-tuple-element.94.h1t_in, bf16[1024,2048]{1,0:T(8,128)(2,1)} %get-tuple-element.109.da, ...), custom_call_target="tpu_custom_call" | custom-call | flops 40000000000 | bytes 12582912 | tf_op jit(solution)/shard_map/attend_back/pallas_call | solution.py:420
  440.3 66.4 %finish.1 = (f32[256,2048]{1,0:T(8,128)}, f32[2,2048]{1,0:T(2,128)}, bf16[64,8192]{1,0:T(8,128)(2,1)}, bf16[256,2048]{1,0:T(8,128)(2,1)}, f32[64,2048]{1,0:T(8,128)}) custom-call(bf16[1024,1536]{1,0:T(8,128)(2,1)} %get-tuple-element.114.dproj, bf16[8,768,512]{2,1,0:T(8,128)(2,1)} %bitcast.66, bf16[512,1024]{1,0:T(8,128)(2,1)} %get-tuple-element.115.refs_0_, ...), custom_call_target="tpu_custom_call" | custom-call | flops 40000000000 | bytes 12582912 | tf_op jit(solution)/shard_map/finish/pallas_call | solution.py:1084
  506.8 2.8 convert_element_type.25
  509.7 1.6 convert_element_type.26
  511.2 1.1 copy-done.5
  512.3 1.5 fusion.1
  513.9 0.1 reshape.134
  514.0 0.3 dynamic_update_slice.11
  514.3 0.1 reshape.130
  514.4 0.1 reshape.131
  514.5 0.1 reshape.126
  514.7 0.1 reshape.127
  514.8 3.2 add.43
  517.9 0.3 dynamic_update_slice.9
  518.2 0.3 dynamic_update_slice.10
  518.5 0.1 concatenate.25
  518.6 0.7 copy_bitcast_fusion.2.sums
  519.3 0.1 reduce-scatter.5.cloned.1.call-done.summed
  519.4 18.2 %home.1 = (f32[64,6144]{1,0:T(8,128)}, f32[64,2048]{1,0:T(8,128)}, f32[8,128]{1,0:T(8,128)}) custom-call(bf16[1024,512]{1,0:T(8,128)(2,1)} %reduce-scatter.5.cloned.1.call-done.summed, f32[8,4,8,128]{3,2,1,0:T(8,128)} %copy_bitcast_fusion.2.sums), custom_call_target="tpu_custom_call" | custom-call | flops 5000000000 | bytes 2097152 | tf_op jit(solution)/shard_map/home/pallas_call | solution.py:1349
  537.5 1.5 fusion.5
  539.0 1.3 slice.93
  540.3 1.2 slice_bitcast_fusion.3
  541.5 2.7 copy.52
  544.2 0.8 copy.53
  (80 shorter events, 0.7 us)
Async XLA Ops:
  7.2 34.3 %all-gather.5.cloned.1.call-start = ((), (), s32[]{:S(2)}) async-start(), calls=%async_computation.2 | async-start | bytes 2359296 | tf_op jit(solution)/shard_map/all_gather | solution.py:1441
  7.9 116.6 %all-gather.7.cloned.1.call-start = ((), (), s32[]{:S(2)}) async-start(), calls=%async_computation.3 | async-start | bytes 7077888 | tf_op jit(solution)/shard_map/all_gather | solution.py:1458
  21.8 21.0 %copy-start.17 = (bf16[64]{0:T(256)(128)(2,1)S(1)}, bf16[64]{0:T(256)(128)(2,1)}, u32[]{:S(2)}) copy-start(bf16[64]{0:T(256)(128)(2,1)} %param.17) | copy-start | bytes 388
  21.8 21.0 %copy-start.18 = (bf16[64]{0:T(256)(128)(2,1)S(1)}, bf16[64]{0:T(256)(128)(2,1)}, u32[]{:S(2)}) copy-start(bf16[64]{0:T(256)(128)(2,1)} %param.18) | copy-start | bytes 388
  21.9 21.0 %copy-start.19 = (bf16[128]{0:T(256)(128)(2,1)S(1)}, bf16[128]{0:T(256)(128)(2,1)}, u32[]{:S(2)}) copy-start(bf16[128]{0:T(256)(128)(2,1)} %param.20) | copy-start | bytes 772
  21.9 21.0 %copy-start.20 = (bf16[64]{0:T(256)(128)(2,1)S(1)}, bf16[64]{0:T(256)(128)(2,1)}, u32[]{:S(2)}) copy-start(bf16[64]{0:T(256)(128)(2,1)} %param.22) | copy-start | bytes 388
  21.9 21.0 %copy-start.21 = (bf16[64]{0:T(256)(128)(2,1)S(1)}, bf16[64]{0:T(256)(128)(2,1)}, u32[]{:S(2)}) copy-start(bf16[64]{0:T(256)(128)(2,1)} %param.23) | copy-start | bytes 388
  21.9 20.9 %copy-start.22 = (bf16[64]{0:T(256)(128)(2,1)S(1)}, bf16[64]{0:T(256)(128)(2,1)}, u32[]{:S(2)}) copy-start(bf16[64]{0:T(256)(128)(2,1)} %param.24) | copy-start | bytes 388
  21.9 20.9 %copy-start.23 = (bf16[256]{0:T(256)(128)(2,1)S(1)}, bf16[256]{0:T(256)(128)(2,1)}, u32[]{:S(2)}) copy-start(bf16[256]{0:T(256)(128)(2,1)} %param.26) | copy-start | bytes 1540
  21.9 20.9 %copy-start.24 = (bf16[64]{0:T(256)(128)(2,1)S(1)}, bf16[64]{0:T(256)(128)(2,1)}, u32[]{:S(2)}) copy-start(bf16[64]{0:T(256)(128)(2,1)} %param.28) | copy-start | bytes 388
  21.9 21.0 %copy-start.1 = (bf16[1,256,2048]{2,1,0:T(8,128)(2,1)S(1)}, bf16[1,256,2048]{2,1,0:T(8,128)(2,1)}, u32[]{:S(2)}) copy-start(bf16[1,256,2048]{2,1,0:T(8,128)(2,1)} %param.29) | copy-start | bytes 3145732
  21.9 21.0 %copy-start.3 = (bf16[1,256,2048]{2,1,0:T(8,128)(2,1)S(1)}, bf16[1,256,2048]{2,1,0:T(8,128)(2,1)}, u32[]{:S(2)}) copy-start(bf16[1,256,2048]{2,1,0:T(8,128)(2,1)} %param.15) | copy-start | bytes 3145732
  21.9 202.4 %all-gather.9.cloned.1.call-start = ((), (), s32[]{:S(2)}) async-start(), calls=%async_computation.4 | async-start | bytes 9437184 | tf_op jit(solution)/shard_map/all_gather | solution.py:1480
  41.5 230.3 %all-gather.11.cloned.1.call-start = ((), (), s32[]{:S(2)}) async-start(), calls=%async_computation.5 | async-start | bytes 9437184 | tf_op jit(solution)/shard_map/all_gather | solution.py:1480
  42.0 398.3 %reduce-scatter.3.cloned.1.call-start = ((), (), s32[]{:S(2)}) async-start(), calls=%async_computation.6 | async-start | bytes 9437184 | tf_op jit(solution)/shard_map/reduce_scatter | solution.py:1390
  115.5 2.1 copy-start
  117.6 2.0 copy-start.4
  306.0 213.4 %reduce-scatter.5.cloned.1.call-start = ((), (), s32[]{:S(2)}) async-start(), calls=%async_computation.7 | async-start | bytes 5242880 | tf_op jit(solution)/shard_map/reduce_scatter | solution.py:1397
  506.8 2.9 copy-start.8
  506.8 4.4 copy-start.7
  506.8 4.4 copy-start.9
  506.8 4.4 copy-start.11
  509.6 1.6 copy-start.2
  509.6 2.7 copy-start.5
  512.3 1.6 copy-start.14
  512.3 1.6 copy-start.15
  512.3 2.0 copy-start.12
  512.3 2.2 copy-start.13
  512.3 2.4 copy-start.6
  514.8 3.2 copy-start.16
  537.5 6.7 %copy-start.10 = (f32[64,2048]{1,0:T(8,128)S(1)}, f32[64,2048]{1,0:T(8,128)}, u32[]{:S(2)}) copy-start(f32[64,2048]{1,0:T(8,128)} %get-tuple-element.185) | copy-start | bytes 1572868
Sparse Core Ops, SparseCore 0:
  9.6 31.7 all-gather.4
  43.1 64.2 all-gather.6
  109.0 80.6 all-gather.8
  191.2 80.5 all-gather.10
  306.1 125.8 reduce-scatter.2
  440.4 78.9 reduce-scatter.4

commit v6 on v5

--- a/solution.py
+++ b/solution.py
@@ -644,12 +644,6 @@
     first_load = pltpu.make_async_copy(h2_in, h2, sems.at[4])
     first_load.start()
     lax.fori_loop(0, ns * nb, load1, 0)
-    second_load = pltpu.make_async_copy(cot_in, cot, sems.at[5])
-    second_load.start()
-    lax.fori_loop(0, nb, load2, 0)
-    if not first:
-        third_load = pltpu.make_async_copy(h2t_in, h2t, sems.at[6])
-        third_load.start()
     if moving:
         line.ready()
         barrier = pltpu.get_barrier_semaphore()
@@ -658,10 +652,16 @@
         pl.semaphore_wait(barrier, 2)
         line.go()
     first_load.wait()
+    pltpu.make_async_copy(w1, w1, sems.at[0]).wait()
+    second_load = pltpu.make_async_copy(cot_in, cot, sems.at[5])
+    second_load.start()
+    lax.fori_loop(0, nb, load2, 0)
+    if not first:
+        third_load = pltpu.make_async_copy(h2t_in, h2t, sems.at[6])
+        third_load.start()
     if first:
         for r in range(0, tokens, step):
             h2t[:, r : r + step] = h2[r : r + step, :].T
-    pltpu.make_async_copy(w1, w1, sems.at[0]).wait()
 
     def one_tile(j, carry):
         at = pl.multiple_of(j * tile, tile)
@@ -689,12 +689,6 @@
             gw1[j, r : r + 512, :] = jnp.dot(
                 h2t[r : r + 512, :], du_out[:, cols], preferred_element_type=F32
             ).astype(BF)
-        gt = g_out[:, cols].T
-        for r in range(0, width, 512):
-            gw2[j, :, r : r + 512] = jnp.dot(
-                gt, cot[:, r : r + 512], preferred_element_type=F32
-            ).astype(BF)
-
         def store1(k, c):
             s, b = k // nb, lax.rem(k, nb)
             pltpu.make_async_copy(
@@ -705,6 +699,11 @@
             return c
 
         lax.fori_loop(0, ns * nb, store1, 0)
+        gt = g_out[:, cols].T
+        for r in range(0, width, 512):
+            gw2[j, :, r : r + 512] = jnp.dot(
+                gt, cot[:, r : r + 512], preferred_element_type=F32
+            ).astype(BF)
         count = tile // part
 
         def store2(k, c):
@@ -777,18 +776,21 @@
     )(*given)
 
 
-def greet(more=()):
+def greet(more=(), later=False):
     me, batch = lax.axis_index("seq"), lax.axis_index("batch")
     by_x = me + 1 - 2 * lax.rem(me, 2)
     by_y = lax.rem(me + 2, 4)
     barrier = pltpu.get_barrier_semaphore()
     for other in [(by_x, batch), (by_y, batch), *more]:
         pl.semaphore_signal(barrier, inc=1, device_id=other, device_id_type=MESH)
+    place = me, by_x, by_y, (by_x, batch), (by_y, batch)
+    if later:
+        return place, lambda: pl.semaphore_wait(barrier, 2 + len(more))
     pl.semaphore_wait(barrier, 2 + len(more))
-    return me, by_x, by_y, (by_x, batch), (by_y, batch)
-
-
-def scatter_steps(partial, place, buffers, send, recv):
+    return place
+
+
+def scatter_steps(partial, place, buffers, send, recv, met=None, split=False):
     me, by_x, by_y, to_x, to_y = place
     out, via, from_x, from_y = buffers
     half = via.shape[1]
@@ -803,6 +805,8 @@
         return one
 
     out[0] = partial(far).astype(BF)
+    if met:
+        met()
     c0 = copy(0, out.at[0, top], via.at[0], to_y)
     c1 = copy(1, out.at[0, low], via.at[1], to_x)
     yield
@@ -828,12 +832,17 @@
     c3.wait_recv()
     c4.wait_recv()
     mine_top = mine[top] + from_x[top].astype(F32) + from_y[top].astype(F32)
+    if split:
+        yield mine_top
     c2.wait_recv()
     c5.wait_recv()
     mine_low = mine[low] + from_x[low].astype(F32) + from_y[low].astype(F32)
+    if split:
+        yield mine_low
     for one in (c0, c1, c2, c3, c4, c5):
         one.wait_send()
-    yield mine_top, mine_low
+    if not split:
+        yield mine_top, mine_low
 
 
 def scatter_sum(partial, place, buffers, send, recv):
@@ -860,8 +869,9 @@
         return send(at, at, send_sems.at[k], recv_sems.at[k], to)
 
     c0 = copy(0, me, 0, to_x)
+    c2 = copy(2, me, 0, to_y)
+    yield
     c3 = copy(3, me, 1, to_y)
-    c2 = copy(2, me, 0, to_y)
     c1 = copy(1, me, 1, to_x)
     yield
     c0.wait_recv()
@@ -930,7 +940,7 @@
     for one in copies:
         one.start()
     line.ready()
-    place = greet(line.neighbours())
+    place, met = greet(line.neighbours(), True)
     pltpu.make_async_copy(w, w, load_sem).wait()
     copies[0].wait()
 
@@ -938,14 +948,17 @@
         at = pl.multiple_of(block * rows, rows)
         return before[pl.ds(at, rows), :].astype(F32) + dot_t(du[pl.ds(at, rows), :], w[...])
 
-    steps = scatter_steps(partial, place, (out, via, from_x, from_y), s1, r1)
+    steps = scatter_steps(partial, place, (out, via, from_x, from_y), s1, r1, met, True)
     next(steps)
     line.go()
-    *_, halves = steps
+    for _ in range(4):
+        next(steps)
     copies[1].wait()
     copies[2].wait()
+    gather = gather_steps(da, rows, place, s2, r2)
     totals = [jnp.zeros((1, width), F32)] * 3
-    for part, grad in enumerate(halves):
+    for part in range(2):
+        grad = next(steps)
         span = slice(part * half, part * half + half)
         normed, rstd = norm_stats(x1[span, :])
         res = cot[span, :].astype(F32) + norm_back(grad, normed, rstd, gain[...])
@@ -953,13 +966,14 @@
         low = res.astype(BF)
         at = pl.multiple_of(place[0] * rows + part * half, half)
         da[pl.ds(at, half), :] = low
+        next(gather)
         for k, term in enumerate((low.astype(F32), grad * normed, grad)):
             totals[k] += jnp.sum(term, 0, keepdims=True)
-    gather = gather_steps(da, rows, place, s2, r2)
-    next(gather)
     for k in range(3):
         sums[k : k + 1, :] = totals[k]
     for _ in gather:
+        pass
+    for _ in steps:
         pass
     line.stop()
 

time: 561 us -> 559 us (level)
  no operation moved by 1% of the time
where the time goes in v6:
time: 559 us; the launch traced here: 550 us
  Pallas kernels  493 us (88%)
  local copies, waits for them, and re-layouts  19.2 us (3%)
  between operations  15.7 us (3%)
  waiting for transfers between devices  12 us (2%)
  other arithmetic  9.71 us (2%)
    pallas_call x1, Pallas kernels, ff_back(): pl.pallas_call(functools.partial(ff_back_kernel, ns, nb), out_shape=(jax....  86.1 us
    pallas_call x1, Pallas kernels, middle(): pl.pallas_call(middle_kernel, out_shape=(jax.ShapeDtypeStruct((rows, widt...  77.8 us
    pallas_call x1, Pallas kernels, collect(): pl.pallas_call(functools.partial(collect_kernel, ns, nb), out_shape=(full...  72.5 us
    pallas_call x1, Pallas kernels, finish(): pl.pallas_call(functools.partial(finish_kernel, ns, nb, count), out_shape...  66.3 us
    pallas_call x1, Pallas kernels, attend_back(): pl.pallas_call(functools.partial(attend_back_kernel, ns, nb, moving), out...  47.2 us
    pallas_call x1, Pallas kernels, ff_first(): pl.pallas_call(functools.partial(ff_first_kernel, ns, nb), out_shape=(jax...  38.9 us
    pallas_call x1, Pallas kernels, ff_chunk(): pl.pallas_call(functools.partial(ff_kernel, ns, nb, first, moving), out_s...  32.8 us
    pallas_call x1, Pallas kernels, attend(): pl.pallas_call(functools.partial(attend_kernel, ns, nb), out_shape=(jax.S...  22 us
  transfers between devices with their start and end apart: 6, of which 3 were waited for; matrix products, arithmetic and copies ran while one was open for 3% of the time, Pallas kernels for 80%

profile of v6, /device:TPU:0, one launch (start us, length us, event | category | flops | bytes accessed | tf_op | source)
XLA Modules:
  0.0 549.8 jit_solution(10386797664062193429)
XLA Ops:
  7.2 0.7 all-gather.5.cloned.1.call-update
  8.0 13.8 %spread.1 = bf16[768,512]{1,0:T(8,128)(2,1)} custom-call(bf16[64,6144]{1,0:T(8,128)(2,1)} %w_qkv.1), custom_call_target="tpu_custom_call" | custom-call | flops 1000000 | bytes 10000 | tf_op jit(solution)/shard_map/spread/pallas_call | solution.py:1166
  22.0 17.6 %spread_ff.1 = (bf16[512,1024]{1,0:T(8,128)(2,1)}, bf16[512,1024]{1,0:T(8,128)(2,1)}) custom-call(bf16[64,8192]{1,0:T(8,128)(2,1)} %w1, bf16[256,2048]{1,0:T(8,128)(2,1)} %w2.1), custom_call_target="tpu_custom_call" | custom-call | flops 1000000 | bytes 10000 | tf_op jit(solution)/shard_map/spread_ff/pallas_call | solution.py:1211
  39.6 1.8 all-gather.5.cloned.1.call-done.wout
  41.5 0.5 all-gather.11.cloned.1.call-update
  42.9 0.1 concatenate.20
  43.0 72.5 %collect.1 = (bf16[1024,2048]{1,0:T(8,128)(2,1)S(1)}, bf16[1024,2048]{1,0:T(8,128)(2,1)S(1)}, f32[8,4,8,128]{3,2,1,0:T(8,128)S(1)}) custom-call(bf16[256,2048]{1,0:T(8,128)(2,1)S(1)} %bitcast.63, bf16[256,2048]{1,0:T(8,128)(2,1)S(1)} %bitcast.59, f32[8,128]{1,0:T(8,128)S(1)} %bitcast_convert_fusion.vec), custom_call_target="tpu_custom_call" | custom-call | flops 1000000 | bytes 10000 | tf_op jit(solution)/shard_map/collect/pallas_call | solution.py:1306
  115.5 2.1 copy-done
  117.6 2.0 copy-done.4
  119.7 0.1 fusion.3
  119.7 0.7 reshape.117.gain
  120.4 0.7 reshape.116.obias
  121.1 0.7 reshape.118.shift
  121.8 0.1 slice_bitcast_fusion
  121.9 0.7 reshape.122.refs_7_
  122.6 0.7 reshape.123
  123.3 0.6 fusion.2.bias
  123.9 0.6 slice_bitcast_fusion.1
  124.5 22.0 %attend.1 = (bf16[1024,1536]{1,0:T(8,128)(2,1)}, bf16[1024,512]{1,0:T(8,128)(2,1)}, bf16[2048,1024]{1,0:T(8,128)(2,1)}) custom-call(s32[1]{0:T(128)S(6)} %copy.51.length, bf16[1024,2048]{1,0:T(8,128)(2,1)} %copy-done, bf16[8,768,512]{2,1,0:T(8,128)(2,1)} %bitcast.65, f32[1,1536]{1,0:T(1,128)} %fusion.2.bias), custom_call_target="tpu_custom_call" | custom-call | flops 1000000 | bytes 10000 | tf_op jit(solution)/shard_map/attend/pallas_call | solution.py:214
  146.5 77.8 %project_out.1 = (f32[256,2048]{1,0:T(8,128)}, bf16[1024,2048]{1,0:T(8,128)(2,1)}) custom-call(bf16[1024,512]{1,0:T(8,128)(2,1)} %get-tuple-element.95.o, bf16[512,2048]{1,0:T(8,128)(2,1)} %all-gather.5.cloned.1.call-done.wout, bf16[256,2048]{1,0:T(8,128)(2,1)} %bitcast.61, f32[1,2048]{1,0:T(1,128)} %reshape.116.obias, f32[1,2048]{1,0:T(1,128)} %reshape.117.gain, ...), custom_call_target="tpu_custom_call" | custom-call | flops 40000000000 | bytes 25165824 | tf_op jit(solution)/shard_map/project_out/pallas_call | solution.py:920
  224.4 38.9 %ff_first.1 = (bf16[4,512,1024]{2,1,0:T(8,128)(2,1)}, bf16[1024,1024]{1,0:T(8,128)(2,1)}, bf16[1024,1024]{1,0:T(8,128)(2,1)}, f32[1,1024]{1,0:T(1,128)}, bf16[20...) custom-call(bf16[1024,2048]{1,0:T(8,128)(2,1)} %get-tuple-element.97.h2.refs_0_, bf16[1024,2048]{1,0:T(8,128)(2,1)} %copy-done.4, ...), custom_call_target="tpu_custom_call" | custom-call | flops 40000000000 | bytes 33554432 | tf_op jit(solution)/shard_map/ff_first/pallas_call | solution.py:576
  263.3 8.5 %all-gather.11.cloned.1.call-done = bf16[4096,1024]{1,0:T(8,128)(2,1)} async-done(((bf16[512,1024]{1,0:T(8,128)(2,1)}), bf16[4096,1024]{1,0:T(8,128)(2,1)}) %all-gather.11.cloned.1.call-update) | async-done | bytes 8388624 | tf_op jit(solution)/shard_map/all_gather | solution.py:1494
  271.8 32.8 %ff_chunk.1 = (bf16[8,512,1024]{2,1,0:T(8,128)(2,1)}, bf16[1024,1024]{1,0:T(8,128)(2,1)}, bf16[1024,1024]{1,0:T(8,128)(2,1)}, f32[1,1024]{1,0:T(1,128)}, bf16[2,512,1024]{2,1,0:T(8,128)(2,1)}) custom-call(bf16[1024,2048]{1,0:T(8,128)(2,1)} %get-tuple-element.97.h2.refs_0_, bf16[2048,1024]{1,0:T(8,128)(2,1)} %get-tuple-element.101.refs_1_, ...), custom_call_target="tpu_custom_call" | custom-call | flops 40000000000 | bytes 16777216 | tf_op jit(solution)/shard_map/ff_chunk/pallas_call | solution.py:751
  304.7 86.1 %ff_back.1 = (f32[256,2048]{1,0:T(8,128)}, bf16[1024,2048]{1,0:T(8,128)(2,1)}, f32[3,2048]{1,0:T(4,128)}, bf16[2,512,1024]{2,1,0:T(8,128)(2,1)}) custom-call(bf16[1024,1024]{1,0:T(8,128)(2,1)} %get-tuple-element.104.du, bf16[8,512,1024]{2,1,0:T(8,128)(2,1)} %bitcast.92, bf16[1024,2048]{1,0:T(8,128)(2,1)} %get-tuple-element.105.before_in, ...), custom_call_target="tpu_custom_call" | custom-call | flops 40000000000 | bytes 25165824 | tf_op jit(solution)/shard_map/ff_back/pallas_call | solution.py:986
  390.8 47.2 %attend_back.1 = (bf16[4,1024,512]{2,1,0:T(8,128)(2,1)}, bf16[1024,1536]{1,0:T(8,128)(2,1)}, f32[1,1536]{1,0:T(1,128)}, bf16[512,1024]{1,0:T(8,128)(2,1)}, f32[192,2048]{1,0:T(8,128)}) custom-call(s32[1]{0:T(128)S(6)} %copy.51.length, bf16[2048,1024]{1,0:T(8,128)(2,1)} %get-tuple-element.94.h1t_in, bf16[1024,2048]{1,0:T(8,128)(2,1)} %get-tuple-element.109.da, ...), custom_call_target="tpu_custom_call" | custom-call | flops 40000000000 | bytes 12582912 | tf_op jit(solution)/shard_map/attend_back/pallas_call | solution.py:420
  438.1 66.3 %finish.1 = (f32[256,2048]{1,0:T(8,128)}, f32[2,2048]{1,0:T(2,128)}, bf16[64,8192]{1,0:T(8,128)(2,1)}, bf16[256,2048]{1,0:T(8,128)(2,1)}, f32[64,2048]{1,0:T(8,128)}) custom-call(bf16[1024,1536]{1,0:T(8,128)(2,1)} %get-tuple-element.114.dproj, bf16[8,768,512]{2,1,0:T(8,128)(2,1)} %bitcast.66, bf16[512,1024]{1,0:T(8,128)(2,1)} %get-tuple-element.115.refs_0_, ...), custom_call_target="tpu_custom_call" | custom-call | flops 40000000000 | bytes 12582912 | tf_op jit(solution)/shard_map/finish/pallas_call | solution.py:1098
  504.5 2.8 convert_element_type.25
  507.3 1.6 convert_element_type.26
  508.9 1.1 copy-done.5
  510.0 1.5 fusion.1
  511.5 0.1 reshape.134
  511.6 0.3 dynamic_update_slice.11
  512.0 0.1 reshape.130
  512.1 0.1 reshape.131
  512.2 0.1 reshape.126
  512.3 0.1 reshape.127
  512.4 3.2 add.43
  515.6 0.3 dynamic_update_slice.9
  515.8 0.3 dynamic_update_slice.10
  516.1 0.1 concatenate.25
  516.2 0.7 copy_bitcast_fusion.2.sums
  516.9 0.3 reduce-scatter.5.cloned.1.call-done.summed
  517.2 17.8 %home.1 = (f32[64,6144]{1,0:T(8,128)}, f32[64,2048]{1,0:T(8,128)}, f32[8,128]{1,0:T(8,128)}) custom-call(bf16[1024,512]{1,0:T(8,128)(2,1)} %reduce-scatter.5.cloned.1.call-done.summed, f32[8,4,8,128]{3,2,1,0:T(8,128)} %copy_bitcast_fusion.2.sums), custom_call_target="tpu_custom_call" | custom-call | flops 5000000000 | bytes 2097152 | tf_op jit(solution)/shard_map/home/pallas_call | solution.py:1363
  535.0 1.5 fusion.5
  536.5 1.3 slice.93
  537.8 1.2 slice_bitcast_fusion.3
  539.0 2.7 copy.52
  541.6 0.8 copy.53
  (80 shorter events, 0.7 us)
Async XLA Ops:
  7.2 34.3 %all-gather.5.cloned.1.call-start = ((), (), s32[]{:S(2)}) async-start(), calls=%async_computation.2 | async-start | bytes 2359296 | tf_op jit(solution)/shard_map/all_gather | solution.py:1455
  7.9 116.6 %all-gather.7.cloned.1.call-start = ((), (), s32[]{:S(2)}) async-start(), calls=%async_computation.3 | async-start | bytes 7077888 | tf_op jit(solution)/shard_map/all_gather | solution.py:1472
  21.8 21.0 %copy-start.17 = (bf16[64]{0:T(256)(128)(2,1)S(1)}, bf16[64]{0:T(256)(128)(2,1)}, u32[]{:S(2)}) copy-start(bf16[64]{0:T(256)(128)(2,1)} %param.17) | copy-start | bytes 388
  21.8 21.0 %copy-start.18 = (bf16[64]{0:T(256)(128)(2,1)S(1)}, bf16[64]{0:T(256)(128)(2,1)}, u32[]{:S(2)}) copy-start(bf16[64]{0:T(256)(128)(2,1)} %param.18) | copy-start | bytes 388
  21.9 21.0 %copy-start.19 = (bf16[128]{0:T(256)(128)(2,1)S(1)}, bf16[128]{0:T(256)(128)(2,1)}, u32[]{:S(2)}) copy-start(bf16[128]{0:T(256)(128)(2,1)} %param.20) | copy-start | bytes 772
  21.9 21.0 %copy-start.20 = (bf16[64]{0:T(256)(128)(2,1)S(1)}, bf16[64]{0:T(256)(128)(2,1)}, u32[]{:S(2)}) copy-start(bf16[64]{0:T(256)(128)(2,1)} %param.22) | copy-start | bytes 388
  21.9 21.0 %copy-start.21 = (bf16[64]{0:T(256)(128)(2,1)S(1)}, bf16[64]{0:T(256)(128)(2,1)}, u32[]{:S(2)}) copy-start(bf16[64]{0:T(256)(128)(2,1)} %param.23) | copy-start | bytes 388
  21.9 20.9 %copy-start.22 = (bf16[64]{0:T(256)(128)(2,1)S(1)}, bf16[64]{0:T(256)(128)(2,1)}, u32[]{:S(2)}) copy-start(bf16[64]{0:T(256)(128)(2,1)} %param.24) | copy-start | bytes 388
  21.9 20.9 %copy-start.23 = (bf16[256]{0:T(256)(128)(2,1)S(1)}, bf16[256]{0:T(256)(128)(2,1)}, u32[]{:S(2)}) copy-start(bf16[256]{0:T(256)(128)(2,1)} %param.26) | copy-start | bytes 1540
  21.9 20.9 %copy-start.24 = (bf16[64]{0:T(256)(128)(2,1)S(1)}, bf16[64]{0:T(256)(128)(2,1)}, u32[]{:S(2)}) copy-start(bf16[64]{0:T(256)(128)(2,1)} %param.28) | copy-start | bytes 388
  21.9 21.0 %copy-start.1 = (bf16[1,256,2048]{2,1,0:T(8,128)(2,1)S(1)}, bf16[1,256,2048]{2,1,0:T(8,128)(2,1)}, u32[]{:S(2)}) copy-start(bf16[1,256,2048]{2,1,0:T(8,128)(2,1)} %param.29) | copy-start | bytes 3145732
  21.9 21.0 %copy-start.3 = (bf16[1,256,2048]{2,1,0:T(8,128)(2,1)S(1)}, bf16[1,256,2048]{2,1,0:T(8,128)(2,1)}, u32[]{:S(2)}) copy-start(bf16[1,256,2048]{2,1,0:T(8,128)(2,1)} %param.15) | copy-start | bytes 3145732
  21.9 202.4 %all-gather.9.cloned.1.call-start = ((), (), s32[]{:S(2)}) async-start(), calls=%async_computation.4 | async-start | bytes 9437184 | tf_op jit(solution)/shard_map/all_gather | solution.py:1494
  41.5 230.3 %all-gather.11.cloned.1.call-start = ((), (), s32[]{:S(2)}) async-start(), calls=%async_computation.5 | async-start | bytes 9437184 | tf_op jit(solution)/shard_map/all_gather | solution.py:1494
  42.0 396.0 %reduce-scatter.3.cloned.1.call-start = ((), (), s32[]{:S(2)}) async-start(), calls=%async_computation.6 | async-start | bytes 9437184 | tf_op jit(solution)/shard_map/reduce_scatter | solution.py:1404
  115.5 2.1 copy-start
  117.6 2.0 copy-start.4
  304.6 212.5 %reduce-scatter.5.cloned.1.call-start = ((), (), s32[]{:S(2)}) async-start(), calls=%async_computation.7 | async-start | bytes 5242880 | tf_op jit(solution)/shard_map/reduce_scatter | solution.py:1411
  504.4 2.9 copy-start.8
  504.4 4.4 copy-start.7
  504.4 4.4 copy-start.9
  504.4 4.4 copy-start.11
  507.3 1.6 copy-start.2
  507.3 2.7 copy-start.5
  510.0 1.6 copy-start.14
  510.0 1.6 copy-start.15
  510.0 2.0 copy-start.12
  510.0 2.2 copy-start.13
  510.0 2.4 copy-start.6
  512.4 3.2 copy-start.16
  535.0 6.7 %copy-start.10 = (f32[64,2048]{1,0:T(8,128)S(1)}, f32[64,2048]{1,0:T(8,128)}, u32[]{:S(2)}) copy-start(f32[64,2048]{1,0:T(8,128)} %get-tuple-element.185) | copy-start | bytes 1572868
Sparse Core Ops, SparseCore 0:
  9.6 31.7 all-gather.4
  43.1 64.2 all-gather.6
  109.0 80.6 all-gather.8
  191.2 80.5 all-gather.10
  304.8 124.7 reduce-scatter.2
  438.2 78.9 reduce-scatter.4
